TPU v7x, 32 devices: a whole 2x2x4 slice. The times are simulated.
32 devices in a mesh: section: 4 (over y, x), clip: 8 (over z, core).
Axes of the slice: x: 2, y: 2, z: 4, core: 2. Of those that a mesh axis runs over, the one named last changes fastest.
Arguments:
- iframe_act: bfloat16 [4, 32, 14, 14, 1024], P('section', 'clip'), may hold values from -18 to 18
- motion_act: bfloat16 [4, 32, 14, 14, 256], P('section', 'clip'), may hold values from -18 to 18
- iframe_grad: bfloat16 [4, 32, 14, 14, 1024], P('section', 'clip'), may hold values from -18 to 18
- motion_grad: bfloat16 [4, 32, 14, 14, 256], P('section', 'clip'), may hold values from -18 to 18
- segment_valid: int32 [4, 32], P(None, 'clip'), may hold values from 0 to 1, as said below
- reduce_weight: bfloat16 [1024, 256], replicated, may hold values from -0.1875 to 0.1875
- spatial_weight: bfloat16 [3, 3, 256, 256], replicated, may hold values from -0.125 to 0.125
- expand_weight: bfloat16 [256, 1024], replicated, may hold values from -0.375 to 0.375
- motion_first: bfloat16 [3, 3, 256, 256], replicated, may hold values from -0.125 to 0.125
- motion_second: bfloat16 [3, 3, 256, 256], replicated, may hold values from -0.125 to 0.125
- reduce_norm: float32 [2, 256], replicated, may hold values from 0.5 to 1.5
- spatial_norm: float32 [2, 256], replicated, may hold values from 0.5 to 1.5
- expand_norm: float32 [2, 1024], replicated, may hold values from 0.5 to 1.5
- first_norm: float32 [2, 256], replicated, may hold values from 0.5 to 1.5
- second_norm: float32 [2, 256], replicated, may hold values from 0.5 to 1.5
Outputs:
- iframe_out: bfloat16 [4, 32, 14, 14, 1024], P('section', 'clip')
- motion_out: bfloat16 [4, 32, 14, 14, 256], P('section', 'clip')
- iframe_back: bfloat16 [4, 32, 14, 14, 1024], P('section', 'clip')
- motion_back: bfloat16 [4, 32, 14, 14, 256], P('section', 'clip')
- grad_reduce: float32 [1024, 256], replicated
- grad_spatial: float32 [3, 3, 256, 256], replicated
- grad_expand: float32 [256, 1024], replicated
- grad_first: float32 [3, 3, 256, 256], replicated
- grad_second: float32 [3, 3, 256, 256], replicated
- grad_reduce_norm: float32 [2, 256], replicated
- grad_spatial_norm: float32 [2, 256], replicated
- grad_expand_norm: float32 [2, 1024], replicated
- grad_first_norm: float32 [2, 256], replicated
- grad_second_norm: float32 [2, 256], replicated
Inputs may be any that keep to these rules, and one draw needn't show every extreme that they name: `segment_valid`: frame 0 of each clip of 4 frames is 1.
All inputs are finite; a program needn't handle non-finite values.
Results may differ from a plain program's by a relative error of at most 0.0088.
Values may be sent and summed in bfloat16 or wider, within the bound.
No kernel may reach another device: no remote copies, remote signals or barrier semaphores. Data moves between devices by JAX's collectives and lax.ppermute only.
A program may use at most 192 MiB of HBM per device.

v0:
```python
import functools

import jax
import jax.numpy as jnp
from jax import lax
from jax.experimental import pallas as pl
from jax.experimental.pallas import tpu as pltpu
from jax.sharding import PartitionSpec as P

EPS = 1e-05
LANES = 128
F32 = jnp.float32
BF16 = jnp.bfloat16


def factors(size):
    steps = []
    stride = 1
    if size % 2 == 0:
        steps.append((stride, 2))
        stride, size = 2, size // 2
    while size % 4 == 0:
        steps.append((stride, 4))
        stride, size = stride * 4, size // 4
    while size % 2 == 0:
        steps.append((stride, 2))
        stride, size = stride * 2, size // 2
    return steps, size


def swap(value, axis, mask):
    size = lax.axis_size(axis)
    return lax.ppermute(value, axis, [(i, i ^ mask) for i in range(size)])


def clip_parts(value):
    steps, rest = factors(lax.axis_size("clip"))
    if rest != 1:
        return [lax.psum(value, "clip")]
    for stride, radix in steps[:-1]:
        parts = [swap(value, "clip", stride * k) for k in range(1, radix)]
        for part in parts:
            value = value + part
    stride, radix = steps[-1]
    return [value] + [swap(value, "clip", stride * k) for k in range(1, radix)]


def sigmoid(u):
    return 0.5 + 0.5 * jnp.tanh(0.5 * u)


def total_of(refs):
    total = refs[0][...]
    for ref in refs[1:]:
        total = total + ref[...]
    return total


def row_of(total, row, channels):
    count = channels // LANES
    return jnp.concatenate([total[row + k : row + k + 1] for k in range(count)], axis=1)


def put_row(ref, row, value):
    for k in range(value.shape[1] // LANES):
        ref[row + k : row + k + 1, :] = value[:, k * LANES : (k + 1) * LANES]


def moments(total, row, apart, channels, count):
    mean = row_of(total, row, channels) / count
    square = row_of(total, row + apart, channels) / count
    return mean, lax.rsqrt(square - mean * mean + EPS)


def eights(value):
    return value.reshape(-1, 8, value.shape[-1])


def rows_of(value):
    return value.reshape(-1, value.shape[-1])


def down(value):
    return jnp.sum(jnp.sum(value, axis=0), axis=0, keepdims=True)


def spread(value, width, frames, same_ref, edge_ref):
    rows, channels = value.shape
    line = width * frames
    index = lax.broadcasted_iota(jnp.int32, (line, channels), 0)
    first = jnp.where(index < frames, 0.0, 1.0).astype(F32)
    final = jnp.where(index >= line - frames, 0.0, 1.0).astype(F32)
    before = pltpu.roll(value, frames, 0).reshape(-1, line, channels) * first
    after = pltpu.roll(value, rows - frames, 0).reshape(-1, line, channels) * final
    zeros = jnp.zeros((line, channels), F32)
    for k, part in enumerate((rows_of(before), value, rows_of(after))):
        lanes = slice(k * channels, (k + 1) * channels)
        same_ref[:, lanes] = part.astype(BF16)
        edge_ref[:, lanes] = jnp.concatenate([zeros, part, zeros], axis=0).astype(BF16)


def tap_rows(same_ref, edge_ref, a):
    rows = same_ref.shape[0]
    if a == 1:
        return same_ref[...]
    start = a * (edge_ref.shape[0] - rows) // 2
    return edge_ref[start : start + rows, :]


def conv_of(same_ref, edge_ref, kernel_ref):
    total = None
    for a in range(3):
        matrix = kernel_ref[a].reshape(-1, kernel_ref.shape[3])
        part = jnp.dot(tap_rows(same_ref, edge_ref, a), matrix, preferred_element_type=F32)
        total = part if total is None else total + part
    return total


def conv_back_of(same_ref, edge_ref, kernel_ref):
    total = None
    channels = kernel_ref.shape[3]
    for a in range(3):
        rows = tap_rows(same_ref, edge_ref, a)
        for b in range(3):
            part = lax.dot_general(
                rows[:, b * channels : (b + 1) * channels],
                kernel_ref[2 - a, 2 - b],
                (((1,), (1,)), ((), ())),
                preferred_element_type=F32,
            )
            total = part if total is None else total + part
    return total


def split_store(core, keep_ref, send_ref, row, value):
    half = value.shape[0] // 2
    low, high = value[:half].astype(BF16), value[half:].astype(BF16)
    keep_ref[row : row + half, :] = jnp.where(core == 0, low, high)
    send_ref[row : row + half, :] = jnp.where(core == 0, high, low)


def across(first, second):
    return lax.dot_general(first, second, (((0,), (0,)), ((), ())), preferred_element_type=F32)


def conv_grad_to(core, picture, same_ref, edge_ref, keep_ref, send_ref, row):
    channels = same_ref.shape[1] // 3
    half = picture.shape[1] // 2
    for a in range(3):
        product = across(picture, tap_rows(same_ref, edge_ref, a))
        for b in range(3):
            tap = 3 * (2 - a) + 2 - b
            part = product[:, b * channels : (b + 1) * channels]
            split_store(core, keep_ref, send_ref, row + tap * half, part)


def back_of(up, z, mean, scale, gain, total_up, total_cross, count, mask):
    share = total_cross * scale / count
    start = total_up / count - mean * share
    return rows_of((gain * scale) * (eights(up) - mask * (start + eights(z) * share)))


def slope_back(grad, z, mean, scale, norm, ups_ref):
    hat = (z - mean) * scale
    u = norm[0:1] * hat + norm[1:2]
    s = sigmoid(u)
    up = grad.astype(BF16).astype(F32) * (s + u * s * (1.0 - s))
    ups_ref[...] = up
    return down(eights(up)), down(eights(up * hat))


def kernel_1(width, valid_far, x_far, m_far, reduce_far, first_far, mask8, zr, z1, sums, *rest):
    same, edge, valid, x, m, reduce_w, first_w, arrived = rest
    copies = []
    for k, (far, near) in enumerate(
        ((m_far, m), (valid_far, valid), (first_far, first_w), (x_far, x), (reduce_far, reduce_w))
    ):
        copies.append(pltpu.make_async_copy(far, near, arrived.at[k]))
        copies[k].start()
    channels = z1.shape[1]
    frames = m.shape[1]
    copies[0].wait()
    spread(rows_of(m[...]).astype(F32), width, frames, same, edge)
    copies[1].wait()
    section = lax.axis_index("section")
    keep = [valid[section, f].astype(F32) for f in range(frames)]
    frame = lax.rem(lax.broadcasted_iota(jnp.int32, (8, channels), 0), frames)
    mask = jnp.full((8, channels), 0.0, F32)
    for f in range(frames):
        mask = jnp.where(frame == f, keep[f], mask)
    mask8[...] = mask
    copies[2].wait()
    z1[...] = conv_of(same, edge, first_w)
    copies[3].wait()
    copies[4].wait()
    zr[...] = jnp.dot(rows_of(x[...]), reduce_w[...], preferred_element_type=F32)
    step = channels // LANES
    sums[...] = jnp.zeros(sums.shape, F32)
    for k, ref in enumerate((zr, z1)):
        z = eights(ref[...])
        kept = mask * z
        put_row(sums, 2 * k * step, down(kept))
        put_row(sums, (2 * k + 1) * step, down(kept * z))
    put_row(sums, 4 * step, jnp.full((1, LANES), 1.0, F32) * (sum(keep) * x.shape[0]))


def kernel_2(place, parts, mask8, zr, z1, reduce_n, first_n, spatial_w, second_w, *rest):
    total_1, ra, mm, zs, z2, sums, same, edge = rest
    channels = zr.shape[1]
    step = channels // LANES
    total = total_of(parts)
    total_1[...] = total
    count = total[4 * step : 4 * step + 1, 0:1]
    mask = mask8[...]
    for k, (z_ref, norm, act, weight, out) in enumerate(
        ((zr, reduce_n, ra, spatial_w, zs), (z1, first_n, mm, second_w, z2))
    ):
        mean, scale = moments(total, 2 * k * step, step, channels, count)
        gain = norm[0:1] * scale
        u = z_ref[...] * gain + (norm[1:2] - mean * gain)
        value = u * sigmoid(u)
        act[...] = value.astype(BF16)
        spread(value, *place, same, edge)
        out[...] = conv_of(same, edge, weight)
        z = eights(out[...])
        kept = mask * z
        put_row(sums, 2 * k * step, down(kept))
        put_row(sums, (2 * k + 1) * step, down(kept * z))


def kernel_3(parts, mask8, total_1, zs, z2, m, gm, spatial_n, second_n, expand_w, *rest):
    total_2, sa, ze, motion_out, up2, sums = rest
    channels, wide = zs.shape[1], ze.shape[1]
    step, wide_step = channels // LANES, wide // LANES
    total = total_of(parts)
    total_2[...] = total
    count = total_1[4 * step : 4 * step + 1, 0:1]
    mean, scale = moments(total, 0, step, channels, count)
    gain = spatial_n[0:1] * scale
    u = zs[...] * gain + (spatial_n[1:2] - mean * gain)
    sa[...] = (u * sigmoid(u)).astype(BF16)
    mask = mask8[...]
    sums[...] = jnp.zeros(sums.shape, F32)
    for at in range(0, wide, channels):
        lanes = slice(at, at + channels)
        ze[:, lanes] = jnp.dot(sa[...], expand_w[:, lanes], preferred_element_type=F32)
        z = eights(ze[:, lanes])
        kept = z * mask
        put_row(sums, at // LANES, down(kept))
        put_row(sums, wide_step + at // LANES, down(kept * z))
    mean, scale = moments(total, 2 * step, step, channels, count)
    hat = eights((z2[...] - mean) * scale)
    motion = eights(rows_of(m[...]).astype(F32))
    u = second_n[0:1] * hat + second_n[1:2] + motion
    s = sigmoid(u)
    w = u * s
    out = mask * w + (1.0 - mask) * motion
    motion_out[...] = rows_of(out).astype(BF16).reshape(motion_out.shape)
    up = eights(rows_of(gm[...]).astype(F32)) * mask * (s + w * (1.0 - s))
    up2[...] = rows_of(up)
    put_row(sums, 2 * wide_step, down(up))
    put_row(sums, 2 * wide_step + step, down(up * hat))


def kernel_4(place, parts, mask8, total_1, total_2, z1, z2, up2, ze, x, gx, *rest):
    expand_n, second_n, first_n, second_w = rest[:4]
    total_3, iframe_out, upe, up1, same, edge, sums = rest[4:]
    channels, wide = z1.shape[1], ze.shape[1]
    step, wide_step = channels // LANES, wide // LANES
    total = total_of(parts)
    total_3[...] = total
    count = total_1[4 * step : 4 * step + 1, 0:1]
    mask = mask8[...]

    mean, scale = moments(total_2[...], 2 * step, step, channels, count)
    low = back_of(
        up2[...], z2[...], mean, scale, second_n[0:1], row_of(total, 2 * wide_step, channels),
        row_of(total, 2 * wide_step + step, channels), count, mask,
    )
    spread(low.astype(BF16).astype(F32), *place, same, edge)
    mid_grad = conv_back_of(same, edge, second_w)
    mean, scale = moments(total_1[...], 2 * step, step, channels, count)
    total_up, total_cross = slope_back(mid_grad, z1[...], mean, scale, first_n, up1)
    sums[...] = jnp.zeros(sums.shape, F32)
    put_row(sums, 2 * wide_step, total_up)
    put_row(sums, 2 * wide_step + step, total_cross)

    part, rows = channels, 16
    frames = place[1]
    eight = (8, part)
    for at in range(0, wide, part):
        lanes = slice(at, at + part)
        mean, scale = moments(total, at // LANES, wide_step, part, count)
        mean8, scale8 = jnp.broadcast_to(mean, eight), jnp.broadcast_to(scale, eight)
        gain8 = jnp.broadcast_to(expand_n[0:1, lanes], eight)
        shift8 = jnp.broadcast_to(expand_n[1:2, lanes], eight)

        def step_of(i, totals):
            here = pl.ds(pl.multiple_of(i * rows, rows), rows)
            pixels = pl.ds(i * (rows // frames), rows // frames)
            hat = (eights(ze[here, lanes]) - mean8) * scale8
            x_here = eights(rows_of(x[pixels, :, lanes]).astype(F32))
            g_here = eights(rows_of(gx[pixels, :, lanes]).astype(F32))
            u = hat * gain8 + shift8 + x_here
            s = sigmoid(u)
            w = u * s
            out = mask * w + (1.0 - mask) * x_here
            iframe_out[pixels, :, lanes] = rows_of(out).astype(BF16).reshape(-1, frames, part)
            up = g_here * mask * (s + w * (1.0 - s))
            upe[here, lanes] = rows_of(up)
            cross = up * hat
            return (totals[0] + jnp.sum(up, axis=0), totals[1] + jnp.sum(cross, axis=0))

        empty = (jnp.zeros(eight, F32), jnp.zeros(eight, F32))
        totals = lax.fori_loop(0, ze.shape[0] // rows, step_of, empty, unroll=7)
        put_row(sums, at // LANES, down(totals[0][None]))
        put_row(sums, wide_step + at // LANES, down(totals[1][None]))


def kernel_5(parts, mask8, total_1, total_2, total_3, ze, upe, zs, expand_n, spatial_n, expand_w, *rest):
    total_4, back_e, ups, sums = rest
    channels, wide = zs.shape[1], ze.shape[1]
    step, wide_step = channels // LANES, wide // LANES
    total = total_of(parts)
    total_4[...] = total
    count = total_1[4 * step : 4 * step + 1, 0:1]
    mask = mask8[...]
    grad = None
    for at in range(0, wide, channels):
        lanes = slice(at, at + channels)
        mean, scale = moments(total_3[...], at // LANES, wide_step, channels, count)
        low = back_of(
            upe[:, lanes], ze[:, lanes], mean, scale, expand_n[0:1, lanes],
            row_of(total, at // LANES, channels), row_of(total, wide_step + at // LANES, channels),
            count, mask,
        )
        back_e[:, lanes] = low.astype(BF16)
        part = lax.dot_general(
            back_e[:, lanes], expand_w[:, lanes], (((1,), (1,)), ((), ())), preferred_element_type=F32
        )
        grad = part if grad is None else grad + part
    mean, scale = moments(total_2[...], 0, step, channels, count)
    total_up, total_cross = slope_back(grad, zs[...], mean, scale, spatial_n, ups)
    sums[...] = jnp.zeros(sums.shape, F32)
    put_row(sums, 0, total_up)
    put_row(sums, step, total_cross)


def kernel_6(place, parts, mask8, total_1, total_2, ups, zs, zr, spatial_n, reduce_n, spatial_w, *rest):
    total_5, upr, same, edge, sums = rest
    channels = zs.shape[1]
    step = channels // LANES
    total = total_of(parts)
    total_5[...] = total
    count = total_1[4 * step : 4 * step + 1, 0:1]
    mask = mask8[...]
    mean, scale = moments(total_2[...], 0, step, channels, count)
    low = back_of(
        ups[...], zs[...], mean, scale, spatial_n[0:1], row_of(total, 0, channels),
        row_of(total, step, channels), count, mask,
    )
    spread(low.astype(BF16).astype(F32), *place, same, edge)
    grad = conv_back_of(same, edge, spatial_w)
    mean, scale = moments(total_1[...], 0, step, channels, count)
    total_up, total_cross = slope_back(grad, zr[...], mean, scale, reduce_n, upr)
    sums[...] = jnp.zeros(sums.shape, F32)
    put_row(sums, 0, total_up)
    put_row(sums, step, total_cross)


def kernel_7(parts, mask8, total_1, upr, zr, reduce_n, back_r):
    channels = zr.shape[1]
    step = channels // LANES
    total = total_of(parts)
    count = total_1[4 * step : 4 * step + 1, 0:1]
    mask = mask8[...]
    mean, scale = moments(total_1[...], 0, step, channels, count)
    low = back_of(
        upr[...], zr[...], mean, scale, reduce_n[0:1], row_of(total, 0, channels),
        row_of(total, step, channels), count, mask,
    )
    back_r[...] = low.astype(BF16)


def kernel_motion(place, mask8, total_1, total_4, up1, z1, first_n, first_w, m, gm, up2, *rest):
    same_2, edge_2, mm, sa, back_e, motion_back, kept_ref, sent_ref, same, edge = rest
    channels = z1.shape[1]
    step, wide_step = channels // LANES, back_e.shape[1] // LANES
    count = total_1[4 * step : 4 * step + 1, 0:1]
    mask = mask8[...]
    mean, scale = moments(total_1[...], 2 * step, step, channels, count)
    total = total_4[...]
    low = back_of(
        up1[...], z1[...], mean, scale, first_n[0:1], row_of(total, 2 * wide_step, channels),
        row_of(total, 2 * wide_step + step, channels), count, mask,
    )
    spread(low.astype(BF16).astype(F32), *place, same, edge)
    out = conv_back_of(same, edge, first_w) + up2[...]
    out = rows_of(eights(out) + eights(rows_of(gm[...]).astype(F32)) * (1.0 - mask))
    motion_back[...] = out.astype(BF16).reshape(motion_back.shape)
    core = core_here()
    half = channels // 2
    conv_grad_to(core, mm[...], same_2, edge_2, kept_ref, sent_ref, 0)
    conv_grad_to(core, rows_of(m[...]), same, edge, kept_ref, sent_ref, 9 * half)
    for k in range(back_e.shape[1] // 256):
        product = across(sa[...], back_e[:, k * 256 : (k + 1) * 256])
        split_store(core, kept_ref, sent_ref, (18 + k) * half, product)


def kernel_last(ra, same, edge, x, back_r, sums_r, sums_s, sums_1, sums_2, kept_ref, sent_ref):
    core = core_here()
    channels, wide = ra.shape[1], x.shape[2]
    conv_grad_to(core, ra[...], same, edge, kept_ref, sent_ref, 0)
    product = across(rows_of(x[...]), back_r[...])
    at = 9 * (channels // 2)
    split_store(core, kept_ref, sent_ref, at, product)
    at = at + wide // 2
    rows = norm_rows(sums_r, 0, channels) + norm_rows(sums_s, 0, channels)
    rows += norm_rows(sums_1, 0, wide) + norm_rows(sums_1, 2 * wide // LANES, channels)
    rows += norm_rows(sums_2, 2 * wide // LANES, channels)
    half = kept_ref.shape[0] - at
    rows.append(jnp.zeros((2 * half - len(rows), 256), F32))
    split_store(core, kept_ref, sent_ref, at, jnp.concatenate(rows, axis=0))


def norm_rows(sums, row, channels):
    count = channels // LANES
    starts = list(range(row + count, row + 2 * count, 2)) + list(range(row, row + count, 2))
    return [jnp.concatenate([sums[k : k + 1, :], sums[k + 1 : k + 2, :]], axis=1) for k in starts]


def kernel_iframe(mask8, gx, upe, back_r, reduce_w, iframe_back):
    wide, part = upe.shape[1], 256
    mask, frames = mask8[...], gx.shape[1]
    for at in range(0, wide, part):
        lanes = slice(at, at + part)
        out = upe[:, lanes] + lax.dot_general(
            back_r[...], reduce_w[lanes, :], (((1,), (1,)), ((), ())), preferred_element_type=F32
        )
        out = eights(out) + eights(rows_of(gx[:, :, lanes]).astype(F32)) * (1.0 - mask)
        iframe_back[:, :, lanes] = rows_of(out).astype(BF16).reshape(-1, frames, part)


def core_here():
    return lax.rem(lax.axis_index("clip"), 2)


def place_on(axis, stride, radix):
    return lax.rem(lax.axis_index(axis) // stride, radix)


def kernel_scatter(axis, stride, radix, *refs):
    here = place_on(axis, stride, radix)
    ins, outs = refs[:-radix], refs[-radix:]
    for k in range(radix):
        at = jnp.bitwise_xor(here, k)
        total = ins[0][at].astype(F32)
        for ref in ins[1:]:
            total = total + ref[at].astype(F32)
        outs[k][...] = total.astype(BF16)


def kernel_sum(*refs):
    total = refs[0][...].astype(F32)
    for ref in refs[1:-1]:
        total = total + ref[...].astype(F32)
    refs[-1][...] = total.astype(BF16)


def kernel_gather(axis, stride, radix, *refs):
    here = place_on(axis, stride, radix)
    for k in range(radix):
        refs[-1][jnp.bitwise_xor(here, k)] = refs[k][...]


def kernel_finish(kinds, own, other, *outs):
    core = core_here()
    at = 0

    def halves(ref, lanes, size, at):
        here = pl.ds(pl.multiple_of(core * size, size), size)
        there = pl.ds(pl.multiple_of((1 - core) * size, size), size)
        ref[here, lanes] = own[at : at + size, :].astype(F32)
        ref[there, lanes] = other[at : at + size, :].astype(F32)

    for kind, out in zip(kinds, outs):
        if kind == "taps":
            size = out.shape[1] // 2
            for k in range(out.shape[0]):
                halves(out.at[k], slice(None), size, at)
                at = at + size
        elif kind == "wide":
            size = out.shape[0] // 2
            for k in range(out.shape[1] // 256):
                halves(out, slice(k * 256, (k + 1) * 256), size, at)
                at = at + size
        else:
            mine, his = own[at : at + 16, :].astype(F32), other[at : at + 16, :].astype(F32)
            rows = jnp.where(core == 0, mine, his)
            start = kind
            count = out.shape[1] // 256
            for k in range(2):
                for j in range(count):
                    row = start + k * count + j
                    out[k : k + 1, j * 256 : (j + 1) * 256] = rows[row : row + 1]


def call(kernel, outs, *args, scratch=(), flops=1 << 20, lists=None, space=pltpu.VMEM):
    def body(*refs):
        if lists:
            return kernel(refs[:lists], *refs[lists:])
        return kernel(*refs)

    moved = sum(arg.size * arg.dtype.itemsize for arg in args)
    moved += sum(out.size * out.dtype.itemsize for out in outs)
    return pl.pallas_call(
        body,
        out_shape=outs,
        in_specs=[pl.BlockSpec(memory_space=space) for _ in args],
        out_specs=[pl.BlockSpec(memory_space=pltpu.VMEM) for _ in outs],
        scratch_shapes=list(scratch),
        compiler_params=pltpu.CompilerParams(vmem_limit_bytes=20 << 20),
        cost_estimate=pl.CostEstimate(flops=flops, bytes_accessed=moved, transcendentals=0),
    )(*args)


def like(shape, dtype):
    return jax.ShapeDtypeStruct(shape, dtype)


def grad_sum(kept, sent, kinds, outs):
    clip_steps, clip_rest = factors(lax.axis_size("clip"))
    section = lax.axis_size("section")
    got = swap(sent, "clip", 1)
    rows, width = kept.shape
    order = [("section", 1, section)] + [("clip",) + step for step in clip_steps[1:]]
    ins = [kept, got]
    for axis, stride, radix in order:
        rows = rows // radix
        chunks = call(
            functools.partial(kernel_scatter, axis, stride, radix),
            [like((rows, width), BF16)] * radix,
            *[part.reshape(radix, rows, width) for part in ins],
        )
        ins = [chunks[0]] + [swap(chunks[k], axis, stride * k) for k in range(1, radix)]
    (value,) = call(kernel_sum, [like((rows, width), BF16)], *ins)
    for axis, stride, radix in reversed(order):
        parts = [value] + [swap(value, axis, stride * k) for k in range(1, radix)]
        (value,) = call(
            functools.partial(kernel_gather, axis, stride, radix),
            [like((radix,) + value.shape, BF16)],
            *parts,
        )
        value = value.reshape(-1, width)
    return call(functools.partial(kernel_finish, kinds), outs, value, swap(value, "clip", 1))


def per_device(
    iframe_act,
    motion_act,
    iframe_grad,
    motion_grad,
    segment_valid,
    reduce_weight,
    spatial_weight,
    expand_weight,
    motion_first,
    motion_second,
    reduce_norm,
    spatial_norm,
    expand_norm,
    first_norm,
    second_norm,
):
    frames, height, width, wide = iframe_act.shape[1:]
    narrow = motion_act.shape[4]

    def pixels_first(value):
        return jnp.transpose(value[0], (1, 2, 0, 3)).reshape(height * width, frames, value.shape[4])

    def frames_first(value):
        value = value.reshape(height, width, frames, value.shape[2])
        return jnp.transpose(value, (2, 0, 1, 3))[None]

    x, m, gx, gm = [pixels_first(v) for v in (iframe_act, motion_act, iframe_grad, motion_grad)]
    step, wide_step = narrow // LANES, wide // LANES
    area = height * width * frames

    def plane(channels, dtype=F32):
        return like((area, channels), dtype)

    def small(count):
        return like(((count + 7) // 8 * 8, LANES), F32)

    def bound(kernel):
        return functools.partial(kernel, (width, frames))

    def far(value):
        return pltpu.with_memory_space_constraint(value, pltpu.HBM)

    point = 2 * area * narrow * wide
    conv = 18 * area * narrow * narrow
    same = (area, 3 * narrow)
    edge = (area + 2 * width * frames, 3 * narrow)
    spread_scratch = [pltpu.VMEM(same, BF16), pltpu.VMEM(edge, BF16)]
    first_size, second_size = small(4 * step + 1), small(4 * step)
    both = small(2 * wide_step + 2 * step)

    mask8, zr, z1, sums = call(
        functools.partial(kernel_1, width),
        [like((8, narrow), F32), plane(narrow), plane(narrow), first_size],
        *[far(v) for v in (segment_valid, x, m, reduce_weight, motion_first)],
        scratch=spread_scratch
        + [pltpu.SMEM(segment_valid.shape, jnp.int32)]
        + [pltpu.VMEM(v.shape, BF16) for v in (x, m, reduce_weight, motion_first)]
        + [pltpu.SemaphoreType.DMA((5,))],
        flops=point + conv,
        space=pltpu.HBM,
    )
    parts = clip_parts(sums)
    total_1, ra, mm, zs, z2, sums = call(
        bound(kernel_2),
        [first_size, plane(narrow, BF16), plane(narrow, BF16), plane(narrow), plane(narrow), second_size],
        *parts, mask8, zr, z1, reduce_norm, first_norm, spatial_weight, motion_second,
        scratch=spread_scratch,
        flops=2 * conv,
        lists=len(parts),
    )
    parts = clip_parts(sums)
    total_2, sa, ze, motion_out, up2, sums = call(
        kernel_3,
        [second_size, plane(narrow, BF16), plane(wide), like(gm.shape, BF16), plane(narrow), both],
        *parts, mask8, total_1, zs, z2, m, gm, spatial_norm, second_norm, expand_weight,
        flops=point,
        lists=len(parts),
    )
    parts = clip_parts(sums)
    up2_sums = sums
    total_3, iframe_out, upe, up1, same_2, edge_2, sums = call(
        bound(kernel_4),
        [both, like(gx.shape, BF16), plane(wide), plane(narrow), like(same, BF16), like(edge, BF16), both],
        *parts, mask8, total_1, total_2, z1, z2, up2, ze, x, gx,
        expand_norm, second_norm, first_norm, motion_second,
        flops=conv,
        lists=len(parts),
    )
    parts = clip_parts(sums)
    up1_sums = sums
    total_4, back_e, ups, sums = call(
        kernel_5,
        [both, plane(wide, BF16), plane(narrow), small(2 * step)],
        *parts, mask8, total_1, total_2, total_3, ze, upe, zs, expand_norm, spatial_norm, expand_weight,
        flops=point,
        lists=len(parts),
    )
    parts = clip_parts(sums)
    ups_sums = sums
    half = narrow // 2
    set_rows = (18 + wide // 256) * half
    motion_back, kept, sent = call(
        bound(kernel_motion),
        [like(m.shape, BF16)] + [like((set_rows, 256), BF16)] * 2,
        mask8, total_1, total_4, up1, z1, first_norm, motion_first, m, gm, up2,
        same_2, edge_2, mm, sa, back_e,
        scratch=spread_scratch,
        flops=3 * conv + point,
    )
    taps = like((9, narrow, narrow), F32)
    grad_second, grad_first, grad_expand = grad_sum(
        kept, sent, ("taps", "taps", "wide"), [taps, taps, like(expand_weight.shape, F32)]
    )
    total_5, upr, same_s, edge_s, sums = call(
        bound(kernel_6),
        [small(2 * step), plane(narrow), like(same, BF16), like(edge, BF16), small(2 * step)],
        *parts, mask8, total_1, total_2, ups, zs, zr, spatial_norm, reduce_norm, spatial_weight,
        flops=conv,
        lists=len(parts),
    )
    parts = clip_parts(sums)
    upr_sums = sums
    (back_r,) = call(
        kernel_7,
        [plane(narrow, BF16)],
        *parts, mask8, total_1, upr, zr, reduce_norm,
        lists=len(parts),
    )

    spare = 128
    set_rows = 9 * half + wide // 2 + spare
    kept, sent = call(
        kernel_last,
        [like((set_rows, 256), BF16)] * 2,
        ra, same_s, edge_s, x, back_r, upr_sums, ups_sums, up1_sums, up2_sums,
        flops=conv + point,
    )
    (iframe_back,) = call(
        kernel_iframe, [like(gx.shape, BF16)], mask8, gx, upe, back_r, reduce_weight,
        flops=point,
    )
    norms = (reduce_norm, spatial_norm, expand_norm, first_norm, second_norm)
    starts = [0]
    for norm in norms:
        starts.append(starts[-1] + norm.size // 256)
    grad_spatial, grad_reduce, *norm_grads = grad_sum(
        kept, sent, ["taps", "taps"] + starts[:-1],
        [taps, like((1, wide, narrow), F32)] + [like(norm.shape, F32) for norm in norms],
    )
    features = tuple(frames_first(v) for v in (iframe_out, motion_out, iframe_back, motion_back))
    return features + (
        grad_reduce[0],
        grad_spatial.reshape(spatial_weight.shape),
        grad_expand,
        grad_first.reshape(motion_first.shape),
        grad_second.reshape(motion_second.shape),
    ) + tuple(norm_grads)


def solution(mesh):
    shared = (P("section", "clip", None, None, None),) * 4
    return jax.shard_map(
        per_device,
        mesh=mesh,
        in_specs=shared + (P(None, "clip"),) + (P(),) * 10,
        out_specs=shared + (P(),) * 10,
        check_vma=False,
    )
```

profile of v0, /device:TPU:0, one launch (start us, length us, event | category | flops | bytes accessed | tf_op | source)
XLA Modules:
  0.0 180.1 jit_solution(9545044626499432831)
XLA Ops:
  0.7 4.2 %shard_map.254 = (f32[8,256]{1,0:T(8,128)S(1)}, f32[784,256]{1,0:T(8,128)S(1)}, f32[784,256]{1,0:T(8,128)S(1)}, f32[16,128]{1,0:T(8,128)S(1)}) custom-call(s32[4,4]{1,0:T(4,128)} %refs_0_.1, bf16[196,4,1024]{2,1,0:T(4,128)(2,1)} %bitcast.60, bf16[196,4,256]{2,1,0:T(4,128)(2,1)} %bitcast.81, bf16[1024,256]{1,0:T(8,128)(2,1)} %refs_4_.3, ...), custom_call_target="tpu_custom_call" | custom-call | flops 1335885824 | bytes 5333056 | tf_op jit(solution)/shard_map/pallas_call | solution.py:516
  6.2 4.9 %collective-permute-start.3 = (f32[16,128]{1,0:T(8,128)S(1)}, f32[16,128]{1,0:T(8,128)S(1)}, u32[]{:S(2)}, u32[]{:S(2)}) collective-permute-start(f32[16,128]{1,0:T(8,128)S(1)} %add.18.refs_0_), channel_id=1, source_target_pairs={{0,6},{1,7},{2,4},{3,5},{4,2},{5,3},{6,0},{7,1},{8,14},{9,15},{10,... | collective-permute-start | bytes 24584 | tf_op jit(solution)/shard_map/ppermute | solution.py:33
  11.8 1.1 collective-permute-done.3.refs_3_
  12.8 2.9 %collective-permute-done.2.refs_2_ = f32[16,128]{1,0:T(8,128)S(1)} collective-permute-done((f32[16,128]{1,0:T(8,128)S(1)}, f32[16,128]{1,0:T(8,128)S(1)}, u32[]{:S(2)}, u32[]{:S(2)}) %collective-permute-start.2) | collective-permute-done | bytes 8224 | tf_op jit(solution)/shard_map/ppermute | solution.py:33
  15.8 2.5 %shard_map.255 = (f32[16,128]{1,0:T(8,128)S(1)}, bf16[784,256]{1,0:T(8,128)(2,1)S(1)}, bf16[784,256]{1,0:T(8,128)(2,1)S(1)}, f32[784,256]{1,0:T(8,128)S(1)}, f32...) custom-call(f32[16,128]{1,0:T(8,128)S(1)} %add.18.refs_0_, f32[16,128]{1,0:T(8,128)S(1)} %collective-permute-done.1.refs_1_, ...), custom_call_target="tpu_custom_call" | custom-call | flops 1849688064 | bytes 6430720 | tf_op jit(solution)/shard_map/pallas_call | solution.py:516
  18.4 1.2 collective-permute-done.4
  19.6 1.4 collective-permute-start.7
  21.6 2.4 %collective-permute-start.5 = (f32[8,128]{1,0:T(8,128)S(1)}, f32[8,128]{1,0:T(8,128)S(1)}, u32[]{:S(2)}, u32[]{:S(2)}) collective-permute-start(f32[8,128]{1,0:T(8,128)S(1)} %add.19.refs_0_), channel_id=1, source_target_pairs={{0,2},{1,3},{2,0},{3,1},{4,6},{5,7},{6,4},{7,5},{8,10},{9,11},{10,... | collective-permute-start | bytes 12296 | tf_op jit(solution)/shard_map/ppermute | solution.py:33
  24.0 1.0 collective-permute-done.7.refs_3_
  25.6 2.3 %shard_map.256 = (f32[8,128]{1,0:T(8,128)S(1)}, bf16[784,256]{1,0:T(8,128)(2,1)S(1)}, f32[784,1024]{1,0:T(8,128)S(1)}, bf16[196,4,256]{2,1,0:T(4,128)(2,1)}, f32...) custom-call(f32[8,128]{1,0:T(8,128)S(1)} %add.19.refs_0_, f32[8,128]{1,0:T(8,128)S(1)} %collective-permute-done.5.refs_1_, ...), custom_call_target="tpu_custom_call" | custom-call | flops 411041792 | bytes 7802880 | tf_op jit(solution)/shard_map/pallas_call | solution.py:516
  28.1 1.2 collective-permute-done.8
  29.2 2.5 %collective-permute-start.11 = (f32[24,128]{1,0:T(8,128)S(1)}, f32[24,128]{1,0:T(8,128)S(1)}, u32[]{:S(2)}, u32[]{:S(2)}) collective-permute-start(f32[24,128]{1,0:T(8,128)S(1)} %add.20.refs_0_), channel_id=1, source_target_pairs={{0,6},{1,7},{2,4},{3,5},{4,2},{5,3},{6,0},{7,1},{8,14},{9,15},{10,... | collective-permute-start | bytes 36872 | tf_op jit(solution)/shard_map/ppermute | solution.py:33
  33.6 1.2 collective-permute-done.11.refs_3_
  34.9 1.5 collective-permute-done.10.refs_2_
  36.5 6.1 %shard_map.257 = (f32[24,128]{1,0:T(8,128)S(1)}, bf16[196,4,1024]{2,1,0:T(4,128)(2,1)}, f32[784,1024]{1,0:T(8,128)S(1)}, f32[784,256]{1,0:T(8,128)S(1)}, bf16[78...) custom-call(f32[24,128]{1,0:T(8,128)S(1)} %add.20.refs_0_, ...), custom_call_target="tpu_custom_call" | custom-call | flops 924844032 | bytes 18317312 | tf_op jit(solution)/shard_map/pallas_call | solution.py:516
  42.6 1.2 collective-permute-done.12
  43.8 1.3 collective-permute-start.15
  46.1 2.1 %collective-permute-start.13 = (f32[24,128]{1,0:T(8,128)S(1)}, f32[24,128]{1,0:T(8,128)S(1)}, u32[]{:S(2)}, u32[]{:S(2)}) collective-permute-start(f32[24,128]{1,0:T(8,128)S(1)} %add.21.refs_0_), channel_id=1, source_target_pairs={{0,2},{1,3},{2,0},{3,1},{4,6},{5,7},{6,4},{7,5},{8,10},{9,11},{10,... | collective-permute-start | bytes 36872 | tf_op jit(solution)/shard_map/ppermute | solution.py:33
  48.2 1.2 collective-permute-done.15.refs_3_
  49.9 1.3 shard_map.258
  51.1 4.3 %shard_map.262 = (bf16[196,4,256]{2,1,0:T(4,128)(2,1)}, bf16[2816,256]{1,0:T(8,128)(2,1)S(1)}, bf16[2816,256]{1,0:T(8,128)(2,1)S(1)}) custom-call(f32[8,256]{1,0:T(8,128)S(1)} %get-tuple-element.77.refs_4_.refs_0_, f32[16,128]{1,0:T(8,128)S(1)} %get-tuple-element.81.refs_5_.refs_1_, f32[24,128]{1,0:T(8,128)S(1)} %get-tuple-element.97.refs_2_, ...), custom_call_target="tpu_custom_call" | custom-call | flops 3185573888 | bytes 12695552 | tf_op jit(solution)/shard_map/pallas_call | solution.py:516
  56.0 2.7 %collective-permute-done.16 = f32[8,128]{1,0:T(8,128)S(1)} collective-permute-done((f32[8,128]{1,0:T(8,128)S(1)}, f32[8,128]{1,0:T(8,128)S(1)}, u32[]{:S(2)}, u32[]{:S(2)}) %collective-permute-start.16) | collective-permute-done | bytes 4128 | tf_op jit(solution)/shard_map/ppermute | solution.py:33
  58.7 2.5 %collective-permute-start.19 = (f32[8,128]{1,0:T(8,128)S(1)}, f32[8,128]{1,0:T(8,128)S(1)}, u32[]{:S(2)}, u32[]{:S(2)}) collective-permute-start(f32[8,128]{1,0:T(8,128)S(1)} %add.22.refs_0_), channel_id=1, source_target_pairs={{0,6},{1,7},{2,4},{3,5},{4,2},{5,3},{6,0},{7,1},{8,14},{9,15},{10,... | collective-permute-start | bytes 12296 | tf_op jit(solution)/shard_map/ppermute | solution.py:33
  64.1 1.6 collective-permute-done.18.refs_2_
  65.8 1.3 shard_map.259
  67.2 1.2 collective-permute-done.20
  68.4 1.4 collective-permute-start.23
  70.7 2.0 %collective-permute-start.21 = (f32[8,128]{1,0:T(8,128)S(1)}, f32[8,128]{1,0:T(8,128)S(1)}, u32[]{:S(2)}, u32[]{:S(2)}) collective-permute-start(f32[8,128]{1,0:T(8,128)S(1)} %add.23.refs_0_), channel_id=1, source_target_pairs={{0,2},{1,3},{2,0},{3,1},{4,6},{5,7},{6,4},{7,5},{8,10},{9,11},{10,... | collective-permute-start | bytes 12296 | tf_op jit(solution)/shard_map/ppermute | solution.py:33
  74.7 2.0 %shard_map.263 = (bf16[1792,256]{1,0:T(8,128)(2,1)S(1)}, bf16[1792,256]{1,0:T(8,128)(2,1)S(1)}) custom-call(bf16[784,256]{1,0:T(8,128)(2,1)S(1)} %get-tuple-element.105.refs_0_, bf16[784,768]{1,0:T(8,128)(2,1)S(1)} %get-tuple-element.106.refs_1_, bf16[896,768]{1,0:T(8,128)(2,1)S(1)} %get-tuple-element.107.refs_2_, bf16[196,4,1024]{2,1,0:T(4,128)(2,1)S(1)} %bitcast.62, ...), custom_call_target="tpu_custom_call" | custom-call | flops 1335885824 | bytes 6856704 | tf_op jit(solution)/shard_map/pallas_call | solution.py:516
  77.2 1.6 collective-permute-start.39
  78.8 1.5 collective-permute-start.40
  80.8 7.7 %collective-permute-done.39 = bf16[704,256]{1,0:T(8,128)(2,1)S(1)} collective-permute-done((bf16[704,256]{1,0:T(8,128)(2,1)S(1)}, bf16[704,256]{1,0:T(8,128)(2,1)S(1)}, u32[]{:S(2)}, u32[]{:S(2)}) %collective-permute-start.39) | collective-permute-done | bytes 360480 | tf_op jit(solution)/shard_map/ppermute | solution.py:33
  88.5 8.5 %collective-permute-done.40 = bf16[704,256]{1,0:T(8,128)(2,1)S(1)} collective-permute-done((bf16[704,256]{1,0:T(8,128)(2,1)S(1)}, bf16[704,256]{1,0:T(8,128)(2,1)S(1)}, u32[]{:S(2)}, u32[]{:S(2)}) %collective-permute-start.40) | collective-permute-done | bytes 360480 | tf_op jit(solution)/shard_map/ppermute | solution.py:33
  97.2 2.1 %collective-permute-start.42 = (bf16[176,256]{1,0:T(8,128)(2,1)S(1)}, bf16[176,256]{1,0:T(8,128)(2,1)S(1)}, u32[]{:S(2)}, u32[]{:S(2)}) collective-permute-start(bf16[176,256]{1,0:T(8,128)(2,1)S(1)} %get-tuple-element.127), channel_id=1, source_target_pairs={{0,2},{1,3},{2,0},{3,1},{4,6},{5,7},{6,4},{7,5},{8,10},{9,11},{10,... | collective-permute-start | bytes 270344 | tf_op jit(solution)/shard_map/ppermute | solution.py:33
  99.3 1.0 collective-permute-start.43
  100.3 1.4 collective-permute-start.44
  102.3 6.1 %collective-permute-done.43.refs_2_ = bf16[176,256]{1,0:T(8,128)(2,1)S(1)} collective-permute-done((bf16[176,256]{1,0:T(8,128)(2,1)S(1)}, bf16[176,256]{1,0:T(8,128)(2,1)S(1)}, u32[]{:S(2)}, u32[]{:S(2)}) %collective-permute-start.43) | collective-permute-done | bytes 90144 | tf_op jit(solution)/shard_map/ppermute | solution.py:33
  108.5 1.6 collective-permute-start.47
  110.2 1.4 collective-permute-start.46
  111.6 1.4 collective-permute-start.45
  113.0 2.2 %collective-permute-done.47.refs_3_ = bf16[176,256]{1,0:T(8,128)(2,1)S(1)} collective-permute-done((bf16[176,256]{1,0:T(8,128)(2,1)S(1)}, bf16[176,256]{1,0:T(8,128)(2,1)S(1)}, u32[]{:S(2)}, u32[]{:S(2)}) %collective-permute-start.47) | collective-permute-done | bytes 90144 | tf_op jit(solution)/shard_map/ppermute | solution.py:33
  115.2 2.5 %collective-permute-done.46.refs_2_ = bf16[176,256]{1,0:T(8,128)(2,1)S(1)} collective-permute-done((bf16[176,256]{1,0:T(8,128)(2,1)S(1)}, bf16[176,256]{1,0:T(8,128)(2,1)S(1)}, u32[]{:S(2)}, u32[]{:S(2)}) %collective-permute-start.46) | collective-permute-done | bytes 90144 | tf_op jit(solution)/shard_map/ppermute | solution.py:33
  117.8 1.5 collective-permute-start.50
  119.3 2.8 %collective-permute-start.49 = (bf16[704,256]{1,0:T(8,128)(2,1)S(1)}, bf16[704,256]{1,0:T(8,128)(2,1)S(1)}, u32[]{:S(2)}, u32[]{:S(2)}) collective-permute-start(bf16[704,256]{1,0:T(8,128)(2,1)S(1)} %bitcast.72), channel_id=1, source_target_pairs={{0,16},{8,24},{16,0},{24,8},{1,17},{9,25},{17,1},{25,9},{2,18},{10... | collective-permute-start | bytes 1081352 | tf_op jit(solution)/shard_map/ppermute | solution.py:33
  122.3 2.1 %collective-permute-start.25 = (bf16[448,256]{1,0:T(8,128)(2,1)S(1)}, bf16[448,256]{1,0:T(8,128)(2,1)S(1)}, u32[]{:S(2)}, u32[]{:S(2)}) collective-permute-start(bf16[448,256]{1,0:T(8,128)(2,1)S(1)} %get-tuple-element.111), channel_id=1, source_target_pairs={{0,8},{8,0},{16,24},{24,16},{1,9},{9,1},{17,25},{25,17},{2,10},{10... | collective-permute-start | bytes 688136 | tf_op jit(solution)/shard_map/ppermute | solution.py:33
  124.3 5.8 %collective-permute-done.50.refs_3_ = bf16[704,256]{1,0:T(8,128)(2,1)S(1)} collective-permute-done((bf16[704,256]{1,0:T(8,128)(2,1)S(1)}, bf16[704,256]{1,0:T(8,128)(2,1)S(1)}, u32[]{:S(2)}, u32[]{:S(2)}) %collective-permute-start.50) | collective-permute-done | bytes 360480 | tf_op jit(solution)/shard_map/ppermute | solution.py:33
  130.1 1.4 collective-permute-start.27
  131.6 4.3 %collective-permute-done.49.refs_2_ = bf16[704,256]{1,0:T(8,128)(2,1)S(1)} collective-permute-done((bf16[704,256]{1,0:T(8,128)(2,1)S(1)}, bf16[704,256]{1,0:T(8,128)(2,1)S(1)}, u32[]{:S(2)}, u32[]{:S(2)}) %collective-permute-start.49) | collective-permute-done | bytes 360480 | tf_op jit(solution)/shard_map/ppermute | solution.py:33
  135.9 1.8 %collective-permute-done.48.refs_1_ = bf16[704,256]{1,0:T(8,128)(2,1)S(1)} collective-permute-done((bf16[704,256]{1,0:T(8,128)(2,1)S(1)}, bf16[704,256]{1,0:T(8,128)(2,1)S(1)}, u32[]{:S(2)}, u32[]{:S(2)}) %collective-permute-start.48) | collective-permute-done | bytes 360480 | tf_op jit(solution)/shard_map/ppermute | solution.py:33
  137.9 4.7 %collective-permute-done.25 = bf16[448,256]{1,0:T(8,128)(2,1)S(1)} collective-permute-done((bf16[448,256]{1,0:T(8,128)(2,1)S(1)}, bf16[448,256]{1,0:T(8,128)(2,1)S(1)}, u32[]{:S(2)}, u32[]{:S(2)}) %collective-permute-start.25) | collective-permute-done | bytes 229408 | tf_op jit(solution)/shard_map/ppermute | solution.py:33
  142.6 2.4 %collective-permute-done.27 = bf16[448,256]{1,0:T(8,128)(2,1)S(1)} collective-permute-done((bf16[448,256]{1,0:T(8,128)(2,1)S(1)}, bf16[448,256]{1,0:T(8,128)(2,1)S(1)}, u32[]{:S(2)}, u32[]{:S(2)}) %collective-permute-start.27) | collective-permute-done | bytes 229408 | tf_op jit(solution)/shard_map/ppermute | solution.py:33
  145.3 4.3 %collective-permute-start.30 = (bf16[112,256]{1,0:T(8,128)(2,1)S(1)}, bf16[112,256]{1,0:T(8,128)(2,1)S(1)}, u32[]{:S(2)}, u32[]{:S(2)}) collective-permute-start(bf16[112,256]{1,0:T(8,128)(2,1)S(1)} %get-tuple-element.117), channel_id=1, source_target_pairs={{0,6},{1,7},{2,4},{3,5},{4,2},{5,3},{6,0},{7,1},{8,14},{9,15},{10,... | collective-permute-start | bytes 172040 | tf_op jit(solution)/shard_map/ppermute | solution.py:33
  150.4 2.1 %collective-permute-done.30.refs_3_ = bf16[112,256]{1,0:T(8,128)(2,1)S(1)} collective-permute-done((bf16[112,256]{1,0:T(8,128)(2,1)S(1)}, bf16[112,256]{1,0:T(8,128)(2,1)S(1)}, u32[]{:S(2)}, u32[]{:S(2)}) %collective-permute-start.30) | collective-permute-done | bytes 57376 | tf_op jit(solution)/shard_map/ppermute | solution.py:33
  152.5 3.2 %collective-permute-start.33 = (bf16[112,256]{1,0:T(8,128)(2,1)S(1)}, bf16[112,256]{1,0:T(8,128)(2,1)S(1)}, u32[]{:S(2)}, u32[]{:S(2)}) collective-permute-start(bf16[112,256]{1,0:T(8,128)(2,1)S(1)} %shard_map.266.refs_0_), channel_id=1, source_target_pairs={{0,6},{1,7},{2,4},{3,5},{4,2},{5,3},{6,0},{7,1},{8,14},{9,15},{10,... | collective-permute-start | bytes 172040 | tf_op jit(solution)/shard_map/ppermute | solution.py:33
  155.7 1.3 collective-permute-start.31
  157.0 1.6 collective-permute-done.33.refs_3_
  158.5 2.2 %collective-permute-done.32.refs_2_ = bf16[112,256]{1,0:T(8,128)(2,1)S(1)} collective-permute-done((bf16[112,256]{1,0:T(8,128)(2,1)S(1)}, bf16[112,256]{1,0:T(8,128)(2,1)S(1)}, u32[]{:S(2)}, u32[]{:S(2)}) %collective-permute-start.32) | collective-permute-done | bytes 57376 | tf_op jit(solution)/shard_map/ppermute | solution.py:33
  160.8 1.5 collective-permute-start.36
  162.3 4.3 %collective-permute-start.35 = (bf16[448,256]{1,0:T(8,128)(2,1)S(1)}, bf16[448,256]{1,0:T(8,128)(2,1)S(1)}, u32[]{:S(2)}, u32[]{:S(2)}) collective-permute-start(bf16[448,256]{1,0:T(8,128)(2,1)S(1)} %bitcast.76), channel_id=1, source_target_pairs={{0,16},{8,24},{16,0},{24,8},{1,17},{9,25},{17,1},{25,9},{2,18},{10... | collective-permute-start | bytes 688136 | tf_op jit(solution)/shard_map/ppermute | solution.py:33
  166.6 3.2 %collective-permute-done.36.refs_3_ = bf16[448,256]{1,0:T(8,128)(2,1)S(1)} collective-permute-done((bf16[448,256]{1,0:T(8,128)(2,1)S(1)}, bf16[448,256]{1,0:T(8,128)(2,1)S(1)}, u32[]{:S(2)}, u32[]{:S(2)}) %collective-permute-start.36) | collective-permute-done | bytes 229408 | tf_op jit(solution)/shard_map/ppermute | solution.py:33
  169.8 1.8 collective-permute-done.35.refs_2_
  172.8 2.1 %shard_map.261 = bf16[196,4,1024]{2,1,0:T(4,128)(2,1)} custom-call(f32[8,256]{1,0:T(8,128)S(1)} %get-tuple-element.77.refs_4_.refs_0_, bf16[196,4,1024]{2,1,0:T(4,128)(2,1)S(1)} %bitcast.64, f32[784,1024]{1,0:T(8,128)S(1)} %get-tuple-element.90.refs_9_.refs_2_, bf16[784,256]{1,0:T(8,128)(2,1)S(1)} %shard_map.260.refs_3_.refs_4_, bf16[1024,256]{1,0:T(8,128)(2,1)S(1)} %copy-done.5), custom_call_target="tpu_custom_call" | custom-call | flops 411041792 | bytes 7356416 | tf_op jit(solution)/shard_map/pallas_call | solution.py:516
  175.3 2.0 %shard_map.269 = (f32[9,256,256]{2,1,0:T(8,128)}, f32[1,1024,256]{2,1,0:T(8,128)}, f32[2,256]{1,0:T(2,128)}, f32[2,256]{1,0:T(2,128)}, f32[2,1024]{1,0:T(2,128)}, /*index=5*/f32[2,256]{1,0:T(2,128)}, f32[2,256]{1,0:T(2,128)}) custom-call(bf16[1792,256]{1,0:T(8,128)(2,1)S(1)} %bitcast.68, bf16[1792,256]{1,0:T(8,128)(2,1)S(1)} %collective-permute-done.37.refs_1_), custom_call_target="tpu_custom_call" | custom-call | flops 1048576 | bytes 5259264 | tf_op jit(solution)/shard_map/pallas_call | solution.py:516
  177.2 2.8 %shard_map.275 = (f32[9,256,256]{2,1,0:T(8,128)}, f32[9,256,256]{2,1,0:T(8,128)}, f32[256,1024]{1,0:T(8,128)}) custom-call(bf16[2816,256]{1,0:T(8,128)(2,1)S(1)} %bitcast.66, bf16[2816,256]{1,0:T(8,128)(2,1)S(1)} %collective-permute-done.51.refs_1_), custom_call_target="tpu_custom_call" | custom-call | flops 1048576 | bytes 8650752 | tf_op jit(solution)/shard_map/pallas_call | solution.py:516
  (96 shorter events, 18.2 us)
Async XLA Ops:
  0.6 15.1 %copy-start.3 = (bf16[3,3,256,256]{3,2,1,0:T(8,128)(2,1)S(1)}, bf16[3,3,256,256]{3,2,1,0:T(8,128)(2,1)}, u32[]{:S(2)}) copy-start(bf16[3,3,256,256]{3,2,1,0:T(8,128)(2,1)} %refs_16_.1) | copy-start | bytes 3538948
  0.7 15.1 %copy-start.4 = (bf16[3,3,256,256]{3,2,1,0:T(8,128)(2,1)S(1)}, bf16[3,3,256,256]{3,2,1,0:T(8,128)(2,1)}, u32[]{:S(2)}) copy-start(bf16[3,3,256,256]{3,2,1,0:T(8,128)(2,1)} %refs_12_.5) | copy-start | bytes 3538948
  0.7 15.1 %copy-start.10 = (f32[2,256]{1,0:T(2,128)S(1)}, f32[2,256]{1,0:T(2,128)}, u32[]{:S(2)}) copy-start(f32[2,256]{1,0:T(2,128)} %refs_8_.3) | copy-start | bytes 6148
  0.7 15.1 %copy-start.12 = (f32[2,256]{1,0:T(2,128)S(1)}, f32[2,256]{1,0:T(2,128)}, u32[]{:S(2)}) copy-start(f32[2,256]{1,0:T(2,128)} %refs_5_.1) | copy-start | bytes 6148
  4.9 1.3 collective-permute-start
  6.2 6.6 %collective-permute-start.3 = (f32[16,128]{1,0:T(8,128)S(1)}, f32[16,128]{1,0:T(8,128)S(1)}, u32[]{:S(2)}, u32[]{:S(2)}) collective-permute-start(f32[16,128]{1,0:T(8,128)S(1)} %add.18.refs_0_), channel_id=1, source_target_pairs={{0,6},{1,7},{2,4},{3,5},{4,2},{5,3},{6,0},{7,1},{8,14},{9,15},{10,... | collective-permute-start | bytes 24584 | tf_op jit(solution)/shard_map/ppermute | solution.py:33
  11.2 4.5 %collective-permute-start.2 = (f32[16,128]{1,0:T(8,128)S(1)}, f32[16,128]{1,0:T(8,128)S(1)}, u32[]{:S(2)}, u32[]{:S(2)}) collective-permute-start(f32[16,128]{1,0:T(8,128)S(1)} %add.18.refs_0_), channel_id=1, source_target_pairs={{0,4},{1,5},{2,6},{3,7},{4,0},{5,1},{6,2},{7,3},{8,12},{9,13},{10,... | collective-permute-start | bytes 24584 | tf_op jit(solution)/shard_map/ppermute | solution.py:33
  11.2 4.5 %collective-permute-start.1 = (f32[16,128]{1,0:T(8,128)S(1)}, f32[16,128]{1,0:T(8,128)S(1)}, u32[]{:S(2)}, u32[]{:S(2)}) collective-permute-start(f32[16,128]{1,0:T(8,128)S(1)} %add.18.refs_0_), channel_id=1, source_target_pairs={{0,2},{1,3},{2,0},{3,1},{4,6},{5,7},{6,4},{7,5},{8,10},{9,11},{10,... | collective-permute-start | bytes 24584 | tf_op jit(solution)/shard_map/ppermute | solution.py:33
  15.8 9.8 %copy-start.2 = (bf16[256,1024]{1,0:T(8,128)(2,1)S(1)}, bf16[256,1024]{1,0:T(8,128)(2,1)}, u32[]{:S(2)}) copy-start(bf16[256,1024]{1,0:T(8,128)(2,1)} %refs_13_.3) | copy-start | bytes 1572868
  15.8 9.8 %copy-start.6 = (bf16[1,4,14,14,256]{4,1,3,2,0:T(4,128)(2,1)S(1)}, bf16[1,4,14,14,256]{4,1,3,2,0:T(4,128)(2,1)}, u32[]{:S(2)}) copy-start(bf16[1,4,14,14,256]{4,1,3,2,0:T(4,128)(2,1)} %param.16) | copy-start | bytes 1204228
  15.8 9.8 %copy-start.7 = (bf16[1,4,14,14,256]{4,1,3,2,0:T(4,128)(2,1)S(1)}, bf16[1,4,14,14,256]{4,1,3,2,0:T(4,128)(2,1)}, u32[]{:S(2)}) copy-start(bf16[1,4,14,14,256]{4,1,3,2,0:T(4,128)(2,1)} %param.18) | copy-start | bytes 1204228
  15.8 9.8 %copy-start.9 = (f32[2,256]{1,0:T(2,128)S(1)}, f32[2,256]{1,0:T(2,128)}, u32[]{:S(2)}) copy-start(f32[2,256]{1,0:T(2,128)} %refs_10_.5) | copy-start | bytes 6148
  15.8 20.7 %copy-start.1 = (bf16[1,4,14,14,1024]{4,1,3,2,0:T(4,128)(2,1)S(1)}, bf16[1,4,14,14,1024]{4,1,3,2,0:T(4,128)(2,1)}, u32[]{:S(2)}) copy-start(bf16[1,4,14,14,1024]{4,1,3,2,0:T(4,128)(2,1)} %param.17) | copy-start | bytes 4816900
  18.3 1.2 collective-permute-start.4
  19.6 5.4 %collective-permute-start.7 = (f32[8,128]{1,0:T(8,128)S(1)}, f32[8,128]{1,0:T(8,128)S(1)}, u32[]{:S(2)}, u32[]{:S(2)}) collective-permute-start(f32[8,128]{1,0:T(8,128)S(1)} %add.19.refs_0_), channel_id=1, source_target_pairs={{0,6},{1,7},{2,4},{3,5},{4,2},{5,3},{6,0},{7,1},{8,14},{9,15},{10,... | collective-permute-start | bytes 12296 | tf_op jit(solution)/shard_map/ppermute | solution.py:33
  21.0 4.5 %collective-permute-start.6 = (f32[8,128]{1,0:T(8,128)S(1)}, f32[8,128]{1,0:T(8,128)S(1)}, u32[]{:S(2)}, u32[]{:S(2)}) collective-permute-start(f32[8,128]{1,0:T(8,128)S(1)} %add.19.refs_0_), channel_id=1, source_target_pairs={{0,4},{1,5},{2,6},{3,7},{4,0},{5,1},{6,2},{7,3},{8,12},{9,13},{10,... | collective-permute-start | bytes 12296 | tf_op jit(solution)/shard_map/ppermute | solution.py:33
  21.6 4.0 %collective-permute-start.5 = (f32[8,128]{1,0:T(8,128)S(1)}, f32[8,128]{1,0:T(8,128)S(1)}, u32[]{:S(2)}, u32[]{:S(2)}) collective-permute-start(f32[8,128]{1,0:T(8,128)S(1)} %add.19.refs_0_), channel_id=1, source_target_pairs={{0,2},{1,3},{2,0},{3,1},{4,6},{5,7},{6,4},{7,5},{8,10},{9,11},{10,... | collective-permute-start | bytes 12296 | tf_op jit(solution)/shard_map/ppermute | solution.py:33
  25.6 10.9 %copy-start = (bf16[1,4,14,14,1024]{4,1,3,2,0:T(4,128)(2,1)S(1)}, bf16[1,4,14,14,1024]{4,1,3,2,0:T(4,128)(2,1)}, u32[]{:S(2)}) copy-start(bf16[1,4,14,14,1024]{4,1,3,2,0:T(4,128)(2,1)} %param.15) | copy-start | bytes 4816900
  25.6 10.9 %copy-start.8 = (f32[2,1024]{1,0:T(2,128)S(1)}, f32[2,1024]{1,0:T(2,128)}, u32[]{:S(2)}) copy-start(f32[2,1024]{1,0:T(2,128)} %refs_11_.4) | copy-start | bytes 24580
  28.0 1.2 collective-permute-start.8
  29.2 5.6 %collective-permute-start.11 = (f32[24,128]{1,0:T(8,128)S(1)}, f32[24,128]{1,0:T(8,128)S(1)}, u32[]{:S(2)}, u32[]{:S(2)}) collective-permute-start(f32[24,128]{1,0:T(8,128)S(1)} %add.20.refs_0_), channel_id=1, source_target_pairs={{0,6},{1,7},{2,4},{3,5},{4,2},{5,3},{6,0},{7,1},{8,14},{9,15},{10,... | collective-permute-start | bytes 36872 | tf_op jit(solution)/shard_map/ppermute | solution.py:33
  31.8 4.6 %collective-permute-start.10 = (f32[24,128]{1,0:T(8,128)S(1)}, f32[24,128]{1,0:T(8,128)S(1)}, u32[]{:S(2)}, u32[]{:S(2)}) collective-permute-start(f32[24,128]{1,0:T(8,128)S(1)} %add.20.refs_0_), channel_id=1, source_target_pairs={{0,4},{1,5},{2,6},{3,7},{4,0},{5,1},{6,2},{7,3},{8,12},{9,13},{10,... | collective-permute-start | bytes 36872 | tf_op jit(solution)/shard_map/ppermute | solution.py:33
  32.7 3.8 %collective-permute-start.9 = (f32[24,128]{1,0:T(8,128)S(1)}, f32[24,128]{1,0:T(8,128)S(1)}, u32[]{:S(2)}, u32[]{:S(2)}) collective-permute-start(f32[24,128]{1,0:T(8,128)S(1)} %add.20.refs_0_), channel_id=1, source_target_pairs={{0,2},{1,3},{2,0},{3,1},{4,6},{5,7},{6,4},{7,5},{8,10},{9,11},{10,... | collective-permute-start | bytes 36872 | tf_op jit(solution)/shard_map/ppermute | solution.py:33
  42.6 1.2 collective-permute-start.12
  43.8 5.5 %collective-permute-start.15 = (f32[24,128]{1,0:T(8,128)S(1)}, f32[24,128]{1,0:T(8,128)S(1)}, u32[]{:S(2)}, u32[]{:S(2)}) collective-permute-start(f32[24,128]{1,0:T(8,128)S(1)} %add.21.refs_0_), channel_id=1, source_target_pairs={{0,6},{1,7},{2,4},{3,5},{4,2},{5,3},{6,0},{7,1},{8,14},{9,15},{10,... | collective-permute-start | bytes 36872 | tf_op jit(solution)/shard_map/ppermute | solution.py:33
  45.1 4.6 %collective-permute-start.14 = (f32[24,128]{1,0:T(8,128)S(1)}, f32[24,128]{1,0:T(8,128)S(1)}, u32[]{:S(2)}, u32[]{:S(2)}) collective-permute-start(f32[24,128]{1,0:T(8,128)S(1)} %add.21.refs_0_), channel_id=1, source_target_pairs={{0,4},{1,5},{2,6},{3,7},{4,0},{5,1},{6,2},{7,3},{8,12},{9,13},{10,... | collective-permute-start | bytes 36872 | tf_op jit(solution)/shard_map/ppermute | solution.py:33
  46.1 3.8 %collective-permute-start.13 = (f32[24,128]{1,0:T(8,128)S(1)}, f32[24,128]{1,0:T(8,128)S(1)}, u32[]{:S(2)}, u32[]{:S(2)}) collective-permute-start(f32[24,128]{1,0:T(8,128)S(1)} %add.21.refs_0_), channel_id=1, source_target_pairs={{0,2},{1,3},{2,0},{3,1},{4,6},{5,7},{6,4},{7,5},{8,10},{9,11},{10,... | collective-permute-start | bytes 36872 | tf_op jit(solution)/shard_map/ppermute | solution.py:33
  55.4 21.4 %collective-permute-start.38 = (bf16[2816,256]{1,0:T(8,128)(2,1)S(1)}, bf16[2816,256]{1,0:T(8,128)(2,1)S(1)}, u32[]{:S(2)}, u32[]{:S(2)}) collective-permute-start(bf16[2816,256]{1,0:T(8,128)(2,1)S(1)} %get-tuple-element.121), channel_id=1, source_target_pairs={{0,1},{1,0},{2,3},{3,2},{4,5},{5,4},{6,7},{7,6},{8,9},{9,8},{10,11... | collective-permute-start | bytes 4325384 | tf_op jit(solution)/shard_map/ppermute | solution.py:33
  55.5 3.2 %collective-permute-start.16 = (f32[8,128]{1,0:T(8,128)S(1)}, f32[8,128]{1,0:T(8,128)S(1)}, u32[]{:S(2)}, u32[]{:S(2)}) collective-permute-start(f32[8,128]{1,0:T(8,128)S(1)} %get-tuple-element.93.refs_6_), channel_id=1, source_target_pairs={{0,1},{1,0},{2,3},{3,2},{4,5},{5,4},{6,7},{7,6},{8,9},{9,8},{10,11... | collective-permute-start | bytes 12296 | tf_op jit(solution)/shard_map/ppermute | solution.py:33
  58.7 5.4 %collective-permute-start.19 = (f32[8,128]{1,0:T(8,128)S(1)}, f32[8,128]{1,0:T(8,128)S(1)}, u32[]{:S(2)}, u32[]{:S(2)}) collective-permute-start(f32[8,128]{1,0:T(8,128)S(1)} %add.22.refs_0_), channel_id=1, source_target_pairs={{0,6},{1,7},{2,4},{3,5},{4,2},{5,3},{6,0},{7,1},{8,14},{9,15},{10,... | collective-permute-start | bytes 12296 | tf_op jit(solution)/shard_map/ppermute | solution.py:33
  61.2 4.5 %collective-permute-start.18 = (f32[8,128]{1,0:T(8,128)S(1)}, f32[8,128]{1,0:T(8,128)S(1)}, u32[]{:S(2)}, u32[]{:S(2)}) collective-permute-start(f32[8,128]{1,0:T(8,128)S(1)} %add.22.refs_0_), channel_id=1, source_target_pairs={{0,4},{1,5},{2,6},{3,7},{4,0},{5,1},{6,2},{7,3},{8,12},{9,13},{10,... | collective-permute-start | bytes 12296 | tf_op jit(solution)/shard_map/ppermute | solution.py:33
  62.2 3.6 %collective-permute-start.17 = (f32[8,128]{1,0:T(8,128)S(1)}, f32[8,128]{1,0:T(8,128)S(1)}, u32[]{:S(2)}, u32[]{:S(2)}) collective-permute-start(f32[8,128]{1,0:T(8,128)S(1)} %add.22.refs_0_), channel_id=1, source_target_pairs={{0,2},{1,3},{2,0},{3,1},{4,6},{5,7},{6,4},{7,5},{8,10},{9,11},{10,... | collective-permute-start | bytes 12296 | tf_op jit(solution)/shard_map/ppermute | solution.py:33
  67.1 1.2 collective-permute-start.20
  68.4 5.4 %collective-permute-start.23 = (f32[8,128]{1,0:T(8,128)S(1)}, f32[8,128]{1,0:T(8,128)S(1)}, u32[]{:S(2)}, u32[]{:S(2)}) collective-permute-start(f32[8,128]{1,0:T(8,128)S(1)} %add.23.refs_0_), channel_id=1, source_target_pairs={{0,6},{1,7},{2,4},{3,5},{4,2},{5,3},{6,0},{7,1},{8,14},{9,15},{10,... | collective-permute-start | bytes 12296 | tf_op jit(solution)/shard_map/ppermute | solution.py:33
  69.7 4.5 %collective-permute-start.22 = (f32[8,128]{1,0:T(8,128)S(1)}, f32[8,128]{1,0:T(8,128)S(1)}, u32[]{:S(2)}, u32[]{:S(2)}) collective-permute-start(f32[8,128]{1,0:T(8,128)S(1)} %add.23.refs_0_), channel_id=1, source_target_pairs={{0,4},{1,5},{2,6},{3,7},{4,0},{5,1},{6,2},{7,3},{8,12},{9,13},{10,... | collective-permute-start | bytes 12296 | tf_op jit(solution)/shard_map/ppermute | solution.py:33
  70.7 3.6 %collective-permute-start.21 = (f32[8,128]{1,0:T(8,128)S(1)}, f32[8,128]{1,0:T(8,128)S(1)}, u32[]{:S(2)}, u32[]{:S(2)}) collective-permute-start(f32[8,128]{1,0:T(8,128)S(1)} %add.23.refs_0_), channel_id=1, source_target_pairs={{0,2},{1,3},{2,0},{3,1},{4,6},{5,7},{6,4},{7,5},{8,10},{9,11},{10,... | collective-permute-start | bytes 12296 | tf_op jit(solution)/shard_map/ppermute | solution.py:33
  76.8 45.3 %collective-permute-start.24 = (bf16[1792,256]{1,0:T(8,128)(2,1)S(1)}, bf16[1792,256]{1,0:T(8,128)(2,1)S(1)}, u32[]{:S(2)}, u32[]{:S(2)}) collective-permute-start(bf16[1792,256]{1,0:T(8,128)(2,1)S(1)} %get-tuple-element.109), channel_id=1, source_target_pairs={{0,1},{1,0},{2,3},{3,2},{4,5},{5,4},{6,7},{7,6},{8,9},{9,8},{10,11... | collective-permute-start | bytes 2752520 | tf_op jit(solution)/shard_map/ppermute | solution.py:33
  77.2 11.3 %collective-permute-start.39 = (bf16[704,256]{1,0:T(8,128)(2,1)S(1)}, bf16[704,256]{1,0:T(8,128)(2,1)S(1)}, u32[]{:S(2)}, u32[]{:S(2)}) collective-permute-start(bf16[704,256]{1,0:T(8,128)(2,1)S(1)} %get-tuple-element.123), channel_id=1, source_target_pairs={{0,8},{8,0},{16,24},{24,16},{1,9},{9,1},{17,25},{25,17},{2,10},{10... | collective-permute-start | bytes 1081352 | tf_op jit(solution)/shard_map/ppermute | solution.py:33
  78.8 18.2 %collective-permute-start.40 = (bf16[704,256]{1,0:T(8,128)(2,1)S(1)}, bf16[704,256]{1,0:T(8,128)(2,1)S(1)}, u32[]{:S(2)}, u32[]{:S(2)}) collective-permute-start(bf16[704,256]{1,0:T(8,128)(2,1)S(1)} %get-tuple-element.124), channel_id=1, source_target_pairs={{0,16},{8,24},{16,0},{24,8},{1,17},{9,25},{17,1},{25,9},{2,18},{10... | collective-permute-start | bytes 1081352 | tf_op jit(solution)/shard_map/ppermute | solution.py:33
  80.3 16.7 %collective-permute-start.41 = (bf16[704,256]{1,0:T(8,128)(2,1)S(1)}, bf16[704,256]{1,0:T(8,128)(2,1)S(1)}, u32[]{:S(2)}, u32[]{:S(2)}) collective-permute-start(bf16[704,256]{1,0:T(8,128)(2,1)S(1)} %get-tuple-element.125), channel_id=1, source_target_pairs={{0,24},{8,16},{16,8},{24,0},{1,25},{9,17},{17,9},{25,1},{2,26},{10... | collective-permute-start | bytes 1081352 | tf_op jit(solution)/shard_map/ppermute | solution.py:33
  97.2 5.2 %collective-permute-start.42 = (bf16[176,256]{1,0:T(8,128)(2,1)S(1)}, bf16[176,256]{1,0:T(8,128)(2,1)S(1)}, u32[]{:S(2)}, u32[]{:S(2)}) collective-permute-start(bf16[176,256]{1,0:T(8,128)(2,1)S(1)} %get-tuple-element.127), channel_id=1, source_target_pairs={{0,2},{1,3},{2,0},{3,1},{4,6},{5,7},{6,4},{7,5},{8,10},{9,11},{10,... | collective-permute-start | bytes 270344 | tf_op jit(solution)/shard_map/ppermute | solution.py:33
  99.3 9.2 %collective-permute-start.43 = (bf16[176,256]{1,0:T(8,128)(2,1)S(1)}, bf16[176,256]{1,0:T(8,128)(2,1)S(1)}, u32[]{:S(2)}, u32[]{:S(2)}) collective-permute-start(bf16[176,256]{1,0:T(8,128)(2,1)S(1)} %get-tuple-element.128), channel_id=1, source_target_pairs={{0,4},{1,5},{2,6},{3,7},{4,0},{5,1},{6,2},{7,3},{8,12},{9,13},{10,... | collective-permute-start | bytes 270344 | tf_op jit(solution)/shard_map/ppermute | solution.py:33
  100.3 8.2 %collective-permute-start.44 = (bf16[176,256]{1,0:T(8,128)(2,1)S(1)}, bf16[176,256]{1,0:T(8,128)(2,1)S(1)}, u32[]{:S(2)}, u32[]{:S(2)}) collective-permute-start(bf16[176,256]{1,0:T(8,128)(2,1)S(1)} %get-tuple-element.129), channel_id=1, source_target_pairs={{0,6},{1,7},{2,4},{3,5},{4,2},{5,3},{6,0},{7,1},{8,14},{9,15},{10,... | collective-permute-start | bytes 270344 | tf_op jit(solution)/shard_map/ppermute | solution.py:33
  108.5 6.7 %collective-permute-start.47 = (bf16[176,256]{1,0:T(8,128)(2,1)S(1)}, bf16[176,256]{1,0:T(8,128)(2,1)S(1)}, u32[]{:S(2)}, u32[]{:S(2)}) collective-permute-start(bf16[176,256]{1,0:T(8,128)(2,1)S(1)} %shard_map.272.refs_0_), channel_id=1, source_target_pairs={{0,6},{1,7},{2,4},{3,5},{4,2},{5,3},{6,0},{7,1},{8,14},{9,15},{10,... | collective-permute-start | bytes 270344 | tf_op jit(solution)/shard_map/ppermute | solution.py:33
  110.2 7.5 %collective-permute-start.46 = (bf16[176,256]{1,0:T(8,128)(2,1)S(1)}, bf16[176,256]{1,0:T(8,128)(2,1)S(1)}, u32[]{:S(2)}, u32[]{:S(2)}) collective-permute-start(bf16[176,256]{1,0:T(8,128)(2,1)S(1)} %shard_map.272.refs_0_), channel_id=1, source_target_pairs={{0,4},{1,5},{2,6},{3,7},{4,0},{5,1},{6,2},{7,3},{8,12},{9,13},{10,... | collective-permute-start | bytes 270344 | tf_op jit(solution)/shard_map/ppermute | solution.py:33
  111.6 6.1 %collective-permute-start.45 = (bf16[176,256]{1,0:T(8,128)(2,1)S(1)}, bf16[176,256]{1,0:T(8,128)(2,1)S(1)}, u32[]{:S(2)}, u32[]{:S(2)}) collective-permute-start(bf16[176,256]{1,0:T(8,128)(2,1)S(1)} %shard_map.272.refs_0_), channel_id=1, source_target_pairs={{0,2},{1,3},{2,0},{3,1},{4,6},{5,7},{6,4},{7,5},{8,10},{9,11},{10,... | collective-permute-start | bytes 270344 | tf_op jit(solution)/shard_map/ppermute | solution.py:33
  117.8 12.4 %collective-permute-start.50 = (bf16[704,256]{1,0:T(8,128)(2,1)S(1)}, bf16[704,256]{1,0:T(8,128)(2,1)S(1)}, u32[]{:S(2)}, u32[]{:S(2)}) collective-permute-start(bf16[704,256]{1,0:T(8,128)(2,1)S(1)} %bitcast.71), channel_id=1, source_target_pairs={{0,24},{8,16},{16,8},{24,0},{1,25},{9,17},{17,9},{25,1},{2,26},{10... | collective-permute-start | bytes 1081352 | tf_op jit(solution)/shard_map/ppermute | solution.py:33
  119.3 16.6 %collective-permute-start.49 = (bf16[704,256]{1,0:T(8,128)(2,1)S(1)}, bf16[704,256]{1,0:T(8,128)(2,1)S(1)}, u32[]{:S(2)}, u32[]{:S(2)}) collective-permute-start(bf16[704,256]{1,0:T(8,128)(2,1)S(1)} %bitcast.72), channel_id=1, source_target_pairs={{0,16},{8,24},{16,0},{24,8},{1,17},{9,25},{17,1},{25,9},{2,18},{10... | collective-permute-start | bytes 1081352 | tf_op jit(solution)/shard_map/ppermute | solution.py:33
  122.0 15.7 %collective-permute-start.48 = (bf16[704,256]{1,0:T(8,128)(2,1)S(1)}, bf16[704,256]{1,0:T(8,128)(2,1)S(1)}, u32[]{:S(2)}, u32[]{:S(2)}) collective-permute-start(bf16[704,256]{1,0:T(8,128)(2,1)S(1)} %bitcast.73), channel_id=1, source_target_pairs={{0,8},{8,0},{16,24},{24,16},{1,9},{9,1},{17,25},{25,17},{2,10},{10... | collective-permute-start | bytes 1081352 | tf_op jit(solution)/shard_map/ppermute | solution.py:33
  122.3 20.4 %collective-permute-start.25 = (bf16[448,256]{1,0:T(8,128)(2,1)S(1)}, bf16[448,256]{1,0:T(8,128)(2,1)S(1)}, u32[]{:S(2)}, u32[]{:S(2)}) collective-permute-start(bf16[448,256]{1,0:T(8,128)(2,1)S(1)} %get-tuple-element.111), channel_id=1, source_target_pairs={{0,8},{8,0},{16,24},{24,16},{1,9},{9,1},{17,25},{25,17},{2,10},{10... | collective-permute-start | bytes 688136 | tf_op jit(solution)/shard_map/ppermute | solution.py:33
  124.3 18.3 %collective-permute-start.26 = (bf16[448,256]{1,0:T(8,128)(2,1)S(1)}, bf16[448,256]{1,0:T(8,128)(2,1)S(1)}, u32[]{:S(2)}, u32[]{:S(2)}) collective-permute-start(bf16[448,256]{1,0:T(8,128)(2,1)S(1)} %get-tuple-element.112), channel_id=1, source_target_pairs={{0,16},{8,24},{16,0},{24,8},{1,17},{9,25},{17,1},{25,9},{2,18},{10... | collective-permute-start | bytes 688136 | tf_op jit(solution)/shard_map/ppermute | solution.py:33
  130.1 14.9 %collective-permute-start.27 = (bf16[448,256]{1,0:T(8,128)(2,1)S(1)}, bf16[448,256]{1,0:T(8,128)(2,1)S(1)}, u32[]{:S(2)}, u32[]{:S(2)}) collective-permute-start(bf16[448,256]{1,0:T(8,128)(2,1)S(1)} %get-tuple-element.113), channel_id=1, source_target_pairs={{0,24},{8,16},{16,8},{24,0},{1,25},{9,17},{17,9},{25,1},{2,26},{10... | collective-permute-start | bytes 688136 | tf_op jit(solution)/shard_map/ppermute | solution.py:33
  137.8 39.4 %collective-permute-start.51 = (bf16[2816,256]{1,0:T(8,128)(2,1)S(1)}, bf16[2816,256]{1,0:T(8,128)(2,1)S(1)}, u32[]{:S(2)}, u32[]{:S(2)}) collective-permute-start(bf16[2816,256]{1,0:T(8,128)(2,1)S(1)} %bitcast.65), channel_id=1, source_target_pairs={{0,1},{1,0},{2,3},{3,2},{4,5},{5,4},{6,7},{7,6},{8,9},{9,8},{10,11... | collective-permute-start | bytes 4325384 | tf_op jit(solution)/shard_map/ppermute | solution.py:33
  145.1 27.7 %copy-start.5 = (bf16[1024,256]{1,0:T(8,128)(2,1)S(1)}, bf16[1024,256]{1,0:T(8,128)(2,1)}, u32[]{:S(2)}) copy-start(bf16[1024,256]{1,0:T(8,128)(2,1)} %refs_4_.3) | copy-start | bytes 1572868
  145.1 4.5 %collective-permute-start.28 = (bf16[112,256]{1,0:T(8,128)(2,1)S(1)}, bf16[112,256]{1,0:T(8,128)(2,1)S(1)}, u32[]{:S(2)}, u32[]{:S(2)}) collective-permute-start(bf16[112,256]{1,0:T(8,128)(2,1)S(1)} %get-tuple-element.115), channel_id=1, source_target_pairs={{0,2},{1,3},{2,0},{3,1},{4,6},{5,7},{6,4},{7,5},{8,10},{9,11},{10,... | collective-permute-start | bytes 172040 | tf_op jit(solution)/shard_map/ppermute | solution.py:33
  145.2 5.1 %collective-permute-start.29 = (bf16[112,256]{1,0:T(8,128)(2,1)S(1)}, bf16[112,256]{1,0:T(8,128)(2,1)S(1)}, u32[]{:S(2)}, u32[]{:S(2)}) collective-permute-start(bf16[112,256]{1,0:T(8,128)(2,1)S(1)} %get-tuple-element.116), channel_id=1, source_target_pairs={{0,4},{1,5},{2,6},{3,7},{4,0},{5,1},{6,2},{7,3},{8,12},{9,13},{10,... | collective-permute-start | bytes 172040 | tf_op jit(solution)/shard_map/ppermute | solution.py:33
  145.3 7.2 %collective-permute-start.30 = (bf16[112,256]{1,0:T(8,128)(2,1)S(1)}, bf16[112,256]{1,0:T(8,128)(2,1)S(1)}, u32[]{:S(2)}, u32[]{:S(2)}) collective-permute-start(bf16[112,256]{1,0:T(8,128)(2,1)S(1)} %get-tuple-element.117), channel_id=1, source_target_pairs={{0,6},{1,7},{2,4},{3,5},{4,2},{5,3},{6,0},{7,1},{8,14},{9,15},{10,... | collective-permute-start | bytes 172040 | tf_op jit(solution)/shard_map/ppermute | solution.py:33
  152.5 6.0 %collective-permute-start.33 = (bf16[112,256]{1,0:T(8,128)(2,1)S(1)}, bf16[112,256]{1,0:T(8,128)(2,1)S(1)}, u32[]{:S(2)}, u32[]{:S(2)}) collective-permute-start(bf16[112,256]{1,0:T(8,128)(2,1)S(1)} %shard_map.266.refs_0_), channel_id=1, source_target_pairs={{0,6},{1,7},{2,4},{3,5},{4,2},{5,3},{6,0},{7,1},{8,14},{9,15},{10,... | collective-permute-start | bytes 172040 | tf_op jit(solution)/shard_map/ppermute | solution.py:33
  155.7 5.1 %collective-permute-start.32 = (bf16[112,256]{1,0:T(8,128)(2,1)S(1)}, bf16[112,256]{1,0:T(8,128)(2,1)S(1)}, u32[]{:S(2)}, u32[]{:S(2)}) collective-permute-start(bf16[112,256]{1,0:T(8,128)(2,1)S(1)} %shard_map.266.refs_0_), channel_id=1, source_target_pairs={{0,4},{1,5},{2,6},{3,7},{4,0},{5,1},{6,2},{7,3},{8,12},{9,13},{10,... | collective-permute-start | bytes 172040 | tf_op jit(solution)/shard_map/ppermute | solution.py:33
  155.7 5.1 %collective-permute-start.31 = (bf16[112,256]{1,0:T(8,128)(2,1)S(1)}, bf16[112,256]{1,0:T(8,128)(2,1)S(1)}, u32[]{:S(2)}, u32[]{:S(2)}) collective-permute-start(bf16[112,256]{1,0:T(8,128)(2,1)S(1)} %shard_map.266.refs_0_), channel_id=1, source_target_pairs={{0,2},{1,3},{2,0},{3,1},{4,6},{5,7},{6,4},{7,5},{8,10},{9,11},{10,... | collective-permute-start | bytes 172040 | tf_op jit(solution)/shard_map/ppermute | solution.py:33
  160.8 9.0 %collective-permute-start.36 = (bf16[448,256]{1,0:T(8,128)(2,1)S(1)}, bf16[448,256]{1,0:T(8,128)(2,1)S(1)}, u32[]{:S(2)}, u32[]{:S(2)}) collective-permute-start(bf16[448,256]{1,0:T(8,128)(2,1)S(1)} %bitcast.75), channel_id=1, source_target_pairs={{0,24},{8,16},{16,8},{24,0},{1,25},{9,17},{17,9},{25,1},{2,26},{10... | collective-permute-start | bytes 688136 | tf_op jit(solution)/shard_map/ppermute | solution.py:33
  162.3 9.3 %collective-permute-start.35 = (bf16[448,256]{1,0:T(8,128)(2,1)S(1)}, bf16[448,256]{1,0:T(8,128)(2,1)S(1)}, u32[]{:S(2)}, u32[]{:S(2)}) collective-permute-start(bf16[448,256]{1,0:T(8,128)(2,1)S(1)} %bitcast.76), channel_id=1, source_target_pairs={{0,16},{8,24},{16,0},{24,8},{1,17},{9,25},{17,1},{25,9},{2,18},{10... | collective-permute-start | bytes 688136 | tf_op jit(solution)/shard_map/ppermute | solution.py:33
  166.6 6.0 %collective-permute-start.34 = (bf16[448,256]{1,0:T(8,128)(2,1)S(1)}, bf16[448,256]{1,0:T(8,128)(2,1)S(1)}, u32[]{:S(2)}, u32[]{:S(2)}) collective-permute-start(bf16[448,256]{1,0:T(8,128)(2,1)S(1)} %bitcast.77), channel_id=1, source_target_pairs={{0,8},{8,0},{16,24},{24,16},{1,9},{9,1},{17,25},{25,17},{2,10},{10... | collective-permute-start | bytes 688136 | tf_op jit(solution)/shard_map/ppermute | solution.py:33
  172.7 2.5 %collective-permute-start.37 = (bf16[1792,256]{1,0:T(8,128)(2,1)S(1)}, bf16[1792,256]{1,0:T(8,128)(2,1)S(1)}, u32[]{:S(2)}, u32[]{:S(2)}) collective-permute-start(bf16[1792,256]{1,0:T(8,128)(2,1)S(1)} %bitcast.67), channel_id=1, source_target_pairs={{0,1},{1,0},{2,3},{3,2},{4,5},{5,4},{6,7},{7,6},{8,9},{9,8},{10,11... | collective-permute-start | bytes 2752520 | tf_op jit(solution)/shard_map/ppermute | solution.py:33
  (2 other events, 11.1 us)
where the time goes:
time: 180 us
  waiting for transfers between devices  82.5 us (46%)
  starting transfers between devices  64 us (36%)
  Pallas kernels  32.5 us (18%)
    ppermute x52, waiting for transfers between devices, swap(): return lax.ppermute(value, axis, [(i, i ^ mask) for i in range(size)])  82.5 us
    ppermute x52, starting transfers between devices, swap(): return lax.ppermute(value, axis, [(i, i ^ mask) for i in range(size)])  64 us
    pallas_call x22, Pallas kernels, call(): pl.pallas_call(body, out_shape=outs, in_specs=[pl.BlockSpec(memory_space=...  32.5 us
  transfers between devices with their start and end apart: 52, of which 41 were waited for; matrix products, arithmetic and copies ran while one was open for 0% of the time, Pallas kernels for 5%

commit v1 on v0

--- a/solution.py
+++ b/solution.py
@@ -9,6 +9,7 @@
 
 EPS = 1e-05
 LANES = 128
+COST = 1024
 F32 = jnp.float32
 BF16 = jnp.bfloat16
 
@@ -229,7 +230,7 @@
 
 
 def kernel_3(parts, mask8, total_1, zs, z2, m, gm, spatial_n, second_n, expand_w, *rest):
-    total_2, sa, ze, motion_out, up2, sums = rest
+    total_2, sa, ze, up2, sums = rest
     channels, wide = zs.shape[1], ze.shape[1]
     step, wide_step = channels // LANES, wide // LANES
     total = total_of(parts)
@@ -253,10 +254,7 @@
     motion = eights(rows_of(m[...]).astype(F32))
     u = second_n[0:1] * hat + second_n[1:2] + motion
     s = sigmoid(u)
-    w = u * s
-    out = mask * w + (1.0 - mask) * motion
-    motion_out[...] = rows_of(out).astype(BF16).reshape(motion_out.shape)
-    up = eights(rows_of(gm[...]).astype(F32)) * mask * (s + w * (1.0 - s))
+    up = eights(rows_of(gm[...]).astype(F32)) * mask * (s + u * s * (1.0 - s))
     up2[...] = rows_of(up)
     put_row(sums, 2 * wide_step, down(up))
     put_row(sums, 2 * wide_step + step, down(up * hat))
@@ -264,7 +262,7 @@
 
 def kernel_4(place, parts, mask8, total_1, total_2, z1, z2, up2, ze, x, gx, *rest):
     expand_n, second_n, first_n, second_w = rest[:4]
-    total_3, iframe_out, upe, up1, same, edge, sums = rest[4:]
+    total_3, upe, up1, same, edge, sums = rest[4:]
     channels, wide = z1.shape[1], ze.shape[1]
     step, wide_step = channels // LANES, wide // LANES
     total = total_of(parts)
@@ -303,10 +301,7 @@
             g_here = eights(rows_of(gx[pixels, :, lanes]).astype(F32))
             u = hat * gain8 + shift8 + x_here
             s = sigmoid(u)
-            w = u * s
-            out = mask * w + (1.0 - mask) * x_here
-            iframe_out[pixels, :, lanes] = rows_of(out).astype(BF16).reshape(-1, frames, part)
-            up = g_here * mask * (s + w * (1.0 - s))
+            up = g_here * mask * (s + u * s * (1.0 - s))
             upe[here, lanes] = rows_of(up)
             cross = up * hat
             return (totals[0] + jnp.sum(up, axis=0), totals[1] + jnp.sum(cross, axis=0))
@@ -368,52 +363,55 @@
     put_row(sums, step, total_cross)
 
 
-def kernel_7(parts, mask8, total_1, upr, zr, reduce_n, back_r):
-    channels = zr.shape[1]
-    step = channels // LANES
-    total = total_of(parts)
-    count = total_1[4 * step : 4 * step + 1, 0:1]
-    mask = mask8[...]
-    mean, scale = moments(total_1[...], 0, step, channels, count)
-    low = back_of(
-        upr[...], zr[...], mean, scale, reduce_n[0:1], row_of(total, 0, channels),
-        row_of(total, step, channels), count, mask,
-    )
-    back_r[...] = low.astype(BF16)
-
-
-def kernel_motion(place, mask8, total_1, total_4, up1, z1, first_n, first_w, m, gm, up2, *rest):
-    same_2, edge_2, mm, sa, back_e, motion_back, kept_ref, sent_ref, same, edge = rest
+def kernel_second(mm, same, edge, kept_ref, sent_ref):
+    conv_grad_to(core_here(), mm[...], same, edge, kept_ref, sent_ref, 0)
+
+
+def kernel_first(place, mask8, total_1, total_4, up1, z1, first_n, m, sa, back_e, *rest):
+    kept_in, sent_in, same, edge, kept_ref, sent_ref = rest
     channels = z1.shape[1]
     step, wide_step = channels // LANES, back_e.shape[1] // LANES
     count = total_1[4 * step : 4 * step + 1, 0:1]
-    mask = mask8[...]
     mean, scale = moments(total_1[...], 2 * step, step, channels, count)
     total = total_4[...]
     low = back_of(
         up1[...], z1[...], mean, scale, first_n[0:1], row_of(total, 2 * wide_step, channels),
-        row_of(total, 2 * wide_step + step, channels), count, mask,
+        row_of(total, 2 * wide_step + step, channels), count, mask8[...],
     )
     spread(low.astype(BF16).astype(F32), *place, same, edge)
-    out = conv_back_of(same, edge, first_w) + up2[...]
-    out = rows_of(eights(out) + eights(rows_of(gm[...]).astype(F32)) * (1.0 - mask))
-    motion_back[...] = out.astype(BF16).reshape(motion_back.shape)
     core = core_here()
     half = channels // 2
-    conv_grad_to(core, mm[...], same_2, edge_2, kept_ref, sent_ref, 0)
     conv_grad_to(core, rows_of(m[...]), same, edge, kept_ref, sent_ref, 9 * half)
     for k in range(back_e.shape[1] // 256):
         product = across(sa[...], back_e[:, k * 256 : (k + 1) * 256])
         split_store(core, kept_ref, sent_ref, (18 + k) * half, product)
 
 
-def kernel_last(ra, same, edge, x, back_r, sums_r, sums_s, sums_1, sums_2, kept_ref, sent_ref):
+def kernel_motion(mask8, same, edge, first_w, gm, up2, motion_back):
+    out = conv_back_of(same, edge, first_w) + up2[...]
+    out = rows_of(eights(out) + eights(rows_of(gm[...]).astype(F32)) * (1.0 - mask8[...]))
+    motion_back[...] = out.astype(BF16).reshape(motion_back.shape)
+
+
+def kernel_spatial(ra, same, edge, kept_ref, sent_ref):
+    conv_grad_to(core_here(), ra[...], same, edge, kept_ref, sent_ref, 0)
+
+
+def kernel_7(parts, mask8, total_1, upr, zr, reduce_n, x, sums_r, sums_s, sums_1, sums_2, *rest):
+    kept_in, sent_in, back_r, kept_ref, sent_ref = rest
+    channels, wide = zr.shape[1], x.shape[2]
+    step = channels // LANES
+    total = total_of(parts)
+    count = total_1[4 * step : 4 * step + 1, 0:1]
+    mean, scale = moments(total_1[...], 0, step, channels, count)
+    low = back_of(
+        upr[...], zr[...], mean, scale, reduce_n[0:1], row_of(total, 0, channels),
+        row_of(total, step, channels), count, mask8[...],
+    )
+    back_r[...] = low.astype(BF16)
     core = core_here()
-    channels, wide = ra.shape[1], x.shape[2]
-    conv_grad_to(core, ra[...], same, edge, kept_ref, sent_ref, 0)
-    product = across(rows_of(x[...]), back_r[...])
     at = 9 * (channels // 2)
-    split_store(core, kept_ref, sent_ref, at, product)
+    split_store(core, kept_ref, sent_ref, at, across(rows_of(x[...]), back_r[...]))
     at = at + wide // 2
     rows = norm_rows(sums_r, 0, channels) + norm_rows(sums_s, 0, channels)
     rows += norm_rows(sums_1, 0, wide) + norm_rows(sums_1, 2 * wide // LANES, channels)
@@ -421,6 +419,36 @@
     half = kept_ref.shape[0] - at
     rows.append(jnp.zeros((2 * half - len(rows), 256), F32))
     split_store(core, kept_ref, sent_ref, at, jnp.concatenate(rows, axis=0))
+
+
+def kernel_out(place, mask8, total_1, total_2, total_3, ze, x, z2, m, expand_n, second_n, iframe_out, motion_out):
+    channels, wide = z2.shape[1], ze.shape[1]
+    step, wide_step = channels // LANES, wide // LANES
+    count = total_1[4 * step : 4 * step + 1, 0:1]
+    mask = mask8[...]
+
+    def joined(z, here, mean, scale, norm):
+        u = eights(z) * (norm[0:1] * scale) + (norm[1:2] - mean * (norm[0:1] * scale)) + here
+        return rows_of(mask * (u * sigmoid(u)) + (1.0 - mask) * here).astype(BF16)
+
+    mean, scale = moments(total_2[...], 2 * step, step, channels, count)
+    motion = eights(rows_of(m[...]).astype(F32))
+    motion_out[...] = joined(z2[...], motion, mean, scale, second_n[...]).reshape(motion_out.shape)
+    part, rows, frames = channels, 16, place[1]
+    for at in range(0, wide, part):
+        lanes = slice(at, at + part)
+        mean, scale = moments(total_3[...], at // LANES, wide_step, part, count)
+        norm = expand_n[:, lanes]
+
+        def step_of(i, carry):
+            here = pl.ds(pl.multiple_of(i * rows, rows), rows)
+            pixels = pl.ds(i * (rows // frames), rows // frames)
+            frame = eights(rows_of(x[pixels, :, lanes]).astype(F32))
+            out = joined(ze[here, lanes], frame, mean, scale, norm)
+            iframe_out[pixels, :, lanes] = out.reshape(-1, frames, part)
+            return carry
+
+        lax.fori_loop(0, ze.shape[0] // rows, step_of, 0, unroll=7)
 
 
 def norm_rows(sums, row, channels):
@@ -445,12 +473,8 @@
     return lax.rem(lax.axis_index("clip"), 2)
 
 
-def place_on(axis, stride, radix):
-    return lax.rem(lax.axis_index(axis) // stride, radix)
-
-
-def kernel_scatter(axis, stride, radix, *refs):
-    here = place_on(axis, stride, radix)
+def kernel_scatter(phase, *refs):
+    here, radix = phase.digit(), phase.radix
     ins, outs = refs[:-radix], refs[-radix:]
     for k in range(radix):
         at = jnp.bitwise_xor(here, k)
@@ -467,9 +491,9 @@
     refs[-1][...] = total.astype(BF16)
 
 
-def kernel_gather(axis, stride, radix, *refs):
-    here = place_on(axis, stride, radix)
-    for k in range(radix):
+def kernel_gather(phase, *refs):
+    here = phase.digit()
+    for k in range(phase.radix):
         refs[-1][jnp.bitwise_xor(here, k)] = refs[k][...]
 
 
@@ -505,54 +529,162 @@
                     out[k : k + 1, j * 256 : (j + 1) * 256] = rows[row : row + 1]
 
 
-def call(kernel, outs, *args, scratch=(), flops=1 << 20, lists=None, space=pltpu.VMEM):
+def call(kernel, outs, *args, scratch=(), lists=None, space=pltpu.VMEM, after=(), alias=(), token=False):
+    used = len(args)
+    if token:
+        outs = list(outs) + [like((8, LANES), F32)]
+
     def body(*refs):
+        refs = refs[:used] + refs[used + len(after) :]
+        if token:
+            at = used + len(outs) - 1
+            refs[at][...] = jnp.zeros((8, LANES), F32)
+            refs = refs[:at] + refs[at + 1 :]
         if lists:
             return kernel(refs[:lists], *refs[lists:])
         return kernel(*refs)
 
-    moved = sum(arg.size * arg.dtype.itemsize for arg in args)
-    moved += sum(out.size * out.dtype.itemsize for out in outs)
     return pl.pallas_call(
         body,
         out_shape=outs,
-        in_specs=[pl.BlockSpec(memory_space=space) for _ in args],
+        in_specs=[pl.BlockSpec(memory_space=space) for _ in args]
+        + [pl.BlockSpec(memory_space=pl.ANY) for _ in after],
         out_specs=[pl.BlockSpec(memory_space=pltpu.VMEM) for _ in outs],
         scratch_shapes=list(scratch),
+        input_output_aliases=dict(alias),
         compiler_params=pltpu.CompilerParams(vmem_limit_bytes=20 << 20),
-        cost_estimate=pl.CostEstimate(flops=flops, bytes_accessed=moved, transcendentals=0),
-    )(*args)
+        cost_estimate=pl.CostEstimate(flops=COST, bytes_accessed=COST, transcendentals=0),
+    )(*args, *after)
 
 
 def like(shape, dtype):
     return jax.ShapeDtypeStruct(shape, dtype)
 
 
-def grad_sum(kept, sent, kinds, outs):
-    clip_steps, clip_rest = factors(lax.axis_size("clip"))
-    section = lax.axis_size("section")
-    got = swap(sent, "clip", 1)
-    rows, width = kept.shape
-    order = [("section", 1, section)] + [("clip",) + step for step in clip_steps[1:]]
-    ins = [kept, got]
-    for axis, stride, radix in order:
-        rows = rows // radix
+class Phase:
+    def __init__(self, radix, digit, partner):
+        self.radix, self.digit, self.partner = radix, digit, partner
+
+    def send(self, value, k):
+        sections, clips = lax.axis_size("section"), lax.axis_size("clip")
+        route = []
+        for s in range(sections):
+            for c in range(clips):
+                to, where = self.partner(s, c, k)
+                route.append((s * clips + c, to * clips + where))
+        return lax.ppermute(value, ("section", "clip"), route)
+
+
+def over_section():
+    size = lax.axis_size("section")
+    return [Phase(size, lambda: lax.axis_index("section"), lambda s, c, k: (s ^ k, c))]
+
+
+def over_section_halves():
+    if lax.axis_size("section") != 4:
+        return over_section()
+
+    def digit(swapped):
+        section = lax.axis_index("section")
+        first = jnp.bitwise_xor(core_here(), swapped) == 0
+        return jnp.where(first, lax.rem(section, 2), section // 2)
+
+    def partner(swapped, s, c, k):
+        return s ^ (k if (c % 2) ^ swapped == 0 else 2 * k), c
+
+    return [
+        Phase(2, functools.partial(digit, swapped), functools.partial(partner, swapped))
+        for swapped in (0, 1)
+    ]
+
+
+def over_clip():
+    def phase(stride, radix):
+        return Phase(
+            radix,
+            lambda: lax.rem(lax.axis_index("clip") // stride, radix),
+            lambda s, c, k: (s, c ^ (stride * k)),
+        )
+
+    return [phase(stride, radix) for stride, radix in factors(lax.axis_size("clip"))[0][1:]]
+
+
+def over_clip_halves():
+    def digit(stride, swapped):
+        first = jnp.bitwise_xor(core_here(), swapped) == 0
+        place = lax.axis_index("clip") // stride
+        return jnp.where(first, lax.rem(place, 2), lax.rem(place // 2, 2))
+
+    def partner(stride, swapped, s, c, k):
+        return s, c ^ (stride * (k if (c % 2) ^ swapped == 0 else 2 * k))
+
+    phases = []
+    for step, (stride, radix) in zip(over_clip(), factors(lax.axis_size("clip"))[0][1:]):
+        if radix != 4:
+            phases.append(step)
+            continue
+        for swapped in (0, 1):
+            phases.append(
+                Phase(
+                    2,
+                    functools.partial(digit, stride, swapped),
+                    functools.partial(partner, stride, swapped),
+                )
+            )
+    return phases
+
+
+class GradSum:
+    def __init__(self, kept, sent, phases):
+        self.phases = phases
+        self.rows, self.width = kept.shape
+        self.parts = [kept, swap(sent, "clip", 1)]
+
+    def scatter(self, k, after=()):
+        phase = self.phases[k]
+        radix = phase.radix
+        self.rows = self.rows // radix
         chunks = call(
-            functools.partial(kernel_scatter, axis, stride, radix),
-            [like((rows, width), BF16)] * radix,
-            *[part.reshape(radix, rows, width) for part in ins],
+            functools.partial(kernel_scatter, phase),
+            [like((self.rows, self.width), BF16)] * radix,
+            *[part.reshape(radix, self.rows, self.width) for part in self.parts],
+            after=after,
         )
-        ins = [chunks[0]] + [swap(chunks[k], axis, stride * k) for k in range(1, radix)]
-    (value,) = call(kernel_sum, [like((rows, width), BF16)], *ins)
-    for axis, stride, radix in reversed(order):
-        parts = [value] + [swap(value, axis, stride * k) for k in range(1, radix)]
+        self.parts = [chunks[0]] + [phase.send(chunks[j], j) for j in range(1, radix)]
+        return chunks[0]
+
+    def spread_from(self, value, k):
+        phase = self.phases[k]
+        self.parts = [value] + [phase.send(value, j) for j in range(1, phase.radix)]
+        return value
+
+    def total(self, after=()):
+        (value,) = call(kernel_sum, [like((self.rows, self.width), BF16)], *self.parts, after=after)
+        return self.spread_from(value, len(self.phases) - 1)
+
+    def gather(self, k, after=()):
+        radix = self.phases[k].radix
         (value,) = call(
-            functools.partial(kernel_gather, axis, stride, radix),
-            [like((radix,) + value.shape, BF16)],
-            *parts,
+            functools.partial(kernel_gather, self.phases[k]),
+            [like((radix, self.rows, self.width), BF16)],
+            *self.parts,
+            after=after,
         )
-        value = value.reshape(-1, width)
-    return call(functools.partial(kernel_finish, kinds), outs, value, swap(value, "clip", 1))
+        self.rows = radix * self.rows
+        value = value.reshape(self.rows, self.width)
+        if k:
+            return self.spread_from(value, k - 1)
+        self.parts = [value, swap(value, "clip", 1)]
+        return value
+
+    def finish(self, kinds, outs, token=False):
+        return call(functools.partial(kernel_finish, kinds), outs, *self.parts, token=token)
+
+
+FIRST_PHASES = (over_section_halves, over_clip)
+SECOND_PHASES = (over_section, over_clip)
+EARLY = 1
+ORDER = ("Ts0", "I", "M", "Fs2", "O", "Ts1", "Ft", "Fg2", "Tt", "Fg1", "Tg1", "Fg0", "X", "Tg0")
 
 
 def per_device(
@@ -598,8 +730,6 @@
     def far(value):
         return pltpu.with_memory_space_constraint(value, pltpu.HBM)
 
-    point = 2 * area * narrow * wide
-    conv = 18 * area * narrow * narrow
     same = (area, 3 * narrow)
     edge = (area + 2 * width * frames, 3 * narrow)
     spread_scratch = [pltpu.VMEM(same, BF16), pltpu.VMEM(edge, BF16)]
@@ -614,7 +744,6 @@
         + [pltpu.SMEM(segment_valid.shape, jnp.int32)]
         + [pltpu.VMEM(v.shape, BF16) for v in (x, m, reduce_weight, motion_first)]
         + [pltpu.SemaphoreType.DMA((5,))],
-        flops=point + conv,
         space=pltpu.HBM,
     )
     parts = clip_parts(sums)
@@ -623,86 +752,142 @@
         [first_size, plane(narrow, BF16), plane(narrow, BF16), plane(narrow), plane(narrow), second_size],
         *parts, mask8, zr, z1, reduce_norm, first_norm, spatial_weight, motion_second,
         scratch=spread_scratch,
-        flops=2 * conv,
         lists=len(parts),
     )
     parts = clip_parts(sums)
-    total_2, sa, ze, motion_out, up2, sums = call(
+    total_2, sa, ze, up2, sums = call(
         kernel_3,
-        [second_size, plane(narrow, BF16), plane(wide), like(gm.shape, BF16), plane(narrow), both],
+        [second_size, plane(narrow, BF16), plane(wide), plane(narrow), both],
         *parts, mask8, total_1, zs, z2, m, gm, spatial_norm, second_norm, expand_weight,
-        flops=point,
         lists=len(parts),
     )
     parts = clip_parts(sums)
     up2_sums = sums
-    total_3, iframe_out, upe, up1, same_2, edge_2, sums = call(
+    total_3, upe, up1, same_2, edge_2, sums = call(
         bound(kernel_4),
-        [both, like(gx.shape, BF16), plane(wide), plane(narrow), like(same, BF16), like(edge, BF16), both],
+        [both, plane(wide), plane(narrow), like(same, BF16), like(edge, BF16), both],
         *parts, mask8, total_1, total_2, z1, z2, up2, ze, x, gx,
         expand_norm, second_norm, first_norm, motion_second,
-        flops=conv,
         lists=len(parts),
     )
     parts = clip_parts(sums)
     up1_sums = sums
+    half = narrow // 2
+    set_rows = (18 + wide // 256) * half
+    kept, sent = call(
+        kernel_second,
+        [like((set_rows, 256), BF16)] * 2,
+        mm, same_2, edge_2,
+        after=parts[:1],
+    )
     total_4, back_e, ups, sums = call(
         kernel_5,
         [both, plane(wide, BF16), plane(narrow), small(2 * step)],
         *parts, mask8, total_1, total_2, total_3, ze, upe, zs, expand_norm, spatial_norm, expand_weight,
-        flops=point,
         lists=len(parts),
+        after=[kept],
     )
     parts = clip_parts(sums)
     ups_sums = sums
-    half = narrow // 2
-    set_rows = (18 + wide // 256) * half
-    motion_back, kept, sent = call(
-        bound(kernel_motion),
-        [like(m.shape, BF16)] + [like((set_rows, 256), BF16)] * 2,
-        mask8, total_1, total_4, up1, z1, first_norm, motion_first, m, gm, up2,
-        same_2, edge_2, mm, sa, back_e,
-        scratch=spread_scratch,
-        flops=3 * conv + point,
-    )
-    taps = like((9, narrow, narrow), F32)
-    grad_second, grad_first, grad_expand = grad_sum(
-        kept, sent, ("taps", "taps", "wide"), [taps, taps, like(expand_weight.shape, F32)]
-    )
+    same_1, edge_1, kept, sent = call(
+        bound(kernel_first),
+        [like(same, BF16), like(edge, BF16)] + [like((set_rows, 256), BF16)] * 2,
+        mask8, total_1, total_4, up1, z1, first_norm, m, sa, back_e, kept, sent,
+        after=parts[:1],
+        alias=[(9, 2), (10, 3)],
+    )
+    first_set = GradSum(kept, sent, FIRST_PHASES[0]() + FIRST_PHASES[1]())
+    first_scattered = first_set.scatter(0, after=parts[1:])
     total_5, upr, same_s, edge_s, sums = call(
         bound(kernel_6),
         [small(2 * step), plane(narrow), like(same, BF16), like(edge, BF16), small(2 * step)],
         *parts, mask8, total_1, total_2, ups, zs, zr, spatial_norm, reduce_norm, spatial_weight,
-        flops=conv,
         lists=len(parts),
+        after=[first_scattered],
     )
     parts = clip_parts(sums)
     upr_sums = sums
-    (back_r,) = call(
-        kernel_7,
-        [plane(narrow, BF16)],
-        *parts, mask8, total_1, upr, zr, reduce_norm,
-        lists=len(parts),
-    )
-
     spare = 128
     set_rows = 9 * half + wide // 2 + spare
     kept, sent = call(
-        kernel_last,
+        kernel_spatial,
         [like((set_rows, 256), BF16)] * 2,
-        ra, same_s, edge_s, x, back_r, upr_sums, ups_sums, up1_sums, up2_sums,
-        flops=conv + point,
-    )
-    (iframe_back,) = call(
-        kernel_iframe, [like(gx.shape, BF16)], mask8, gx, upe, back_r, reduce_weight,
-        flops=point,
-    )
+        ra, same_s, edge_s,
+        after=parts[:1],
+    )
+    last = kept
+    for k in range(1, EARLY + 1):
+        last = first_set.scatter(k, after=[last])
+    back_r, kept, sent = call(
+        kernel_7,
+        [plane(narrow, BF16)] + [like((set_rows, 256), BF16)] * 2,
+        *parts, mask8, total_1, upr, zr, reduce_norm, x, upr_sums, ups_sums, up1_sums, up2_sums, kept, sent,
+        lists=len(parts),
+        after=[last],
+        alias=[(len(parts) + 10, 1), (len(parts) + 11, 2)],
+    )
+    second_set = GradSum(kept, sent, SECOND_PHASES[0]() + SECOND_PHASES[1]())
+
+    taps = like((9, narrow, narrow), F32)
+    made = {}
+
+    def iframe(after):
+        made["iframe"], token = call(
+            kernel_iframe, [like(gx.shape, BF16)], mask8, gx, upe, back_r, reduce_weight,
+            after=after, token=True,
+        )
+        return token
+
+    def motion(after):
+        made["motion"], token = call(
+            kernel_motion, [like(gm.shape, BF16)], mask8, same_1, edge_1, motion_first, gm, up2,
+            after=after, token=True,
+        )
+        return token
+
+    def outputs(after):
+        *made["outputs"], token = call(
+            bound(kernel_out),
+            [like(gx.shape, BF16), like(gm.shape, BF16)],
+            mask8, total_1, total_2, total_3, ze, x, z2, m, expand_norm, second_norm,
+            after=after, token=True,
+        )
+        return token
+
+    def finish(after):
+        *made["first"], token = first_set.finish(
+            ("taps", "taps", "wide"), [taps, taps, like(expand_weight.shape, F32)], token=True
+        )
+        return token
+
+    last = kept
+    for step in ORDER:
+        if step == "I":
+            last = iframe([last])
+        elif step == "M":
+            last = motion([last])
+        elif step == "O":
+            last = outputs([last])
+        elif step == "X":
+            last = finish([last])
+        else:
+            own = first_set if step[0] == "F" else second_set
+            after = [last] if len(step) < 4 else []
+            if step[1] == "t":
+                last = own.total(after)
+            elif step[1] == "s":
+                last = own.scatter(int(step[2]), after)
+            else:
+                last = own.gather(int(step[2]), after)
+    iframe_back, motion_back = made["iframe"], made["motion"]
+    iframe_out, motion_out = made["outputs"]
+    grad_second, grad_first, grad_expand = made["first"]
     norms = (reduce_norm, spatial_norm, expand_norm, first_norm, second_norm)
     starts = [0]
     for norm in norms:
         starts.append(starts[-1] + norm.size // 256)
-    grad_spatial, grad_reduce, *norm_grads = grad_sum(
-        kept, sent, ["taps", "taps"] + starts[:-1],
+    grad_spatial, grad_reduce, *norm_grads = second_set.finish(
+        ["taps", "taps"] + starts[:-1],
         [taps, like((1, wide, narrow), F32)] + [like(norm.shape, F32) for norm in norms],
     )
     features = tuple(frames_first(v) for v in (iframe_out, motion_out, iframe_back, motion_back))

time: 180 us -> 145 us (0.81)
  waiting for transfers between devices: 82.5 us -> 46.7 us
  Pallas kernels: 32.5 us -> 36.6 us
  starting transfers between devices: 64 us -> 59.9 us
    ppermute x52 -> x28, waiting for transfers between devices: 82.5 us -> 21.4 us  [swap(): return lax.ppermute(value, axis, [(i, i ^ mask) for i in range(size)])]
    ppermute x52 -> x28, starting transfers between devices: 64 us -> 28.8 us  [swap(): return lax.ppermute(value, axis, [(i, i ^ mask) for i in range(size)])]
    ppermute x0 -> x22, starting transfers between devices: none -> 31.1 us  [send(): return lax.ppermute(value, ('section', 'clip'), route)]
    ppermute x0 -> x22, waiting for transfers between devices: none -> 25.4 us  [send(): return lax.ppermute(value, ('section', 'clip'), route)]
    pallas_call x22 -> x27, Pallas kernels: 32.5 us -> 36.6 us  [call(): pl.pallas_call(body, out_shape=outs, in_specs=[pl.BlockSpec(memory_space=...]
  transfers between devices with their start and end apart: 52 -> 50, of which waited for: 41 -> 31; matrix products, arithmetic and copies ran while one was open for 0% -> 0% of each run, Pallas kernels for 5% -> 11%
where the time goes in v1:
time: 145 us; the launch traced here: 144 us
  starting transfers between devices  59.9 us (41%)
  waiting for transfers between devices  46.7 us (32%)
  Pallas kernels  36.6 us (25%)
    pallas_call x27, Pallas kernels, call(): pl.pallas_call(body, out_shape=outs, in_specs=[pl.BlockSpec(memory_space=...  36.6 us
    ppermute x22, starting transfers between devices, send(): return lax.ppermute(value, ('section', 'clip'), route)  31.1 us
    ppermute x28, starting transfers between devices, swap(): return lax.ppermute(value, axis, [(i, i ^ mask) for i in range(size)])  28.8 us
    ppermute x22, waiting for transfers between devices, send(): return lax.ppermute(value, ('section', 'clip'), route)  25.4 us
    ppermute x28, waiting for transfers between devices, swap(): return lax.ppermute(value, axis, [(i, i ^ mask) for i in range(size)])  21.4 us
  transfers between devices with their start and end apart: 50, of which 31 were waited for; matrix products, arithmetic and copies ran while one was open for 0% of the time, Pallas kernels for 11%

profile of v1, /device:TPU:0, one launch (start us, length us, event | category | flops | bytes accessed | tf_op | source)
XLA Modules:
  0.0 144.4 jit_solution(16155697953722334844)
XLA Ops:
  0.7 4.2 %shard_map.254 = (f32[8,256]{1,0:T(8,128)S(1)}, f32[784,256]{1,0:T(8,128)S(1)}, f32[784,256]{1,0:T(8,128)S(1)}, f32[16,128]{1,0:T(8,128)S(1)}) custom-call(s32[4,4]{1,0:T(4,128)} %refs_0_.1, bf16[196,4,1024]{2,1,0:T(4,128)(2,1)} %bitcast.61, bf16[196,4,256]{2,1,0:T(4,128)(2,1)} %bitcast.72, bf16[1024,256]{1,0:T(8,128)(2,1)} %refs_4_.3, ...), custom_call_target="tpu_custom_call" | custom-call | flops 1024 | bytes 1024 | tf_op jit(solution)/shard_map/pallas_call | solution.py:547
  6.2 4.9 %collective-permute-start.3 = (f32[16,128]{1,0:T(8,128)S(1)}, f32[16,128]{1,0:T(8,128)S(1)}, u32[]{:S(2)}, u32[]{:S(2)}) collective-permute-start(f32[16,128]{1,0:T(8,128)S(1)} %add.18.refs_0_), channel_id=1, source_target_pairs={{0,6},{1,7},{2,4},{3,5},{4,2},{5,3},{6,0},{7,1},{8,14},{9,15},{10,... | collective-permute-start | bytes 24584 | tf_op jit(solution)/shard_map/ppermute | solution.py:34
  11.8 1.1 collective-permute-done.3.refs_3_
  12.8 2.9 %collective-permute-done.2.refs_2_ = f32[16,128]{1,0:T(8,128)S(1)} collective-permute-done((f32[16,128]{1,0:T(8,128)S(1)}, f32[16,128]{1,0:T(8,128)S(1)}, u32[]{:S(2)}, u32[]{:S(2)}) %collective-permute-start.2) | collective-permute-done | bytes 8224 | tf_op jit(solution)/shard_map/ppermute | solution.py:34
  15.8 2.5 %shard_map.255 = (f32[16,128]{1,0:T(8,128)S(1)}, bf16[784,256]{1,0:T(8,128)(2,1)S(1)}, bf16[784,256]{1,0:T(8,128)(2,1)S(1)}, f32[784,256]{1,0:T(8,128)S(1)}, f32...) custom-call(f32[16,128]{1,0:T(8,128)S(1)} %add.18.refs_0_, f32[16,128]{1,0:T(8,128)S(1)} %collective-permute-done.1.refs_1_, ...), custom_call_target="tpu_custom_call" | custom-call | flops 1024 | bytes 1024 | tf_op jit(solution)/shard_map/pallas_call | solution.py:547
  18.4 1.2 collective-permute-done.4
  19.6 1.5 %collective-permute-start.7 = (f32[8,128]{1,0:T(8,128)S(1)}, f32[8,128]{1,0:T(8,128)S(1)}, u32[]{:S(2)}, u32[]{:S(2)}) collective-permute-start(f32[8,128]{1,0:T(8,128)S(1)} %add.19.refs_0_), channel_id=1, source_target_pairs={{0,6},{1,7},{2,4},{3,5},{4,2},{5,3},{6,0},{7,1},{8,14},{9,15},{10,... | collective-permute-start | bytes 12296 | tf_op jit(solution)/shard_map/ppermute | solution.py:34
  21.6 2.4 %collective-permute-start.5 = (f32[8,128]{1,0:T(8,128)S(1)}, f32[8,128]{1,0:T(8,128)S(1)}, u32[]{:S(2)}, u32[]{:S(2)}) collective-permute-start(f32[8,128]{1,0:T(8,128)S(1)} %add.19.refs_0_), channel_id=1, source_target_pairs={{0,2},{1,3},{2,0},{3,1},{4,6},{5,7},{6,4},{7,5},{8,10},{9,11},{10,... | collective-permute-start | bytes 12296 | tf_op jit(solution)/shard_map/ppermute | solution.py:34
  24.0 1.0 collective-permute-done.7.refs_3_
  25.6 2.1 %shard_map.256 = (f32[8,128]{1,0:T(8,128)S(1)}, bf16[784,256]{1,0:T(8,128)(2,1)S(1)}, f32[784,1024]{1,0:T(8,128)S(1)}, f32[784,256]{1,0:T(8,128)S(1)}, f32[24,128]{1,0:T(8,128)S(1)}) custom-call(f32[8,128]{1,0:T(8,128)S(1)} %add.19.refs_0_, f32[8,128]{1,0:T(8,128)S(1)} %collective-permute-done.5.refs_1_, f32[8,128]{1,0:T(8,128)S(1)} %collective-permute-done.6.refs_2_, ...), custom_call_target="tpu_custom_call" | custom-call | flops 1024 | bytes 1024 | tf_op jit(solution)/shard_map/pallas_call | solution.py:547
  27.8 1.2 collective-permute-done.8
  29.0 2.5 %collective-permute-start.11 = (f32[24,128]{1,0:T(8,128)S(1)}, f32[24,128]{1,0:T(8,128)S(1)}, u32[]{:S(2)}, u32[]{:S(2)}) collective-permute-start(f32[24,128]{1,0:T(8,128)S(1)} %add.20.refs_0_), channel_id=1, source_target_pairs={{0,6},{1,7},{2,4},{3,5},{4,2},{5,3},{6,0},{7,1},{8,14},{9,15},{10,... | collective-permute-start | bytes 36872 | tf_op jit(solution)/shard_map/ppermute | solution.py:34
  33.4 1.2 collective-permute-done.11.refs_3_
  34.6 1.5 %collective-permute-done.10.refs_2_ = f32[24,128]{1,0:T(8,128)S(1)} collective-permute-done((f32[24,128]{1,0:T(8,128)S(1)}, f32[24,128]{1,0:T(8,128)S(1)}, u32[]{:S(2)}, u32[]{:S(2)}) %collective-permute-start.10) | collective-permute-done | bytes 12320 | tf_op jit(solution)/shard_map/ppermute | solution.py:34
  36.3 4.5 %shard_map.257 = (f32[24,128]{1,0:T(8,128)S(1)}, f32[784,1024]{1,0:T(8,128)S(1)}, f32[784,256]{1,0:T(8,128)S(1)}, bf16[784,768]{1,0:T(8,128)(2,1)S(1)}, bf16[896...) custom-call(f32[24,128]{1,0:T(8,128)S(1)} %add.20.refs_0_, f32[24,128]{1,0:T(8,128)S(1)} %collective-permute-done.9.refs_1_, ...), custom_call_target="tpu_custom_call" | custom-call | flops 1024 | bytes 1024 | tf_op jit(solution)/shard_map/pallas_call | solution.py:547
  40.9 1.2 collective-permute-done.12
  42.1 1.3 collective-permute-start.15
  44.3 2.1 %collective-permute-start.13 = (f32[24,128]{1,0:T(8,128)S(1)}, f32[24,128]{1,0:T(8,128)S(1)}, u32[]{:S(2)}, u32[]{:S(2)}) collective-permute-start(f32[24,128]{1,0:T(8,128)S(1)} %add.21.refs_3_.refs_0_), channel_id=1, source_target_pairs={{0,2},{1,3},{2,0},{3,1},{4,6},{5,7},{6,4},{7,5},{8,10},{9,11},{10,... | collective-permute-start | bytes 36872 | tf_op jit(solution)/shard_map/ppermute | solution.py:34
  46.5 1.4 shard_map.258
  48.1 1.3 shard_map.259
  49.5 1.2 collective-permute-done.16
  50.7 2.3 %shard_map.260 = (bf16[784,768]{1,0:T(8,128)(2,1)S(1)}, bf16[896,768]{1,0:T(8,128)(2,1)S(1)}, bf16[2816,256]{1,0:T(8,128)(2,1)S(1)}, bf16[2816,256]{1,0:T(8,128)(2,1)S(1)}) custom-call(f32[8,256]{1,0:T(8,128)S(1)} %get-tuple-element.88.refs_4_.refs_0_, ...), custom_call_target="tpu_custom_call", output_to_operand_aliasing={{2}: (9, {}), {3}: (10, {})} | custom-call | flops 1024 | bytes 1024 | tf_op jit(solution)/shard_map/pallas_call | solution.py:547
  53.2 2.5 %collective-permute-start.20 = (f32[8,128]{1,0:T(8,128)S(1)}, f32[8,128]{1,0:T(8,128)S(1)}, u32[]{:S(2)}, u32[]{:S(2)}) collective-permute-start(f32[8,128]{1,0:T(8,128)S(1)} %add.22.refs_11_.refs_0_), channel_id=1, source_target_pairs={{0,6},{1,7},{2,4},{3,5},{4,2},{5,3},{6,0},{7,1},{8,14},{9,15},{10,... | collective-permute-start | bytes 12296 | tf_op jit(solution)/shard_map/ppermute | solution.py:34
  55.7 1.0 collective-permute-start.19
  57.6 1.0 collective-permute-done.20.refs_4_.refs_3_
  58.6 1.6 %collective-permute-done.19.refs_3_.refs_2_ = f32[8,128]{1,0:T(8,128)S(1)} collective-permute-done((f32[8,128]{1,0:T(8,128)S(1)}, f32[8,128]{1,0:T(8,128)S(1)}, u32[]{:S(2)}, u32[]{:S(2)}) %collective-permute-start.19) | collective-permute-done | bytes 4128 | tf_op jit(solution)/shard_map/ppermute | solution.py:34
  60.7 1.5 %collective-permute-start.21 = (bf16[1408,256]{1,0:T(8,128)(2,1)S(1)}, bf16[1408,256]{1,0:T(8,128)(2,1)S(1)}, u32[]{:S(2)}, u32[]{:S(2)}) collective-permute-start(bf16[1408,256]{1,0:T(8,128)(2,1)S(1)} %get-tuple-element.116), channel_id=1, source_target_pairs={{0,8},{1,17},{2,10},{3,19},{4,12},{5,21},{6,14},{7,23},{8,0},{9,25... | collective-permute-start | bytes 2162696 | tf_op jit(solution)/shard_map/ppermute | solution.py:575
  62.2 1.3 shard_map.262
  63.6 1.2 collective-permute-done.22
  64.8 1.4 collective-permute-start.26
  66.1 1.0 collective-permute-start.25
  67.2 2.0 %collective-permute-start.24 = (f32[8,128]{1,0:T(8,128)S(1)}, f32[8,128]{1,0:T(8,128)S(1)}, u32[]{:S(2)}, u32[]{:S(2)}) collective-permute-start(f32[8,128]{1,0:T(8,128)S(1)} %add.23.refs_3_.refs_0_), channel_id=1, source_target_pairs={{0,2},{1,3},{2,0},{3,1},{4,6},{5,7},{6,4},{7,5},{8,10},{9,11},{10,... | collective-permute-start | bytes 12296 | tf_op jit(solution)/shard_map/ppermute | solution.py:34
  69.2 1.4 shard_map.263
  70.6 1.4 collective-permute-done.21
  73.3 1.6 %collective-permute-start.23 = (bf16[704,256]{1,0:T(8,128)(2,1)S(1)}, bf16[704,256]{1,0:T(8,128)(2,1)S(1)}, u32[]{:S(2)}, u32[]{:S(2)}) collective-permute-start(bf16[704,256]{1,0:T(8,128)(2,1)S(1)} %get-tuple-element.124), channel_id=1, source_target_pairs={{0,16},{1,9},{2,18},{3,11},{4,20},{5,13},{6,22},{7,15},{8,24},{9,1... | collective-permute-start | bytes 1081352 | tf_op jit(solution)/shard_map/ppermute | solution.py:575
  76.0 1.5 %collective-permute-start.28 = (bf16[448,256]{1,0:T(8,128)(2,1)S(1)}, bf16[448,256]{1,0:T(8,128)(2,1)S(1)}, u32[]{:S(2)}, u32[]{:S(2)}) collective-permute-start(bf16[448,256]{1,0:T(8,128)(2,1)S(1)} %get-tuple-element.140), channel_id=1, source_target_pairs={{0,8},{1,9},{2,10},{3,11},{4,12},{5,13},{6,14},{7,15},{8,0},{9,1},... | collective-permute-start | bytes 688136 | tf_op jit(solution)/shard_map/ppermute | solution.py:575
  77.5 1.6 %collective-permute-start.29 = (bf16[448,256]{1,0:T(8,128)(2,1)S(1)}, bf16[448,256]{1,0:T(8,128)(2,1)S(1)}, u32[]{:S(2)}, u32[]{:S(2)}) collective-permute-start(bf16[448,256]{1,0:T(8,128)(2,1)S(1)} %get-tuple-element.141), channel_id=1, source_target_pairs={{0,16},{1,17},{2,18},{3,19},{4,20},{5,21},{6,22},{7,23},{8,24},{9,... | collective-permute-start | bytes 688136 | tf_op jit(solution)/shard_map/ppermute | solution.py:575
  79.6 2.1 %shard_map.267 = (bf16[196,4,1024]{2,1,0:T(4,128)(2,1)}, f32[8,128]{1,0:T(8,128)S(1)}) custom-call(f32[8,256]{1,0:T(8,128)S(1)} %get-tuple-element.88.refs_4_.refs_0_, bf16[196,4,1024]{2,1,0:T(4,128)(2,1)S(1)} %bitcast.71, f32[784,1024]{1,0:T(8,128)S(1)} %get-tuple-element.102.refs_9_.refs_2_, bf16[784,256]{1,0:T(8,128)(2,1)S(1)} %get-tuple-element.129.refs_3_, ...), custom_call_target="tpu_custom_call" | custom-call | flops 1024 | bytes 1024 | tf_op jit(solution)/shard_map/pallas_call | solution.py:547
  81.6 1.9 %shard_map.268 = (bf16[196,4,256]{2,1,0:T(4,128)(2,1)}, f32[8,128]{1,0:T(8,128)S(1)}) custom-call(f32[8,256]{1,0:T(8,128)S(1)} %get-tuple-element.88.refs_4_.refs_0_, bf16[784,768]{1,0:T(8,128)(2,1)S(1)} %get-tuple-element.125.refs_1_, bf16[896,768]{1,0:T(8,128)(2,1)S(1)} %get-tuple-element.126.refs_2_, bf16[3,3,256,256]{3,2,1,0:T(8,128)(2,1)S(1)} %copy-done.5, ...), custom_call_target="tpu_custom_call" | custom-call | flops 1024 | bytes 1024 | tf_op jit(solution)/shard_map/pallas_call | solution.py:547
  84.6 1.1 collective-permute-start.35
  85.7 2.4 %collective-permute-start.36 = (bf16[176,256]{1,0:T(8,128)(2,1)S(1)}, bf16[176,256]{1,0:T(8,128)(2,1)S(1)}, u32[]{:S(2)}, u32[]{:S(2)}) collective-permute-start(bf16[176,256]{1,0:T(8,128)(2,1)S(1)} %get-tuple-element.150), channel_id=1, source_target_pairs={{0,6},{1,7},{2,4},{3,5},{4,2},{5,3},{6,0},{7,1},{8,14},{9,15},{10,... | collective-permute-start | bytes 270344 | tf_op jit(solution)/shard_map/ppermute | solution.py:575
  88.1 4.3 %shard_map.270 = (bf16[196,4,1024]{2,1,0:T(4,128)(2,1)}, bf16[196,4,256]{2,1,0:T(4,128)(2,1)}, f32[8,128]{1,0:T(8,128)S(1)}) custom-call(f32[8,256]{1,0:T(8,128)S(1)} %get-tuple-element.88.refs_4_.refs_0_, f32[16,128]{1,0:T(8,128)S(1)} %get-tuple-element.92.refs_5_.refs_1_, f32[8,128]{1,0:T(8,128)S(1)} %get-tuple-element.96.refs_6_.refs_2_, ...), custom_call_target="tpu_custom_call" | custom-call | flops 1024 | bytes 1024 | tf_op jit(solution)/shard_map/pallas_call | solution.py:547
  92.5 1.3 collective-permute-done.35.refs_2_
  93.9 2.3 %collective-permute-start.39 = (bf16[176,256]{1,0:T(8,128)(2,1)S(1)}, bf16[176,256]{1,0:T(8,128)(2,1)S(1)}, u32[]{:S(2)}, u32[]{:S(2)}) collective-permute-start(bf16[176,256]{1,0:T(8,128)(2,1)S(1)} %shard_map.272.refs_0_.refs_4_), channel_id=1, source_target_pairs={{0,6},{1,7},{2,4},{3,5},{4,2},{5,3},{6,0},{7,1},{8,14},{9,15},{10,... | collective-permute-start | bytes 270344 | tf_op jit(solution)/shard_map/ppermute | solution.py:575
  97.0 1.4 collective-permute-start.37
  98.4 2.8 %collective-permute-done.39.refs_3_ = bf16[176,256]{1,0:T(8,128)(2,1)S(1)} collective-permute-done((bf16[176,256]{1,0:T(8,128)(2,1)S(1)}, bf16[176,256]{1,0:T(8,128)(2,1)S(1)}, u32[]{:S(2)}, u32[]{:S(2)}) %collective-permute-start.39) | collective-permute-done | bytes 90144 | tf_op jit(solution)/shard_map/ppermute | solution.py:575
  101.2 2.9 %collective-permute-done.38.refs_2_ = bf16[176,256]{1,0:T(8,128)(2,1)S(1)} collective-permute-done((bf16[176,256]{1,0:T(8,128)(2,1)S(1)}, bf16[176,256]{1,0:T(8,128)(2,1)S(1)}, u32[]{:S(2)}, u32[]{:S(2)}) %collective-permute-start.38) | collective-permute-done | bytes 90144 | tf_op jit(solution)/shard_map/ppermute | solution.py:575
  104.1 1.6 %collective-permute-start.43 = (bf16[704,256]{1,0:T(8,128)(2,1)S(1)}, bf16[704,256]{1,0:T(8,128)(2,1)S(1)}, u32[]{:S(2)}, u32[]{:S(2)}) collective-permute-start(bf16[704,256]{1,0:T(8,128)(2,1)S(1)} %bitcast.80), channel_id=1, source_target_pairs={{0,16},{1,9},{2,18},{3,11},{4,20},{5,13},{6,22},{7,15},{8,24},{9,1... | collective-permute-start | bytes 1081352 | tf_op jit(solution)/shard_map/ppermute | solution.py:575
  105.7 2.7 %collective-permute-start.32 = (bf16[112,256]{1,0:T(8,128)(2,1)S(1)}, bf16[112,256]{1,0:T(8,128)(2,1)S(1)}, u32[]{:S(2)}, u32[]{:S(2)}) collective-permute-start(bf16[112,256]{1,0:T(8,128)(2,1)S(1)} %get-tuple-element.146), channel_id=1, source_target_pairs={{0,4},{1,5},{2,6},{3,7},{4,0},{5,1},{6,2},{7,3},{8,12},{9,13},{10,... | collective-permute-start | bytes 172040 | tf_op jit(solution)/shard_map/ppermute | solution.py:575
  108.3 1.7 %collective-permute-start.33 = (bf16[112,256]{1,0:T(8,128)(2,1)S(1)}, bf16[112,256]{1,0:T(8,128)(2,1)S(1)}, u32[]{:S(2)}, u32[]{:S(2)}) collective-permute-start(bf16[112,256]{1,0:T(8,128)(2,1)S(1)} %get-tuple-element.147), channel_id=1, source_target_pairs={{0,6},{1,7},{2,4},{3,5},{4,2},{5,3},{6,0},{7,1},{8,14},{9,15},{10,... | collective-permute-start | bytes 172040 | tf_op jit(solution)/shard_map/ppermute | solution.py:575
  110.7 3.5 %collective-permute-done.33.refs_3_ = bf16[112,256]{1,0:T(8,128)(2,1)S(1)} collective-permute-done((bf16[112,256]{1,0:T(8,128)(2,1)S(1)}, bf16[112,256]{1,0:T(8,128)(2,1)S(1)}, u32[]{:S(2)}, u32[]{:S(2)}) %collective-permute-start.33) | collective-permute-done | bytes 57376 | tf_op jit(solution)/shard_map/ppermute | solution.py:575
  114.4 1.7 %collective-permute-start.47 = (bf16[1408,256]{1,0:T(8,128)(2,1)S(1)}, bf16[1408,256]{1,0:T(8,128)(2,1)S(1)}, u32[]{:S(2)}, u32[]{:S(2)}) collective-permute-start(bf16[1408,256]{1,0:T(8,128)(2,1)S(1)} %bitcast.67), channel_id=1, source_target_pairs={{0,8},{1,17},{2,10},{3,19},{4,12},{5,21},{6,14},{7,23},{8,0},{9,25... | collective-permute-start | bytes 2162696 | tf_op jit(solution)/shard_map/ppermute | solution.py:575
  116.1 1.7 %collective-permute-start.42 = (bf16[112,256]{1,0:T(8,128)(2,1)S(1)}, bf16[112,256]{1,0:T(8,128)(2,1)S(1)}, u32[]{:S(2)}, u32[]{:S(2)}) collective-permute-start(bf16[112,256]{1,0:T(8,128)(2,1)S(1)} %shard_map.274.refs_2_.refs_0_), channel_id=1, source_target_pairs={{0,6},{1,7},{2,4},{3,5},{4,2},{5,3},{6,0},{7,1},{8,14},{9,15},{10,... | collective-permute-start | bytes 172040 | tf_op jit(solution)/shard_map/ppermute | solution.py:575
  117.8 2.7 %collective-permute-start.40 = (bf16[112,256]{1,0:T(8,128)(2,1)S(1)}, bf16[112,256]{1,0:T(8,128)(2,1)S(1)}, u32[]{:S(2)}, u32[]{:S(2)}) collective-permute-start(bf16[112,256]{1,0:T(8,128)(2,1)S(1)} %shard_map.274.refs_2_.refs_0_), channel_id=1, source_target_pairs={{0,2},{1,3},{2,0},{3,1},{4,6},{5,7},{6,4},{7,5},{8,10},{9,11},{10,... | collective-permute-start | bytes 172040 | tf_op jit(solution)/shard_map/ppermute | solution.py:575
  120.5 1.6 %collective-permute-done.42.refs_3_ = bf16[112,256]{1,0:T(8,128)(2,1)S(1)} collective-permute-done((bf16[112,256]{1,0:T(8,128)(2,1)S(1)}, bf16[112,256]{1,0:T(8,128)(2,1)S(1)}, u32[]{:S(2)}, u32[]{:S(2)}) %collective-permute-start.42) | collective-permute-done | bytes 57376 | tf_op jit(solution)/shard_map/ppermute | solution.py:575
  122.1 1.2 collective-permute-done.41.refs_2_
  123.3 2.4 %collective-permute-done.47.refs_1_ = bf16[1408,256]{1,0:T(8,128)(2,1)S(1)} collective-permute-done((bf16[1408,256]{1,0:T(8,128)(2,1)S(1)}, bf16[1408,256]{1,0:T(8,128)(2,1)S(1)}, u32[]{:S(2)}, u32[]{:S(2)}) %collective-permute-start.47) | collective-permute-done | bytes 720928 | tf_op jit(solution)/shard_map/ppermute | solution.py:575
  126.0 1.6 %collective-permute-start.46 = (bf16[448,256]{1,0:T(8,128)(2,1)S(1)}, bf16[448,256]{1,0:T(8,128)(2,1)S(1)}, u32[]{:S(2)}, u32[]{:S(2)}) collective-permute-start(bf16[448,256]{1,0:T(8,128)(2,1)S(1)} %bitcast.85), channel_id=1, source_target_pairs={{0,24},{1,25},{2,26},{3,27},{4,28},{5,29},{6,30},{7,31},{8,16},{9,... | collective-permute-start | bytes 688136 | tf_op jit(solution)/shard_map/ppermute | solution.py:575
  127.6 1.6 %collective-permute-start.45 = (bf16[448,256]{1,0:T(8,128)(2,1)S(1)}, bf16[448,256]{1,0:T(8,128)(2,1)S(1)}, u32[]{:S(2)}, u32[]{:S(2)}) collective-permute-start(bf16[448,256]{1,0:T(8,128)(2,1)S(1)} %bitcast.86), channel_id=1, source_target_pairs={{0,16},{1,17},{2,18},{3,19},{4,20},{5,21},{6,22},{7,23},{8,24},{9,... | collective-permute-start | bytes 688136 | tf_op jit(solution)/shard_map/ppermute | solution.py:575
  129.5 2.8 %shard_map.278 = (f32[9,256,256]{2,1,0:T(8,128)}, f32[9,256,256]{2,1,0:T(8,128)}, f32[256,1024]{1,0:T(8,128)}, f32[8,128]{1,0:T(8,128)S(1)}) custom-call(bf16[2816,256]{1,0:T(8,128)(2,1)S(1)} %bitcast.77, bf16[2816,256]{1,0:T(8,128)(2,1)S(1)} %collective-permute-done.48.refs_1_), custom_call_target="tpu_custom_call" | custom-call | flops 1024 | bytes 1024 | tf_op jit(solution)/shard_map/pallas_call | solution.py:547
  132.3 3.0 %collective-permute-done.46.refs_3_ = bf16[448,256]{1,0:T(8,128)(2,1)S(1)} collective-permute-done((bf16[448,256]{1,0:T(8,128)(2,1)S(1)}, bf16[448,256]{1,0:T(8,128)(2,1)S(1)}, u32[]{:S(2)}, u32[]{:S(2)}) %collective-permute-start.46) | collective-permute-done | bytes 229408 | tf_op jit(solution)/shard_map/ppermute | solution.py:575
  135.4 4.4 %collective-permute-done.45.refs_2_ = bf16[448,256]{1,0:T(8,128)(2,1)S(1)} collective-permute-done((bf16[448,256]{1,0:T(8,128)(2,1)S(1)}, bf16[448,256]{1,0:T(8,128)(2,1)S(1)}, u32[]{:S(2)}, u32[]{:S(2)}) %collective-permute-start.45) | collective-permute-done | bytes 229408 | tf_op jit(solution)/shard_map/ppermute | solution.py:575
  140.0 2.4 %collective-permute-done.49.refs_1_ = bf16[1792,256]{1,0:T(8,128)(2,1)S(1)} collective-permute-done((bf16[1792,256]{1,0:T(8,128)(2,1)S(1)}, bf16[1792,256]{1,0:T(8,128)(2,1)S(1)}, u32[]{:S(2)}, u32[]{:S(2)}) %collective-permute-start.49) | collective-permute-done | bytes 917536 | tf_op jit(solution)/shard_map/ppermute | solution.py:34
  142.4 2.0 %shard_map.280 = (f32[9,256,256]{2,1,0:T(8,128)}, f32[1,1024,256]{2,1,0:T(8,128)}, f32[2,256]{1,0:T(2,128)}, f32[2,256]{1,0:T(2,128)}, f32[2,1024]{1,0:T(2,128)}, /*index=5*/f32[2,256]{1,0:T(2,128)}, f32[2,256]{1,0:T(2,128)}) custom-call(bf16[1792,256]{1,0:T(8,128)(2,1)S(1)} %bitcast.79, bf16[1792,256]{1,0:T(8,128)(2,1)S(1)} %collective-permute-done.49.refs_1_), custom_call_target="tpu_custom_call" | custom-call | flops 1024 | bytes 1024 | tf_op jit(solution)/shard_map/pallas_call | solution.py:547
  (97 shorter events, 14.7 us)
Async XLA Ops:
  0.6 15.1 %copy-start.3 = (bf16[3,3,256,256]{3,2,1,0:T(8,128)(2,1)S(1)}, bf16[3,3,256,256]{3,2,1,0:T(8,128)(2,1)}, u32[]{:S(2)}) copy-start(bf16[3,3,256,256]{3,2,1,0:T(8,128)(2,1)} %refs_16_.1) | copy-start | bytes 3538948
  0.7 15.1 %copy-start.4 = (bf16[3,3,256,256]{3,2,1,0:T(8,128)(2,1)S(1)}, bf16[3,3,256,256]{3,2,1,0:T(8,128)(2,1)}, u32[]{:S(2)}) copy-start(bf16[3,3,256,256]{3,2,1,0:T(8,128)(2,1)} %refs_12_.5) | copy-start | bytes 3538948
  0.7 15.1 %copy-start.10 = (f32[2,256]{1,0:T(2,128)S(1)}, f32[2,256]{1,0:T(2,128)}, u32[]{:S(2)}) copy-start(f32[2,256]{1,0:T(2,128)} %refs_5_.1) | copy-start | bytes 6148
  0.7 15.1 %copy-start.11 = (f32[2,256]{1,0:T(2,128)S(1)}, f32[2,256]{1,0:T(2,128)}, u32[]{:S(2)}) copy-start(f32[2,256]{1,0:T(2,128)} %refs_8_.4) | copy-start | bytes 6148
  4.9 1.3 collective-permute-start
  6.2 6.6 %collective-permute-start.3 = (f32[16,128]{1,0:T(8,128)S(1)}, f32[16,128]{1,0:T(8,128)S(1)}, u32[]{:S(2)}, u32[]{:S(2)}) collective-permute-start(f32[16,128]{1,0:T(8,128)S(1)} %add.18.refs_0_), channel_id=1, source_target_pairs={{0,6},{1,7},{2,4},{3,5},{4,2},{5,3},{6,0},{7,1},{8,14},{9,15},{10,... | collective-permute-start | bytes 24584 | tf_op jit(solution)/shard_map/ppermute | solution.py:34
  11.2 4.5 %collective-permute-start.2 = (f32[16,128]{1,0:T(8,128)S(1)}, f32[16,128]{1,0:T(8,128)S(1)}, u32[]{:S(2)}, u32[]{:S(2)}) collective-permute-start(f32[16,128]{1,0:T(8,128)S(1)} %add.18.refs_0_), channel_id=1, source_target_pairs={{0,4},{1,5},{2,6},{3,7},{4,0},{5,1},{6,2},{7,3},{8,12},{9,13},{10,... | collective-permute-start | bytes 24584 | tf_op jit(solution)/shard_map/ppermute | solution.py:34
  11.2 4.5 %collective-permute-start.1 = (f32[16,128]{1,0:T(8,128)S(1)}, f32[16,128]{1,0:T(8,128)S(1)}, u32[]{:S(2)}, u32[]{:S(2)}) collective-permute-start(f32[16,128]{1,0:T(8,128)S(1)} %add.18.refs_0_), channel_id=1, source_target_pairs={{0,2},{1,3},{2,0},{3,1},{4,6},{5,7},{6,4},{7,5},{8,10},{9,11},{10,... | collective-permute-start | bytes 24584 | tf_op jit(solution)/shard_map/ppermute | solution.py:34
  15.8 9.8 %copy-start.2 = (bf16[1,4,14,14,256]{4,1,3,2,0:T(4,128)(2,1)S(1)}, bf16[1,4,14,14,256]{4,1,3,2,0:T(4,128)(2,1)}, u32[]{:S(2)}) copy-start(bf16[1,4,14,14,256]{4,1,3,2,0:T(4,128)(2,1)} %param.16) | copy-start | bytes 1204228
  15.8 9.8 %copy-start.7 = (bf16[256,1024]{1,0:T(8,128)(2,1)S(1)}, bf16[256,1024]{1,0:T(8,128)(2,1)}, u32[]{:S(2)}) copy-start(bf16[256,1024]{1,0:T(8,128)(2,1)} %refs_13_.3) | copy-start | bytes 1572868
  15.8 9.8 %copy-start.8 = (bf16[1,4,14,14,256]{4,1,3,2,0:T(4,128)(2,1)S(1)}, bf16[1,4,14,14,256]{4,1,3,2,0:T(4,128)(2,1)}, u32[]{:S(2)}) copy-start(bf16[1,4,14,14,256]{4,1,3,2,0:T(4,128)(2,1)} %param.18) | copy-start | bytes 1204228
  15.8 9.8 %copy-start.12 = (f32[2,256]{1,0:T(2,128)S(1)}, f32[2,256]{1,0:T(2,128)}, u32[]{:S(2)}) copy-start(f32[2,256]{1,0:T(2,128)} %refs_10_.5) | copy-start | bytes 6148
  15.8 9.8 %copy-start.13 = (f32[2,256]{1,0:T(2,128)S(1)}, f32[2,256]{1,0:T(2,128)}, u32[]{:S(2)}) copy-start(f32[2,256]{1,0:T(2,128)} %refs_9_.3) | copy-start | bytes 6148
  15.8 20.5 %copy-start.1 = (bf16[1,4,14,14,1024]{4,1,3,2,0:T(4,128)(2,1)S(1)}, bf16[1,4,14,14,1024]{4,1,3,2,0:T(4,128)(2,1)}, u32[]{:S(2)}) copy-start(bf16[1,4,14,14,1024]{4,1,3,2,0:T(4,128)(2,1)} %param.17) | copy-start | bytes 4816900
  18.3 1.2 collective-permute-start.4
  19.6 5.4 %collective-permute-start.7 = (f32[8,128]{1,0:T(8,128)S(1)}, f32[8,128]{1,0:T(8,128)S(1)}, u32[]{:S(2)}, u32[]{:S(2)}) collective-permute-start(f32[8,128]{1,0:T(8,128)S(1)} %add.19.refs_0_), channel_id=1, source_target_pairs={{0,6},{1,7},{2,4},{3,5},{4,2},{5,3},{6,0},{7,1},{8,14},{9,15},{10,... | collective-permute-start | bytes 12296 | tf_op jit(solution)/shard_map/ppermute | solution.py:34
  21.0 4.5 %collective-permute-start.6 = (f32[8,128]{1,0:T(8,128)S(1)}, f32[8,128]{1,0:T(8,128)S(1)}, u32[]{:S(2)}, u32[]{:S(2)}) collective-permute-start(f32[8,128]{1,0:T(8,128)S(1)} %add.19.refs_0_), channel_id=1, source_target_pairs={{0,4},{1,5},{2,6},{3,7},{4,0},{5,1},{6,2},{7,3},{8,12},{9,13},{10,... | collective-permute-start | bytes 12296 | tf_op jit(solution)/shard_map/ppermute | solution.py:34
  21.6 4.0 %collective-permute-start.5 = (f32[8,128]{1,0:T(8,128)S(1)}, f32[8,128]{1,0:T(8,128)S(1)}, u32[]{:S(2)}, u32[]{:S(2)}) collective-permute-start(f32[8,128]{1,0:T(8,128)S(1)} %add.19.refs_0_), channel_id=1, source_target_pairs={{0,2},{1,3},{2,0},{3,1},{4,6},{5,7},{6,4},{7,5},{8,10},{9,11},{10,... | collective-permute-start | bytes 12296 | tf_op jit(solution)/shard_map/ppermute | solution.py:34
  25.6 10.7 %copy-start = (bf16[1,4,14,14,1024]{4,1,3,2,0:T(4,128)(2,1)S(1)}, bf16[1,4,14,14,1024]{4,1,3,2,0:T(4,128)(2,1)}, u32[]{:S(2)}) copy-start(bf16[1,4,14,14,1024]{4,1,3,2,0:T(4,128)(2,1)} %param.15) | copy-start | bytes 4816900
  25.6 10.7 %copy-start.9 = (f32[2,1024]{1,0:T(2,128)S(1)}, f32[2,1024]{1,0:T(2,128)}, u32[]{:S(2)}) copy-start(f32[2,1024]{1,0:T(2,128)} %refs_8_.5) | copy-start | bytes 24580
  27.8 1.2 collective-permute-start.8
  29.0 5.6 %collective-permute-start.11 = (f32[24,128]{1,0:T(8,128)S(1)}, f32[24,128]{1,0:T(8,128)S(1)}, u32[]{:S(2)}, u32[]{:S(2)}) collective-permute-start(f32[24,128]{1,0:T(8,128)S(1)} %add.20.refs_0_), channel_id=1, source_target_pairs={{0,6},{1,7},{2,4},{3,5},{4,2},{5,3},{6,0},{7,1},{8,14},{9,15},{10,... | collective-permute-start | bytes 36872 | tf_op jit(solution)/shard_map/ppermute | solution.py:34
  31.6 4.6 %collective-permute-start.10 = (f32[24,128]{1,0:T(8,128)S(1)}, f32[24,128]{1,0:T(8,128)S(1)}, u32[]{:S(2)}, u32[]{:S(2)}) collective-permute-start(f32[24,128]{1,0:T(8,128)S(1)} %add.20.refs_0_), channel_id=1, source_target_pairs={{0,4},{1,5},{2,6},{3,7},{4,0},{5,1},{6,2},{7,3},{8,12},{9,13},{10,... | collective-permute-start | bytes 36872 | tf_op jit(solution)/shard_map/ppermute | solution.py:34
  32.5 3.8 %collective-permute-start.9 = (f32[24,128]{1,0:T(8,128)S(1)}, f32[24,128]{1,0:T(8,128)S(1)}, u32[]{:S(2)}, u32[]{:S(2)}) collective-permute-start(f32[24,128]{1,0:T(8,128)S(1)} %add.20.refs_0_), channel_id=1, source_target_pairs={{0,2},{1,3},{2,0},{3,1},{4,6},{5,7},{6,4},{7,5},{8,10},{9,11},{10,... | collective-permute-start | bytes 36872 | tf_op jit(solution)/shard_map/ppermute | solution.py:34
  40.8 1.2 collective-permute-start.12
  42.1 5.8 %collective-permute-start.15 = (f32[24,128]{1,0:T(8,128)S(1)}, f32[24,128]{1,0:T(8,128)S(1)}, u32[]{:S(2)}, u32[]{:S(2)}) collective-permute-start(f32[24,128]{1,0:T(8,128)S(1)} %add.21.refs_3_.refs_0_), channel_id=1, source_target_pairs={{0,6},{1,7},{2,4},{3,5},{4,2},{5,3},{6,0},{7,1},{8,14},{9,15},{10,... | collective-permute-start | bytes 36872 | tf_op jit(solution)/shard_map/ppermute | solution.py:34
  43.4 4.6 %collective-permute-start.14 = (f32[24,128]{1,0:T(8,128)S(1)}, f32[24,128]{1,0:T(8,128)S(1)}, u32[]{:S(2)}, u32[]{:S(2)}) collective-permute-start(f32[24,128]{1,0:T(8,128)S(1)} %add.21.refs_3_.refs_0_), channel_id=1, source_target_pairs={{0,4},{1,5},{2,6},{3,7},{4,0},{5,1},{6,2},{7,3},{8,12},{9,13},{10,... | collective-permute-start | bytes 36872 | tf_op jit(solution)/shard_map/ppermute | solution.py:34
  44.3 3.8 %collective-permute-start.13 = (f32[24,128]{1,0:T(8,128)S(1)}, f32[24,128]{1,0:T(8,128)S(1)}, u32[]{:S(2)}, u32[]{:S(2)}) collective-permute-start(f32[24,128]{1,0:T(8,128)S(1)} %add.21.refs_3_.refs_0_), channel_id=1, source_target_pairs={{0,2},{1,3},{2,0},{3,1},{4,6},{5,7},{6,4},{7,5},{8,10},{9,11},{10,... | collective-permute-start | bytes 36872 | tf_op jit(solution)/shard_map/ppermute | solution.py:34
  49.4 1.2 collective-permute-start.16
  53.0 7.3 %collective-permute-start.17 = (bf16[2816,256]{1,0:T(8,128)(2,1)S(1)}, bf16[2816,256]{1,0:T(8,128)(2,1)S(1)}, u32[]{:S(2)}, u32[]{:S(2)}) collective-permute-start(bf16[2816,256]{1,0:T(8,128)(2,1)S(1)} %get-tuple-element.114), channel_id=1, source_target_pairs={{0,1},{1,0},{2,3},{3,2},{4,5},{5,4},{6,7},{7,6},{8,9},{9,8},{10,11... | collective-permute-start | bytes 4325384 | tf_op jit(solution)/shard_map/ppermute | solution.py:34
  53.2 5.4 %collective-permute-start.20 = (f32[8,128]{1,0:T(8,128)S(1)}, f32[8,128]{1,0:T(8,128)S(1)}, u32[]{:S(2)}, u32[]{:S(2)}) collective-permute-start(f32[8,128]{1,0:T(8,128)S(1)} %add.22.refs_11_.refs_0_), channel_id=1, source_target_pairs={{0,6},{1,7},{2,4},{3,5},{4,2},{5,3},{6,0},{7,1},{8,14},{9,15},{10,... | collective-permute-start | bytes 12296 | tf_op jit(solution)/shard_map/ppermute | solution.py:34
  55.7 4.5 %collective-permute-start.19 = (f32[8,128]{1,0:T(8,128)S(1)}, f32[8,128]{1,0:T(8,128)S(1)}, u32[]{:S(2)}, u32[]{:S(2)}) collective-permute-start(f32[8,128]{1,0:T(8,128)S(1)} %add.22.refs_11_.refs_0_), channel_id=1, source_target_pairs={{0,4},{1,5},{2,6},{3,7},{4,0},{5,1},{6,2},{7,3},{8,12},{9,13},{10,... | collective-permute-start | bytes 12296 | tf_op jit(solution)/shard_map/ppermute | solution.py:34
  56.7 3.6 %collective-permute-start.18 = (f32[8,128]{1,0:T(8,128)S(1)}, f32[8,128]{1,0:T(8,128)S(1)}, u32[]{:S(2)}, u32[]{:S(2)}) collective-permute-start(f32[8,128]{1,0:T(8,128)S(1)} %add.22.refs_11_.refs_0_), channel_id=1, source_target_pairs={{0,2},{1,3},{2,0},{3,1},{4,6},{5,7},{6,4},{7,5},{8,10},{9,11},{10,... | collective-permute-start | bytes 12296 | tf_op jit(solution)/shard_map/ppermute | solution.py:34
  60.7 11.4 %collective-permute-start.21 = (bf16[1408,256]{1,0:T(8,128)(2,1)S(1)}, bf16[1408,256]{1,0:T(8,128)(2,1)S(1)}, u32[]{:S(2)}, u32[]{:S(2)}) collective-permute-start(bf16[1408,256]{1,0:T(8,128)(2,1)S(1)} %get-tuple-element.116), channel_id=1, source_target_pairs={{0,8},{1,17},{2,10},{3,19},{4,12},{5,21},{6,14},{7,23},{8,0},{9,25... | collective-permute-start | bytes 2162696 | tf_op jit(solution)/shard_map/ppermute | solution.py:575
  63.5 1.2 collective-permute-start.22
  64.8 7.4 %collective-permute-start.26 = (f32[8,128]{1,0:T(8,128)S(1)}, f32[8,128]{1,0:T(8,128)S(1)}, u32[]{:S(2)}, u32[]{:S(2)}) collective-permute-start(f32[8,128]{1,0:T(8,128)S(1)} %add.23.refs_3_.refs_0_), channel_id=1, source_target_pairs={{0,6},{1,7},{2,4},{3,5},{4,2},{5,3},{6,0},{7,1},{8,14},{9,15},{10,... | collective-permute-start | bytes 12296 | tf_op jit(solution)/shard_map/ppermute | solution.py:34
  66.1 6.1 %collective-permute-start.25 = (f32[8,128]{1,0:T(8,128)S(1)}, f32[8,128]{1,0:T(8,128)S(1)}, u32[]{:S(2)}, u32[]{:S(2)}) collective-permute-start(f32[8,128]{1,0:T(8,128)S(1)} %add.23.refs_3_.refs_0_), channel_id=1, source_target_pairs={{0,4},{1,5},{2,6},{3,7},{4,0},{5,1},{6,2},{7,3},{8,12},{9,13},{10,... | collective-permute-start | bytes 12296 | tf_op jit(solution)/shard_map/ppermute | solution.py:34
  67.2 5.1 %collective-permute-start.24 = (f32[8,128]{1,0:T(8,128)S(1)}, f32[8,128]{1,0:T(8,128)S(1)}, u32[]{:S(2)}, u32[]{:S(2)}) collective-permute-start(f32[8,128]{1,0:T(8,128)S(1)} %add.23.refs_3_.refs_0_), channel_id=1, source_target_pairs={{0,2},{1,3},{2,0},{3,1},{4,6},{5,7},{6,4},{7,5},{8,10},{9,11},{10,... | collective-permute-start | bytes 12296 | tf_op jit(solution)/shard_map/ppermute | solution.py:34
  73.2 6.3 %copy-start.6 = (bf16[1024,256]{1,0:T(8,128)(2,1)S(1)}, bf16[1024,256]{1,0:T(8,128)(2,1)}, u32[]{:S(2)}) copy-start(bf16[1024,256]{1,0:T(8,128)(2,1)} %refs_4_.3) | copy-start | bytes 1572868
  73.3 2.5 %collective-permute-start.27 = (bf16[1792,256]{1,0:T(8,128)(2,1)S(1)}, bf16[1792,256]{1,0:T(8,128)(2,1)S(1)}, u32[]{:S(2)}, u32[]{:S(2)}) collective-permute-start(bf16[1792,256]{1,0:T(8,128)(2,1)S(1)} %get-tuple-element.131), channel_id=1, source_target_pairs={{0,1},{1,0},{2,3},{3,2},{4,5},{5,4},{6,7},{7,6},{8,9},{9,8},{10,11... | collective-permute-start | bytes 2752520 | tf_op jit(solution)/shard_map/ppermute | solution.py:34
  73.3 10.2 %collective-permute-start.23 = (bf16[704,256]{1,0:T(8,128)(2,1)S(1)}, bf16[704,256]{1,0:T(8,128)(2,1)S(1)}, u32[]{:S(2)}, u32[]{:S(2)}) collective-permute-start(bf16[704,256]{1,0:T(8,128)(2,1)S(1)} %get-tuple-element.124), channel_id=1, source_target_pairs={{0,16},{1,9},{2,18},{3,11},{4,20},{5,13},{6,22},{7,15},{8,24},{9,1... | collective-permute-start | bytes 1081352 | tf_op jit(solution)/shard_map/ppermute | solution.py:575
  76.0 9.7 %collective-permute-start.28 = (bf16[448,256]{1,0:T(8,128)(2,1)S(1)}, bf16[448,256]{1,0:T(8,128)(2,1)S(1)}, u32[]{:S(2)}, u32[]{:S(2)}) collective-permute-start(bf16[448,256]{1,0:T(8,128)(2,1)S(1)} %get-tuple-element.140), channel_id=1, source_target_pairs={{0,8},{1,9},{2,10},{3,11},{4,12},{5,13},{6,14},{7,15},{8,0},{9,1},... | collective-permute-start | bytes 688136 | tf_op jit(solution)/shard_map/ppermute | solution.py:575
  77.5 14.9 %collective-permute-start.29 = (bf16[448,256]{1,0:T(8,128)(2,1)S(1)}, bf16[448,256]{1,0:T(8,128)(2,1)S(1)}, u32[]{:S(2)}, u32[]{:S(2)}) collective-permute-start(bf16[448,256]{1,0:T(8,128)(2,1)S(1)} %get-tuple-element.141), channel_id=1, source_target_pairs={{0,16},{1,17},{2,18},{3,19},{4,20},{5,21},{6,22},{7,23},{8,24},{9,... | collective-permute-start | bytes 688136 | tf_op jit(solution)/shard_map/ppermute | solution.py:575
  79.1 13.3 %collective-permute-start.30 = (bf16[448,256]{1,0:T(8,128)(2,1)S(1)}, bf16[448,256]{1,0:T(8,128)(2,1)S(1)}, u32[]{:S(2)}, u32[]{:S(2)}) collective-permute-start(bf16[448,256]{1,0:T(8,128)(2,1)S(1)} %get-tuple-element.142), channel_id=1, source_target_pairs={{0,24},{1,25},{2,26},{3,27},{4,28},{5,29},{6,30},{7,31},{8,16},{9,... | collective-permute-start | bytes 688136 | tf_op jit(solution)/shard_map/ppermute | solution.py:575
  79.6 2.1 %copy-start.5 = (bf16[3,3,256,256]{3,2,1,0:T(8,128)(2,1)S(1)}, bf16[3,3,256,256]{3,2,1,0:T(8,128)(2,1)}, u32[]{:S(2)}) copy-start(bf16[3,3,256,256]{3,2,1,0:T(8,128)(2,1)} %refs_3_.3) | copy-start | bytes 3538948
  83.6 8.9 %collective-permute-start.34 = (bf16[176,256]{1,0:T(8,128)(2,1)S(1)}, bf16[176,256]{1,0:T(8,128)(2,1)S(1)}, u32[]{:S(2)}, u32[]{:S(2)}) collective-permute-start(bf16[176,256]{1,0:T(8,128)(2,1)S(1)} %get-tuple-element.148), channel_id=1, source_target_pairs={{0,2},{1,3},{2,0},{3,1},{4,6},{5,7},{6,4},{7,5},{8,10},{9,11},{10,... | collective-permute-start | bytes 270344 | tf_op jit(solution)/shard_map/ppermute | solution.py:575
  84.6 9.3 %collective-permute-start.35 = (bf16[176,256]{1,0:T(8,128)(2,1)S(1)}, bf16[176,256]{1,0:T(8,128)(2,1)S(1)}, u32[]{:S(2)}, u32[]{:S(2)}) collective-permute-start(bf16[176,256]{1,0:T(8,128)(2,1)S(1)} %get-tuple-element.149), channel_id=1, source_target_pairs={{0,4},{1,5},{2,6},{3,7},{4,0},{5,1},{6,2},{7,3},{8,12},{9,13},{10,... | collective-permute-start | bytes 270344 | tf_op jit(solution)/shard_map/ppermute | solution.py:575
  85.7 8.2 %collective-permute-start.36 = (bf16[176,256]{1,0:T(8,128)(2,1)S(1)}, bf16[176,256]{1,0:T(8,128)(2,1)S(1)}, u32[]{:S(2)}, u32[]{:S(2)}) collective-permute-start(bf16[176,256]{1,0:T(8,128)(2,1)S(1)} %get-tuple-element.150), channel_id=1, source_target_pairs={{0,6},{1,7},{2,4},{3,5},{4,2},{5,3},{6,0},{7,1},{8,14},{9,15},{10,... | collective-permute-start | bytes 270344 | tf_op jit(solution)/shard_map/ppermute | solution.py:575
  93.9 7.2 %collective-permute-start.39 = (bf16[176,256]{1,0:T(8,128)(2,1)S(1)}, bf16[176,256]{1,0:T(8,128)(2,1)S(1)}, u32[]{:S(2)}, u32[]{:S(2)}) collective-permute-start(bf16[176,256]{1,0:T(8,128)(2,1)S(1)} %shard_map.272.refs_0_.refs_4_), channel_id=1, source_target_pairs={{0,6},{1,7},{2,4},{3,5},{4,2},{5,3},{6,0},{7,1},{8,14},{9,15},{10,... | collective-permute-start | bytes 270344 | tf_op jit(solution)/shard_map/ppermute | solution.py:575
  96.3 7.8 %collective-permute-start.38 = (bf16[176,256]{1,0:T(8,128)(2,1)S(1)}, bf16[176,256]{1,0:T(8,128)(2,1)S(1)}, u32[]{:S(2)}, u32[]{:S(2)}) collective-permute-start(bf16[176,256]{1,0:T(8,128)(2,1)S(1)} %shard_map.272.refs_0_.refs_4_), channel_id=1, source_target_pairs={{0,4},{1,5},{2,6},{3,7},{4,0},{5,1},{6,2},{7,3},{8,12},{9,13},{10,... | collective-permute-start | bytes 270344 | tf_op jit(solution)/shard_map/ppermute | solution.py:575
  97.0 7.1 %collective-permute-start.37 = (bf16[176,256]{1,0:T(8,128)(2,1)S(1)}, bf16[176,256]{1,0:T(8,128)(2,1)S(1)}, u32[]{:S(2)}, u32[]{:S(2)}) collective-permute-start(bf16[176,256]{1,0:T(8,128)(2,1)S(1)} %shard_map.272.refs_0_.refs_4_), channel_id=1, source_target_pairs={{0,2},{1,3},{2,0},{3,1},{4,6},{5,7},{6,4},{7,5},{8,10},{9,11},{10,... | collective-permute-start | bytes 270344 | tf_op jit(solution)/shard_map/ppermute | solution.py:575
  104.1 10.2 %collective-permute-start.43 = (bf16[704,256]{1,0:T(8,128)(2,1)S(1)}, bf16[704,256]{1,0:T(8,128)(2,1)S(1)}, u32[]{:S(2)}, u32[]{:S(2)}) collective-permute-start(bf16[704,256]{1,0:T(8,128)(2,1)S(1)} %bitcast.80), channel_id=1, source_target_pairs={{0,16},{1,9},{2,18},{3,11},{4,20},{5,13},{6,22},{7,15},{8,24},{9,1... | collective-permute-start | bytes 1081352 | tf_op jit(solution)/shard_map/ppermute | solution.py:575
  105.6 4.4 %collective-permute-start.31 = (bf16[112,256]{1,0:T(8,128)(2,1)S(1)}, bf16[112,256]{1,0:T(8,128)(2,1)S(1)}, u32[]{:S(2)}, u32[]{:S(2)}) collective-permute-start(bf16[112,256]{1,0:T(8,128)(2,1)S(1)} %get-tuple-element.145), channel_id=1, source_target_pairs={{0,2},{1,3},{2,0},{3,1},{4,6},{5,7},{6,4},{7,5},{8,10},{9,11},{10,... | collective-permute-start | bytes 172040 | tf_op jit(solution)/shard_map/ppermute | solution.py:575
  105.7 5.1 %collective-permute-start.32 = (bf16[112,256]{1,0:T(8,128)(2,1)S(1)}, bf16[112,256]{1,0:T(8,128)(2,1)S(1)}, u32[]{:S(2)}, u32[]{:S(2)}) collective-permute-start(bf16[112,256]{1,0:T(8,128)(2,1)S(1)} %get-tuple-element.146), channel_id=1, source_target_pairs={{0,4},{1,5},{2,6},{3,7},{4,0},{5,1},{6,2},{7,3},{8,12},{9,13},{10,... | collective-permute-start | bytes 172040 | tf_op jit(solution)/shard_map/ppermute | solution.py:575
  108.3 6.0 %collective-permute-start.33 = (bf16[112,256]{1,0:T(8,128)(2,1)S(1)}, bf16[112,256]{1,0:T(8,128)(2,1)S(1)}, u32[]{:S(2)}, u32[]{:S(2)}) collective-permute-start(bf16[112,256]{1,0:T(8,128)(2,1)S(1)} %get-tuple-element.147), channel_id=1, source_target_pairs={{0,6},{1,7},{2,4},{3,5},{4,2},{5,3},{6,0},{7,1},{8,14},{9,15},{10,... | collective-permute-start | bytes 172040 | tf_op jit(solution)/shard_map/ppermute | solution.py:575
  114.4 11.4 %collective-permute-start.47 = (bf16[1408,256]{1,0:T(8,128)(2,1)S(1)}, bf16[1408,256]{1,0:T(8,128)(2,1)S(1)}, u32[]{:S(2)}, u32[]{:S(2)}) collective-permute-start(bf16[1408,256]{1,0:T(8,128)(2,1)S(1)} %bitcast.67), channel_id=1, source_target_pairs={{0,8},{1,17},{2,10},{3,19},{4,12},{5,21},{6,14},{7,23},{8,0},{9,25... | collective-permute-start | bytes 2162696 | tf_op jit(solution)/shard_map/ppermute | solution.py:575
  116.1 6.0 %collective-permute-start.42 = (bf16[112,256]{1,0:T(8,128)(2,1)S(1)}, bf16[112,256]{1,0:T(8,128)(2,1)S(1)}, u32[]{:S(2)}, u32[]{:S(2)}) collective-permute-start(bf16[112,256]{1,0:T(8,128)(2,1)S(1)} %shard_map.274.refs_2_.refs_0_), channel_id=1, source_target_pairs={{0,6},{1,7},{2,4},{3,5},{4,2},{5,3},{6,0},{7,1},{8,14},{9,15},{10,... | collective-permute-start | bytes 172040 | tf_op jit(solution)/shard_map/ppermute | solution.py:575
  117.8 5.5 %collective-permute-start.41 = (bf16[112,256]{1,0:T(8,128)(2,1)S(1)}, bf16[112,256]{1,0:T(8,128)(2,1)S(1)}, u32[]{:S(2)}, u32[]{:S(2)}) collective-permute-start(bf16[112,256]{1,0:T(8,128)(2,1)S(1)} %shard_map.274.refs_2_.refs_0_), channel_id=1, source_target_pairs={{0,4},{1,5},{2,6},{3,7},{4,0},{5,1},{6,2},{7,3},{8,12},{9,13},{10,... | collective-permute-start | bytes 172040 | tf_op jit(solution)/shard_map/ppermute | solution.py:575
  117.8 5.5 %collective-permute-start.40 = (bf16[112,256]{1,0:T(8,128)(2,1)S(1)}, bf16[112,256]{1,0:T(8,128)(2,1)S(1)}, u32[]{:S(2)}, u32[]{:S(2)}) collective-permute-start(bf16[112,256]{1,0:T(8,128)(2,1)S(1)} %shard_map.274.refs_2_.refs_0_), channel_id=1, source_target_pairs={{0,2},{1,3},{2,0},{3,1},{4,6},{5,7},{6,4},{7,5},{8,10},{9,11},{10,... | collective-permute-start | bytes 172040 | tf_op jit(solution)/shard_map/ppermute | solution.py:575
  125.9 3.6 %collective-permute-start.48 = (bf16[2816,256]{1,0:T(8,128)(2,1)S(1)}, bf16[2816,256]{1,0:T(8,128)(2,1)S(1)}, u32[]{:S(2)}, u32[]{:S(2)}) collective-permute-start(bf16[2816,256]{1,0:T(8,128)(2,1)S(1)} %bitcast.76), channel_id=1, source_target_pairs={{0,1},{1,0},{2,3},{3,2},{4,5},{5,4},{6,7},{7,6},{8,9},{9,8},{10,11... | collective-permute-start | bytes 4325384 | tf_op jit(solution)/shard_map/ppermute | solution.py:34
  126.0 9.4 %collective-permute-start.46 = (bf16[448,256]{1,0:T(8,128)(2,1)S(1)}, bf16[448,256]{1,0:T(8,128)(2,1)S(1)}, u32[]{:S(2)}, u32[]{:S(2)}) collective-permute-start(bf16[448,256]{1,0:T(8,128)(2,1)S(1)} %bitcast.85), channel_id=1, source_target_pairs={{0,24},{1,25},{2,26},{3,27},{4,28},{5,29},{6,30},{7,31},{8,16},{9,... | collective-permute-start | bytes 688136 | tf_op jit(solution)/shard_map/ppermute | solution.py:575
  127.6 12.2 %collective-permute-start.45 = (bf16[448,256]{1,0:T(8,128)(2,1)S(1)}, bf16[448,256]{1,0:T(8,128)(2,1)S(1)}, u32[]{:S(2)}, u32[]{:S(2)}) collective-permute-start(bf16[448,256]{1,0:T(8,128)(2,1)S(1)} %bitcast.86), channel_id=1, source_target_pairs={{0,16},{1,17},{2,18},{3,19},{4,20},{5,21},{6,22},{7,23},{8,24},{9,... | collective-permute-start | bytes 688136 | tf_op jit(solution)/shard_map/ppermute | solution.py:575
  129.1 10.7 %collective-permute-start.44 = (bf16[448,256]{1,0:T(8,128)(2,1)S(1)}, bf16[448,256]{1,0:T(8,128)(2,1)S(1)}, u32[]{:S(2)}, u32[]{:S(2)}) collective-permute-start(bf16[448,256]{1,0:T(8,128)(2,1)S(1)} %bitcast.87), channel_id=1, source_target_pairs={{0,8},{1,9},{2,10},{3,11},{4,12},{5,13},{6,14},{7,15},{8,0},{9,1},... | collective-permute-start | bytes 688136 | tf_op jit(solution)/shard_map/ppermute | solution.py:575
  139.9 2.5 %collective-permute-start.49 = (bf16[1792,256]{1,0:T(8,128)(2,1)S(1)}, bf16[1792,256]{1,0:T(8,128)(2,1)S(1)}, u32[]{:S(2)}, u32[]{:S(2)}) collective-permute-start(bf16[1792,256]{1,0:T(8,128)(2,1)S(1)} %bitcast.78), channel_id=1, source_target_pairs={{0,1},{1,0},{2,3},{3,2},{4,5},{5,4},{6,7},{7,6},{8,9},{9,8},{10,11... | collective-permute-start | bytes 2752520 | tf_op jit(solution)/shard_map/ppermute | solution.py:34

commit v2 on v1

--- a/solution.py
+++ b/solution.py
@@ -46,8 +46,13 @@
     return [value] + [swap(value, "clip", stride * k) for k in range(1, radix)]
 
 
-def sigmoid(u):
-    return 0.5 + 0.5 * jnp.tanh(0.5 * u)
+def silu_of_half(v):
+    return v * (1.0 + jnp.tanh(v))
+
+
+def twice_slope_of_half(v):
+    t = jnp.tanh(v)
+    return (1.0 + t) * (1.0 + v * (1.0 - t))
 
 
 def total_of(refs):
@@ -162,12 +167,12 @@
 
 
 def slope_back(grad, z, mean, scale, norm, ups_ref):
-    hat = (z - mean) * scale
-    u = norm[0:1] * hat + norm[1:2]
-    s = sigmoid(u)
-    up = grad.astype(BF16).astype(F32) * (s + u * s * (1.0 - s))
+    gain = 0.5 * norm[0:1] * scale
+    half = z * gain + (0.5 * norm[1:2] - mean * gain)
+    up = (0.5 * grad.astype(BF16).astype(F32)) * twice_slope_of_half(half)
     ups_ref[...] = up
-    return down(eights(up)), down(eights(up * hat))
+    total_up = down(eights(up))
+    return total_up, scale * (down(eights(up * z)) - mean * total_up)
 
 
 def kernel_1(width, valid_far, x_far, m_far, reduce_far, first_far, mask8, zr, z1, sums, *rest):
@@ -217,9 +222,8 @@
         ((zr, reduce_n, ra, spatial_w, zs), (z1, first_n, mm, second_w, z2))
     ):
         mean, scale = moments(total, 2 * k * step, step, channels, count)
-        gain = norm[0:1] * scale
-        u = z_ref[...] * gain + (norm[1:2] - mean * gain)
-        value = u * sigmoid(u)
+        gain = 0.5 * norm[0:1] * scale
+        value = silu_of_half(z_ref[...] * gain + (0.5 * norm[1:2] - mean * gain))
         act[...] = value.astype(BF16)
         spread(value, *place, same, edge)
         out[...] = conv_of(same, edge, weight)
@@ -237,9 +241,8 @@
     total_2[...] = total
     count = total_1[4 * step : 4 * step + 1, 0:1]
     mean, scale = moments(total, 0, step, channels, count)
-    gain = spatial_n[0:1] * scale
-    u = zs[...] * gain + (spatial_n[1:2] - mean * gain)
-    sa[...] = (u * sigmoid(u)).astype(BF16)
+    gain = 0.5 * spatial_n[0:1] * scale
+    sa[...] = silu_of_half(zs[...] * gain + (0.5 * spatial_n[1:2] - mean * gain)).astype(BF16)
     mask = mask8[...]
     sums[...] = jnp.zeros(sums.shape, F32)
     for at in range(0, wide, channels):
@@ -250,14 +253,14 @@
         put_row(sums, at // LANES, down(kept))
         put_row(sums, wide_step + at // LANES, down(kept * z))
     mean, scale = moments(total, 2 * step, step, channels, count)
-    hat = eights((z2[...] - mean) * scale)
-    motion = eights(rows_of(m[...]).astype(F32))
-    u = second_n[0:1] * hat + second_n[1:2] + motion
-    s = sigmoid(u)
-    up = eights(rows_of(gm[...]).astype(F32)) * mask * (s + u * s * (1.0 - s))
+    gain = 0.5 * second_n[0:1] * scale
+    z = eights(z2[...])
+    half = z * gain + (0.5 * second_n[1:2] - mean * gain) + 0.5 * eights(rows_of(m[...]).astype(F32))
+    up = (eights(rows_of(gm[...]).astype(F32)) * (0.5 * mask)) * twice_slope_of_half(half)
     up2[...] = rows_of(up)
-    put_row(sums, 2 * wide_step, down(up))
-    put_row(sums, 2 * wide_step + step, down(up * hat))
+    total_up = down(up)
+    put_row(sums, 2 * wide_step, total_up)
+    put_row(sums, 2 * wide_step + step, scale * (down(up * z) - mean * total_up))
 
 
 def kernel_4(place, parts, mask8, total_1, total_2, z1, z2, up2, ze, x, gx, *rest):
@@ -286,30 +289,31 @@
     part, rows = channels, 16
     frames = place[1]
     eight = (8, part)
+    half_mask = 0.5 * mask
     for at in range(0, wide, part):
         lanes = slice(at, at + part)
         mean, scale = moments(total, at // LANES, wide_step, part, count)
-        mean8, scale8 = jnp.broadcast_to(mean, eight), jnp.broadcast_to(scale, eight)
-        gain8 = jnp.broadcast_to(expand_n[0:1, lanes], eight)
-        shift8 = jnp.broadcast_to(expand_n[1:2, lanes], eight)
+        gain = 0.5 * expand_n[0:1, lanes] * scale
+        gain8 = jnp.broadcast_to(gain, eight)
+        shift8 = jnp.broadcast_to(0.5 * expand_n[1:2, lanes] - mean * gain, eight)
 
         def step_of(i, totals):
             here = pl.ds(pl.multiple_of(i * rows, rows), rows)
             pixels = pl.ds(i * (rows // frames), rows // frames)
-            hat = (eights(ze[here, lanes]) - mean8) * scale8
+            z = eights(ze[here, lanes])
             x_here = eights(rows_of(x[pixels, :, lanes]).astype(F32))
             g_here = eights(rows_of(gx[pixels, :, lanes]).astype(F32))
-            u = hat * gain8 + shift8 + x_here
-            s = sigmoid(u)
-            up = g_here * mask * (s + u * s * (1.0 - s))
+            half = z * gain8 + shift8 + 0.5 * x_here
+            up = (g_here * half_mask) * twice_slope_of_half(half)
             upe[here, lanes] = rows_of(up)
-            cross = up * hat
-            return (totals[0] + jnp.sum(up, axis=0), totals[1] + jnp.sum(cross, axis=0))
+            return (totals[0] + jnp.sum(up, axis=0), totals[1] + jnp.sum(up * z, axis=0))
 
         empty = (jnp.zeros(eight, F32), jnp.zeros(eight, F32))
-        totals = lax.fori_loop(0, ze.shape[0] // rows, step_of, empty, unroll=7)
-        put_row(sums, at // LANES, down(totals[0][None]))
-        put_row(sums, wide_step + at // LANES, down(totals[1][None]))
+        totals = lax.fori_loop(0, ze.shape[0] // rows, step_of, empty, unroll=True)
+        total_up = down(totals[0][None])
+        put_row(sums, at // LANES, total_up)
+        total_cross = scale * (down(totals[1][None]) - mean * total_up)
+        put_row(sums, wide_step + at // LANES, total_cross)
 
 
 def kernel_5(parts, mask8, total_1, total_2, total_3, ze, upe, zs, expand_n, spatial_n, expand_w, *rest):
@@ -427,28 +431,34 @@
     count = total_1[4 * step : 4 * step + 1, 0:1]
     mask = mask8[...]
 
-    def joined(z, here, mean, scale, norm):
-        u = eights(z) * (norm[0:1] * scale) + (norm[1:2] - mean * (norm[0:1] * scale)) + here
-        return rows_of(mask * (u * sigmoid(u)) + (1.0 - mask) * here).astype(BF16)
+    def folded(mean, scale, norm):
+        gain = 0.5 * norm[0:1] * scale
+        shape = (8, gain.shape[1])
+        return jnp.broadcast_to(gain, shape), jnp.broadcast_to(0.5 * norm[1:2] - mean * gain, shape)
+
+    def joined(z, here, gain, shift):
+        out = silu_of_half(eights(z) * gain + shift + 0.5 * here)
+        return rows_of(here + mask * (out - here)).astype(BF16)
 
     mean, scale = moments(total_2[...], 2 * step, step, channels, count)
+    gain, shift = folded(mean, scale, second_n[...])
     motion = eights(rows_of(m[...]).astype(F32))
-    motion_out[...] = joined(z2[...], motion, mean, scale, second_n[...]).reshape(motion_out.shape)
+    motion_out[...] = joined(z2[...], motion, gain, shift).reshape(motion_out.shape)
     part, rows, frames = channels, 16, place[1]
     for at in range(0, wide, part):
         lanes = slice(at, at + part)
         mean, scale = moments(total_3[...], at // LANES, wide_step, part, count)
-        norm = expand_n[:, lanes]
+        gain, shift = folded(mean, scale, expand_n[:, lanes])
 
         def step_of(i, carry):
             here = pl.ds(pl.multiple_of(i * rows, rows), rows)
             pixels = pl.ds(i * (rows // frames), rows // frames)
             frame = eights(rows_of(x[pixels, :, lanes]).astype(F32))
-            out = joined(ze[here, lanes], frame, mean, scale, norm)
+            out = joined(ze[here, lanes], frame, gain, shift)
             iframe_out[pixels, :, lanes] = out.reshape(-1, frames, part)
             return carry
 
-        lax.fori_loop(0, ze.shape[0] // rows, step_of, 0, unroll=7)
+        lax.fori_loop(0, ze.shape[0] // rows, step_of, 0, unroll=True)
 
 
 def norm_rows(sums, row, channels):
@@ -684,7 +694,7 @@
 FIRST_PHASES = (over_section_halves, over_clip)
 SECOND_PHASES = (over_section, over_clip)
 EARLY = 1
-ORDER = ("Ts0", "I", "M", "Fs2", "O", "Ts1", "Ft", "Fg2", "Tt", "Fg1", "Tg1", "Fg0", "X", "Tg0")
+ORDER = ('Ts0', 'I', 'M', 'Fs2', 'Ts1', 'Ft', 'Fg2', 'Tt', 'Fg1', 'O', 'Tg1', 'Fg0', 'X', 'Tg0')
 
 
 def per_device(

time: 145 us -> 142 us (0.979)
  Pallas kernels: 36.6 us -> 34.7 us
    pallas_call x27, Pallas kernels: 36.6 us -> 34.7 us  [call(): pl.pallas_call(body, out_shape=outs, in_specs=[pl.BlockSpec(memory_space=...]
where the time goes in v2:
time: 142 us
  starting transfers between devices  59.9 us (42%)
  waiting for transfers between devices  46.4 us (33%)
  Pallas kernels  34.7 us (24%)
    pallas_call x27, Pallas kernels, call(): pl.pallas_call(body, out_shape=outs, in_specs=[pl.BlockSpec(memory_space=...  34.7 us
    ppermute x22, starting transfers between devices, send(): return lax.ppermute(value, ('section', 'clip'), route)  31.1 us
    ppermute x28, starting transfers between devices, swap(): return lax.ppermute(value, axis, [(i, i ^ mask) for i in range(size)])  28.8 us
    ppermute x22, waiting for transfers between devices, send(): return lax.ppermute(value, ('section', 'clip'), route)  25.1 us
    ppermute x28, waiting for transfers between devices, swap(): return lax.ppermute(value, axis, [(i, i ^ mask) for i in range(size)])  21.3 us
  transfers between devices with their start and end apart: 50, of which 31 were waited for; matrix products, arithmetic and copies ran while one was open for 0% of the time, Pallas kernels for 11%

profile of v2, /device:TPU:0, one launch (start us, length us, event | category | flops | bytes accessed | tf_op | source)
XLA Modules:
  0.0 142.2 jit_solution(10376777587296080672)
XLA Ops:
  0.7 4.2 %shard_map.254 = (f32[8,256]{1,0:T(8,128)S(1)}, f32[784,256]{1,0:T(8,128)S(1)}, f32[784,256]{1,0:T(8,128)S(1)}, f32[16,128]{1,0:T(8,128)S(1)}) custom-call(s32[4,4]{1,0:T(4,128)} %refs_0_.1, bf16[196,4,1024]{2,1,0:T(4,128)(2,1)} %bitcast.61, bf16[196,4,256]{2,1,0:T(4,128)(2,1)} %bitcast.72, bf16[1024,256]{1,0:T(8,128)(2,1)} %refs_4_.3, ...), custom_call_target="tpu_custom_call" | custom-call | flops 1024 | bytes 1024 | tf_op jit(solution)/shard_map/pallas_call | solution.py:557
  6.2 4.9 %collective-permute-start.3 = (f32[16,128]{1,0:T(8,128)S(1)}, f32[16,128]{1,0:T(8,128)S(1)}, u32[]{:S(2)}, u32[]{:S(2)}) collective-permute-start(f32[16,128]{1,0:T(8,128)S(1)} %add.18.refs_0_), channel_id=1, source_target_pairs={{0,6},{1,7},{2,4},{3,5},{4,2},{5,3},{6,0},{7,1},{8,14},{9,15},{10,... | collective-permute-start | bytes 24584 | tf_op jit(solution)/shard_map/ppermute | solution.py:34
  11.8 1.1 collective-permute-done.3.refs_3_
  12.8 2.9 %collective-permute-done.2.refs_2_ = f32[16,128]{1,0:T(8,128)S(1)} collective-permute-done((f32[16,128]{1,0:T(8,128)S(1)}, f32[16,128]{1,0:T(8,128)S(1)}, u32[]{:S(2)}, u32[]{:S(2)}) %collective-permute-start.2) | collective-permute-done | bytes 8224 | tf_op jit(solution)/shard_map/ppermute | solution.py:34
  15.8 2.4 %shard_map.255 = (f32[16,128]{1,0:T(8,128)S(1)}, bf16[784,256]{1,0:T(8,128)(2,1)S(1)}, bf16[784,256]{1,0:T(8,128)(2,1)S(1)}, f32[784,256]{1,0:T(8,128)S(1)}, f32...) custom-call(f32[16,128]{1,0:T(8,128)S(1)} %add.18.refs_0_, f32[16,128]{1,0:T(8,128)S(1)} %collective-permute-done.1.refs_1_, ...), custom_call_target="tpu_custom_call" | custom-call | flops 1024 | bytes 1024 | tf_op jit(solution)/shard_map/pallas_call | solution.py:557
  18.3 1.2 collective-permute-done.4
  19.5 1.5 %collective-permute-start.7 = (f32[8,128]{1,0:T(8,128)S(1)}, f32[8,128]{1,0:T(8,128)S(1)}, u32[]{:S(2)}, u32[]{:S(2)}) collective-permute-start(f32[8,128]{1,0:T(8,128)S(1)} %add.19.refs_0_), channel_id=1, source_target_pairs={{0,6},{1,7},{2,4},{3,5},{4,2},{5,3},{6,0},{7,1},{8,14},{9,15},{10,... | collective-permute-start | bytes 12296 | tf_op jit(solution)/shard_map/ppermute | solution.py:34
  21.5 2.4 %collective-permute-start.5 = (f32[8,128]{1,0:T(8,128)S(1)}, f32[8,128]{1,0:T(8,128)S(1)}, u32[]{:S(2)}, u32[]{:S(2)}) collective-permute-start(f32[8,128]{1,0:T(8,128)S(1)} %add.19.refs_0_), channel_id=1, source_target_pairs={{0,2},{1,3},{2,0},{3,1},{4,6},{5,7},{6,4},{7,5},{8,10},{9,11},{10,... | collective-permute-start | bytes 12296 | tf_op jit(solution)/shard_map/ppermute | solution.py:34
  23.9 1.0 collective-permute-done.7.refs_3_
  25.5 1.7 %shard_map.256 = (f32[8,128]{1,0:T(8,128)S(1)}, bf16[784,256]{1,0:T(8,128)(2,1)S(1)}, f32[784,1024]{1,0:T(8,128)S(1)}, f32[784,256]{1,0:T(8,128)S(1)}, f32[24,128]{1,0:T(8,128)S(1)}) custom-call(f32[8,128]{1,0:T(8,128)S(1)} %add.19.refs_0_, f32[8,128]{1,0:T(8,128)S(1)} %collective-permute-done.5.refs_1_, f32[8,128]{1,0:T(8,128)S(1)} %collective-permute-done.6.refs_2_, ...), custom_call_target="tpu_custom_call" | custom-call | flops 1024 | bytes 1024 | tf_op jit(solution)/shard_map/pallas_call | solution.py:557
  27.4 1.2 collective-permute-done.8
  28.5 2.5 %collective-permute-start.11 = (f32[24,128]{1,0:T(8,128)S(1)}, f32[24,128]{1,0:T(8,128)S(1)}, u32[]{:S(2)}, u32[]{:S(2)}) collective-permute-start(f32[24,128]{1,0:T(8,128)S(1)} %add.20.refs_0_), channel_id=1, source_target_pairs={{0,6},{1,7},{2,4},{3,5},{4,2},{5,3},{6,0},{7,1},{8,14},{9,15},{10,... | collective-permute-start | bytes 36872 | tf_op jit(solution)/shard_map/ppermute | solution.py:34
  32.9 1.2 collective-permute-done.11.refs_3_
  34.2 1.5 %collective-permute-done.10.refs_2_ = f32[24,128]{1,0:T(8,128)S(1)} collective-permute-done((f32[24,128]{1,0:T(8,128)S(1)}, f32[24,128]{1,0:T(8,128)S(1)}, u32[]{:S(2)}, u32[]{:S(2)}) %collective-permute-start.10) | collective-permute-done | bytes 12320 | tf_op jit(solution)/shard_map/ppermute | solution.py:34
  35.8 3.3 %shard_map.257 = (f32[24,128]{1,0:T(8,128)S(1)}, f32[784,1024]{1,0:T(8,128)S(1)}, f32[784,256]{1,0:T(8,128)S(1)}, bf16[784,768]{1,0:T(8,128)(2,1)S(1)}, bf16[896...) custom-call(f32[24,128]{1,0:T(8,128)S(1)} %add.20.refs_0_, f32[24,128]{1,0:T(8,128)S(1)} %collective-permute-done.9.refs_1_, ...), custom_call_target="tpu_custom_call" | custom-call | flops 1024 | bytes 1024 | tf_op jit(solution)/shard_map/pallas_call | solution.py:557
  39.2 1.2 collective-permute-done.12
  40.4 1.3 collective-permute-start.15
  42.7 2.1 %collective-permute-start.13 = (f32[24,128]{1,0:T(8,128)S(1)}, f32[24,128]{1,0:T(8,128)S(1)}, u32[]{:S(2)}, u32[]{:S(2)}) collective-permute-start(f32[24,128]{1,0:T(8,128)S(1)} %add.21.refs_3_.refs_0_), channel_id=1, source_target_pairs={{0,2},{1,3},{2,0},{3,1},{4,6},{5,7},{6,4},{7,5},{8,10},{9,11},{10,... | collective-permute-start | bytes 36872 | tf_op jit(solution)/shard_map/ppermute | solution.py:34
  44.8 1.4 %shard_map.258 = (bf16[2816,256]{1,0:T(8,128)(2,1)S(1)}, bf16[2816,256]{1,0:T(8,128)(2,1)S(1)}) custom-call(bf16[784,256]{1,0:T(8,128)(2,1)S(1)} %get-tuple-element.103.refs_0_, bf16[784,768]{1,0:T(8,128)(2,1)S(1)} %get-tuple-element.104.refs_1_, bf16[896,768]{1,0:T(8,128)(2,1)S(1)} %get-tuple-element.105.refs_2_, f32[24,128]{1,0:T(8,128)S(1)} %add.21.refs_3_.refs_0_), custom_call_target="tpu_custom_call" | custom-call | flops 1024 | bytes 1024 | tf_op jit(solution)/shard_map/pallas_call | solution.py:557
  46.5 1.4 shard_map.259
  47.9 1.2 collective-permute-done.16
  49.1 2.3 %shard_map.260 = (bf16[784,768]{1,0:T(8,128)(2,1)S(1)}, bf16[896,768]{1,0:T(8,128)(2,1)S(1)}, bf16[2816,256]{1,0:T(8,128)(2,1)S(1)}, bf16[2816,256]{1,0:T(8,128)(2,1)S(1)}) custom-call(f32[8,256]{1,0:T(8,128)S(1)} %get-tuple-element.88.refs_4_.refs_0_, ...), custom_call_target="tpu_custom_call", output_to_operand_aliasing={{2}: (9, {}), {3}: (10, {})} | custom-call | flops 1024 | bytes 1024 | tf_op jit(solution)/shard_map/pallas_call | solution.py:557
  51.6 2.5 %collective-permute-start.20 = (f32[8,128]{1,0:T(8,128)S(1)}, f32[8,128]{1,0:T(8,128)S(1)}, u32[]{:S(2)}, u32[]{:S(2)}) collective-permute-start(f32[8,128]{1,0:T(8,128)S(1)} %add.22.refs_11_.refs_0_), channel_id=1, source_target_pairs={{0,6},{1,7},{2,4},{3,5},{4,2},{5,3},{6,0},{7,1},{8,14},{9,15},{10,... | collective-permute-start | bytes 12296 | tf_op jit(solution)/shard_map/ppermute | solution.py:34
  54.1 1.0 collective-permute-start.19
  56.0 1.0 collective-permute-done.20.refs_4_.refs_3_
  57.0 1.6 %collective-permute-done.19.refs_3_.refs_2_ = f32[8,128]{1,0:T(8,128)S(1)} collective-permute-done((f32[8,128]{1,0:T(8,128)S(1)}, f32[8,128]{1,0:T(8,128)S(1)}, u32[]{:S(2)}, u32[]{:S(2)}) %collective-permute-start.19) | collective-permute-done | bytes 4128 | tf_op jit(solution)/shard_map/ppermute | solution.py:34
  59.1 1.6 %collective-permute-start.21 = (bf16[1408,256]{1,0:T(8,128)(2,1)S(1)}, bf16[1408,256]{1,0:T(8,128)(2,1)S(1)}, u32[]{:S(2)}, u32[]{:S(2)}) collective-permute-start(bf16[1408,256]{1,0:T(8,128)(2,1)S(1)} %get-tuple-element.116), channel_id=1, source_target_pairs={{0,8},{1,17},{2,10},{3,19},{4,12},{5,21},{6,14},{7,23},{8,0},{9,25... | collective-permute-start | bytes 2162696 | tf_op jit(solution)/shard_map/ppermute | solution.py:585
  60.7 1.3 shard_map.262
  62.1 1.2 collective-permute-done.22
  63.2 1.4 collective-permute-start.26
  64.6 1.0 collective-permute-start.25
  65.6 2.0 %collective-permute-start.24 = (f32[8,128]{1,0:T(8,128)S(1)}, f32[8,128]{1,0:T(8,128)S(1)}, u32[]{:S(2)}, u32[]{:S(2)}) collective-permute-start(f32[8,128]{1,0:T(8,128)S(1)} %add.23.refs_3_.refs_0_), channel_id=1, source_target_pairs={{0,2},{1,3},{2,0},{3,1},{4,6},{5,7},{6,4},{7,5},{8,10},{9,11},{10,... | collective-permute-start | bytes 12296 | tf_op jit(solution)/shard_map/ppermute | solution.py:34
  67.6 1.4 %shard_map.263 = (bf16[1792,256]{1,0:T(8,128)(2,1)S(1)}, bf16[1792,256]{1,0:T(8,128)(2,1)S(1)}) custom-call(bf16[784,256]{1,0:T(8,128)(2,1)S(1)} %get-tuple-element.117.refs_0_, bf16[784,768]{1,0:T(8,128)(2,1)S(1)} %get-tuple-element.119.refs_1_, bf16[896,768]{1,0:T(8,128)(2,1)S(1)} %get-tuple-element.120.refs_2_, f32[8,128]{1,0:T(8,128)S(1)} %add.23.refs_3_.refs_0_), custom_call_target="tpu_custom_call" | custom-call | flops 1024 | bytes 1024 | tf_op jit(solution)/shard_map/pallas_call | solution.py:557
  69.0 1.4 collective-permute-done.21
  71.8 1.6 %collective-permute-start.23 = (bf16[704,256]{1,0:T(8,128)(2,1)S(1)}, bf16[704,256]{1,0:T(8,128)(2,1)S(1)}, u32[]{:S(2)}, u32[]{:S(2)}) collective-permute-start(bf16[704,256]{1,0:T(8,128)(2,1)S(1)} %get-tuple-element.124), channel_id=1, source_target_pairs={{0,16},{1,9},{2,18},{3,11},{4,20},{5,13},{6,22},{7,15},{8,24},{9,1... | collective-permute-start | bytes 1081352 | tf_op jit(solution)/shard_map/ppermute | solution.py:585
  74.4 1.6 %collective-permute-start.31 = (bf16[448,256]{1,0:T(8,128)(2,1)S(1)}, bf16[448,256]{1,0:T(8,128)(2,1)S(1)}, u32[]{:S(2)}, u32[]{:S(2)}) collective-permute-start(bf16[448,256]{1,0:T(8,128)(2,1)S(1)} %get-tuple-element.139), channel_id=1, source_target_pairs={{0,8},{1,9},{2,10},{3,11},{4,12},{5,13},{6,14},{7,15},{8,0},{9,1},... | collective-permute-start | bytes 688136 | tf_op jit(solution)/shard_map/ppermute | solution.py:585
  76.0 1.5 %collective-permute-start.32 = (bf16[448,256]{1,0:T(8,128)(2,1)S(1)}, bf16[448,256]{1,0:T(8,128)(2,1)S(1)}, u32[]{:S(2)}, u32[]{:S(2)}) collective-permute-start(bf16[448,256]{1,0:T(8,128)(2,1)S(1)} %get-tuple-element.140), channel_id=1, source_target_pairs={{0,16},{1,17},{2,18},{3,19},{4,20},{5,21},{6,22},{7,23},{8,24},{9,... | collective-permute-start | bytes 688136 | tf_op jit(solution)/shard_map/ppermute | solution.py:585
  78.0 2.1 %shard_map.267 = (bf16[196,4,1024]{2,1,0:T(4,128)(2,1)}, f32[8,128]{1,0:T(8,128)S(1)}) custom-call(f32[8,256]{1,0:T(8,128)S(1)} %get-tuple-element.88.refs_4_.refs_0_, bf16[196,4,1024]{2,1,0:T(4,128)(2,1)S(1)} %bitcast.71, f32[784,1024]{1,0:T(8,128)S(1)} %get-tuple-element.102.refs_9_.refs_2_, bf16[784,256]{1,0:T(8,128)(2,1)S(1)} %get-tuple-element.129.refs_3_, ...), custom_call_target="tpu_custom_call" | custom-call | flops 1024 | bytes 1024 | tf_op jit(solution)/shard_map/pallas_call | solution.py:557
  80.1 1.9 %shard_map.268 = (bf16[196,4,256]{2,1,0:T(4,128)(2,1)}, f32[8,128]{1,0:T(8,128)S(1)}) custom-call(f32[8,256]{1,0:T(8,128)S(1)} %get-tuple-element.88.refs_4_.refs_0_, bf16[784,768]{1,0:T(8,128)(2,1)S(1)} %get-tuple-element.125.refs_1_, bf16[896,768]{1,0:T(8,128)(2,1)S(1)} %get-tuple-element.126.refs_2_, bf16[3,3,256,256]{3,2,1,0:T(8,128)(2,1)S(1)} %copy-done.5, ...), custom_call_target="tpu_custom_call" | custom-call | flops 1024 | bytes 1024 | tf_op jit(solution)/shard_map/pallas_call | solution.py:557
  83.0 1.1 collective-permute-start.29
  84.1 2.4 %collective-permute-start.30 = (bf16[176,256]{1,0:T(8,128)(2,1)S(1)}, bf16[176,256]{1,0:T(8,128)(2,1)S(1)}, u32[]{:S(2)}, u32[]{:S(2)}) collective-permute-start(bf16[176,256]{1,0:T(8,128)(2,1)S(1)} %get-tuple-element.138), channel_id=1, source_target_pairs={{0,6},{1,7},{2,4},{3,5},{4,2},{5,3},{6,0},{7,1},{8,14},{9,15},{10,... | collective-permute-start | bytes 270344 | tf_op jit(solution)/shard_map/ppermute | solution.py:585
  86.5 1.6 %collective-permute-done.32 = bf16[448,256]{1,0:T(8,128)(2,1)S(1)} collective-permute-done((bf16[448,256]{1,0:T(8,128)(2,1)S(1)}, bf16[448,256]{1,0:T(8,128)(2,1)S(1)}, u32[]{:S(2)}, u32[]{:S(2)}) %collective-permute-start.32) | collective-permute-done | bytes 229408 | tf_op jit(solution)/shard_map/ppermute | solution.py:585
  89.0 3.3 %collective-permute-done.29.refs_2_ = bf16[176,256]{1,0:T(8,128)(2,1)S(1)} collective-permute-done((bf16[176,256]{1,0:T(8,128)(2,1)S(1)}, bf16[176,256]{1,0:T(8,128)(2,1)S(1)}, u32[]{:S(2)}, u32[]{:S(2)}) %collective-permute-start.29) | collective-permute-done | bytes 90144 | tf_op jit(solution)/shard_map/ppermute | solution.py:585
  92.4 2.4 %collective-permute-start.36 = (bf16[176,256]{1,0:T(8,128)(2,1)S(1)}, bf16[176,256]{1,0:T(8,128)(2,1)S(1)}, u32[]{:S(2)}, u32[]{:S(2)}) collective-permute-start(bf16[176,256]{1,0:T(8,128)(2,1)S(1)} %shard_map.271.refs_0_.refs_4_), channel_id=1, source_target_pairs={{0,6},{1,7},{2,4},{3,5},{4,2},{5,3},{6,0},{7,1},{8,14},{9,15},{10,... | collective-permute-start | bytes 270344 | tf_op jit(solution)/shard_map/ppermute | solution.py:585
  95.4 1.4 collective-permute-start.34
  96.8 2.8 %collective-permute-done.36.refs_3_ = bf16[176,256]{1,0:T(8,128)(2,1)S(1)} collective-permute-done((bf16[176,256]{1,0:T(8,128)(2,1)S(1)}, bf16[176,256]{1,0:T(8,128)(2,1)S(1)}, u32[]{:S(2)}, u32[]{:S(2)}) %collective-permute-start.36) | collective-permute-done | bytes 90144 | tf_op jit(solution)/shard_map/ppermute | solution.py:585
  99.6 2.8 %collective-permute-done.35.refs_2_ = bf16[176,256]{1,0:T(8,128)(2,1)S(1)} collective-permute-done((bf16[176,256]{1,0:T(8,128)(2,1)S(1)}, bf16[176,256]{1,0:T(8,128)(2,1)S(1)}, u32[]{:S(2)}, u32[]{:S(2)}) %collective-permute-start.35) | collective-permute-done | bytes 90144 | tf_op jit(solution)/shard_map/ppermute | solution.py:585
  102.5 1.6 %collective-permute-start.37 = (bf16[704,256]{1,0:T(8,128)(2,1)S(1)}, bf16[704,256]{1,0:T(8,128)(2,1)S(1)}, u32[]{:S(2)}, u32[]{:S(2)}) collective-permute-start(bf16[704,256]{1,0:T(8,128)(2,1)S(1)} %bitcast.80), channel_id=1, source_target_pairs={{0,16},{1,9},{2,18},{3,11},{4,20},{5,13},{6,22},{7,15},{8,24},{9,1... | collective-permute-start | bytes 1081352 | tf_op jit(solution)/shard_map/ppermute | solution.py:585
  104.1 1.9 %collective-permute-start.39 = (bf16[112,256]{1,0:T(8,128)(2,1)S(1)}, bf16[112,256]{1,0:T(8,128)(2,1)S(1)}, u32[]{:S(2)}, u32[]{:S(2)}) collective-permute-start(bf16[112,256]{1,0:T(8,128)(2,1)S(1)} %get-tuple-element.144), channel_id=1, source_target_pairs={{0,4},{1,5},{2,6},{3,7},{4,0},{5,1},{6,2},{7,3},{8,12},{9,13},{10,... | collective-permute-start | bytes 172040 | tf_op jit(solution)/shard_map/ppermute | solution.py:585
  106.0 2.4 %collective-permute-start.40 = (bf16[112,256]{1,0:T(8,128)(2,1)S(1)}, bf16[112,256]{1,0:T(8,128)(2,1)S(1)}, u32[]{:S(2)}, u32[]{:S(2)}) collective-permute-start(bf16[112,256]{1,0:T(8,128)(2,1)S(1)} %get-tuple-element.145), channel_id=1, source_target_pairs={{0,6},{1,7},{2,4},{3,5},{4,2},{5,3},{6,0},{7,1},{8,14},{9,15},{10,... | collective-permute-start | bytes 172040 | tf_op jit(solution)/shard_map/ppermute | solution.py:585
  108.5 1.0 collective-permute-done.39.refs_2_
  109.5 2.5 %collective-permute-done.40.refs_3_ = bf16[112,256]{1,0:T(8,128)(2,1)S(1)} collective-permute-done((bf16[112,256]{1,0:T(8,128)(2,1)S(1)}, bf16[112,256]{1,0:T(8,128)(2,1)S(1)}, u32[]{:S(2)}, u32[]{:S(2)}) %collective-permute-start.40) | collective-permute-done | bytes 57376 | tf_op jit(solution)/shard_map/ppermute | solution.py:585
  112.2 1.6 %collective-permute-start.47 = (bf16[1408,256]{1,0:T(8,128)(2,1)S(1)}, bf16[1408,256]{1,0:T(8,128)(2,1)S(1)}, u32[]{:S(2)}, u32[]{:S(2)}) collective-permute-start(bf16[1408,256]{1,0:T(8,128)(2,1)S(1)} %bitcast.67), channel_id=1, source_target_pairs={{0,8},{1,17},{2,10},{3,19},{4,12},{5,21},{6,14},{7,23},{8,0},{9,25... | collective-permute-start | bytes 2162696 | tf_op jit(solution)/shard_map/ppermute | solution.py:585
  113.8 2.3 %collective-permute-start.43 = (bf16[112,256]{1,0:T(8,128)(2,1)S(1)}, bf16[112,256]{1,0:T(8,128)(2,1)S(1)}, u32[]{:S(2)}, u32[]{:S(2)}) collective-permute-start(bf16[112,256]{1,0:T(8,128)(2,1)S(1)} %shard_map.273.refs_2_.refs_0_), channel_id=1, source_target_pairs={{0,6},{1,7},{2,4},{3,5},{4,2},{5,3},{6,0},{7,1},{8,14},{9,15},{10,... | collective-permute-start | bytes 172040 | tf_op jit(solution)/shard_map/ppermute | solution.py:585
  116.2 2.0 %collective-permute-start.41 = (bf16[112,256]{1,0:T(8,128)(2,1)S(1)}, bf16[112,256]{1,0:T(8,128)(2,1)S(1)}, u32[]{:S(2)}, u32[]{:S(2)}) collective-permute-start(bf16[112,256]{1,0:T(8,128)(2,1)S(1)} %shard_map.273.refs_2_.refs_0_), channel_id=1, source_target_pairs={{0,2},{1,3},{2,0},{3,1},{4,6},{5,7},{6,4},{7,5},{8,10},{9,11},{10,... | collective-permute-start | bytes 172040 | tf_op jit(solution)/shard_map/ppermute | solution.py:585
  118.2 3.9 %shard_map.275 = (bf16[196,4,1024]{2,1,0:T(4,128)(2,1)}, bf16[196,4,256]{2,1,0:T(4,128)(2,1)}, f32[8,128]{1,0:T(8,128)S(1)}) custom-call(f32[8,256]{1,0:T(8,128)S(1)} %get-tuple-element.88.refs_4_.refs_0_, f32[16,128]{1,0:T(8,128)S(1)} %get-tuple-element.92.refs_5_.refs_1_, f32[8,128]{1,0:T(8,128)S(1)} %get-tuple-element.96.refs_6_.refs_2_, ...), custom_call_target="tpu_custom_call" | custom-call | flops 1024 | bytes 1024 | tf_op jit(solution)/shard_map/pallas_call | solution.py:557
  122.2 1.3 collective-permute-done.47.refs_1_
  123.7 1.6 %collective-permute-start.46 = (bf16[448,256]{1,0:T(8,128)(2,1)S(1)}, bf16[448,256]{1,0:T(8,128)(2,1)S(1)}, u32[]{:S(2)}, u32[]{:S(2)}) collective-permute-start(bf16[448,256]{1,0:T(8,128)(2,1)S(1)} %bitcast.85), channel_id=1, source_target_pairs={{0,24},{1,25},{2,26},{3,27},{4,28},{5,29},{6,30},{7,31},{8,16},{9,... | collective-permute-start | bytes 688136 | tf_op jit(solution)/shard_map/ppermute | solution.py:585
  125.3 1.5 %collective-permute-start.45 = (bf16[448,256]{1,0:T(8,128)(2,1)S(1)}, bf16[448,256]{1,0:T(8,128)(2,1)S(1)}, u32[]{:S(2)}, u32[]{:S(2)}) collective-permute-start(bf16[448,256]{1,0:T(8,128)(2,1)S(1)} %bitcast.86), channel_id=1, source_target_pairs={{0,16},{1,17},{2,18},{3,19},{4,20},{5,21},{6,22},{7,23},{8,24},{9,... | collective-permute-start | bytes 688136 | tf_op jit(solution)/shard_map/ppermute | solution.py:585
  127.3 2.8 %shard_map.278 = (f32[9,256,256]{2,1,0:T(8,128)}, f32[9,256,256]{2,1,0:T(8,128)}, f32[256,1024]{1,0:T(8,128)}, f32[8,128]{1,0:T(8,128)S(1)}) custom-call(bf16[2816,256]{1,0:T(8,128)(2,1)S(1)} %bitcast.77, bf16[2816,256]{1,0:T(8,128)(2,1)S(1)} %collective-permute-done.48.refs_1_), custom_call_target="tpu_custom_call" | custom-call | flops 1024 | bytes 1024 | tf_op jit(solution)/shard_map/pallas_call | solution.py:557
  130.1 3.0 %collective-permute-done.46.refs_3_ = bf16[448,256]{1,0:T(8,128)(2,1)S(1)} collective-permute-done((bf16[448,256]{1,0:T(8,128)(2,1)S(1)}, bf16[448,256]{1,0:T(8,128)(2,1)S(1)}, u32[]{:S(2)}, u32[]{:S(2)}) %collective-permute-start.46) | collective-permute-done | bytes 229408 | tf_op jit(solution)/shard_map/ppermute | solution.py:585
  133.1 4.4 %collective-permute-done.45.refs_2_ = bf16[448,256]{1,0:T(8,128)(2,1)S(1)} collective-permute-done((bf16[448,256]{1,0:T(8,128)(2,1)S(1)}, bf16[448,256]{1,0:T(8,128)(2,1)S(1)}, u32[]{:S(2)}, u32[]{:S(2)}) %collective-permute-start.45) | collective-permute-done | bytes 229408 | tf_op jit(solution)/shard_map/ppermute | solution.py:585
  137.7 2.4 %collective-permute-done.49.refs_1_ = bf16[1792,256]{1,0:T(8,128)(2,1)S(1)} collective-permute-done((bf16[1792,256]{1,0:T(8,128)(2,1)S(1)}, bf16[1792,256]{1,0:T(8,128)(2,1)S(1)}, u32[]{:S(2)}, u32[]{:S(2)}) %collective-permute-start.49) | collective-permute-done | bytes 917536 | tf_op jit(solution)/shard_map/ppermute | solution.py:34
  140.2 2.0 %shard_map.280 = (f32[9,256,256]{2,1,0:T(8,128)}, f32[1,1024,256]{2,1,0:T(8,128)}, f32[2,256]{1,0:T(2,128)}, f32[2,256]{1,0:T(2,128)}, f32[2,1024]{1,0:T(2,128)}, /*index=5*/f32[2,256]{1,0:T(2,128)}, f32[2,256]{1,0:T(2,128)}) custom-call(bf16[1792,256]{1,0:T(8,128)(2,1)S(1)} %bitcast.79, bf16[1792,256]{1,0:T(8,128)(2,1)S(1)} %collective-permute-done.49.refs_1_), custom_call_target="tpu_custom_call" | custom-call | flops 1024 | bytes 1024 | tf_op jit(solution)/shard_map/pallas_call | solution.py:557
  (97 shorter events, 14.8 us)
Async XLA Ops:
  0.6 15.1 %copy-start.3 = (bf16[3,3,256,256]{3,2,1,0:T(8,128)(2,1)S(1)}, bf16[3,3,256,256]{3,2,1,0:T(8,128)(2,1)}, u32[]{:S(2)}) copy-start(bf16[3,3,256,256]{3,2,1,0:T(8,128)(2,1)} %refs_16_.1) | copy-start | bytes 3538948
  0.7 15.1 %copy-start.4 = (bf16[3,3,256,256]{3,2,1,0:T(8,128)(2,1)S(1)}, bf16[3,3,256,256]{3,2,1,0:T(8,128)(2,1)}, u32[]{:S(2)}) copy-start(bf16[3,3,256,256]{3,2,1,0:T(8,128)(2,1)} %refs_12_.5) | copy-start | bytes 3538948
  0.7 15.1 %copy-start.10 = (f32[2,256]{1,0:T(2,128)S(1)}, f32[2,256]{1,0:T(2,128)}, u32[]{:S(2)}) copy-start(f32[2,256]{1,0:T(2,128)} %refs_5_.1) | copy-start | bytes 6148
  0.7 15.1 %copy-start.11 = (f32[2,256]{1,0:T(2,128)S(1)}, f32[2,256]{1,0:T(2,128)}, u32[]{:S(2)}) copy-start(f32[2,256]{1,0:T(2,128)} %refs_8_.4) | copy-start | bytes 6148
  4.9 1.3 collective-permute-start
  6.2 6.6 %collective-permute-start.3 = (f32[16,128]{1,0:T(8,128)S(1)}, f32[16,128]{1,0:T(8,128)S(1)}, u32[]{:S(2)}, u32[]{:S(2)}) collective-permute-start(f32[16,128]{1,0:T(8,128)S(1)} %add.18.refs_0_), channel_id=1, source_target_pairs={{0,6},{1,7},{2,4},{3,5},{4,2},{5,3},{6,0},{7,1},{8,14},{9,15},{10,... | collective-permute-start | bytes 24584 | tf_op jit(solution)/shard_map/ppermute | solution.py:34
  11.2 4.5 %collective-permute-start.2 = (f32[16,128]{1,0:T(8,128)S(1)}, f32[16,128]{1,0:T(8,128)S(1)}, u32[]{:S(2)}, u32[]{:S(2)}) collective-permute-start(f32[16,128]{1,0:T(8,128)S(1)} %add.18.refs_0_), channel_id=1, source_target_pairs={{0,4},{1,5},{2,6},{3,7},{4,0},{5,1},{6,2},{7,3},{8,12},{9,13},{10,... | collective-permute-start | bytes 24584 | tf_op jit(solution)/shard_map/ppermute | solution.py:34
  11.2 4.5 %collective-permute-start.1 = (f32[16,128]{1,0:T(8,128)S(1)}, f32[16,128]{1,0:T(8,128)S(1)}, u32[]{:S(2)}, u32[]{:S(2)}) collective-permute-start(f32[16,128]{1,0:T(8,128)S(1)} %add.18.refs_0_), channel_id=1, source_target_pairs={{0,2},{1,3},{2,0},{3,1},{4,6},{5,7},{6,4},{7,5},{8,10},{9,11},{10,... | collective-permute-start | bytes 24584 | tf_op jit(solution)/shard_map/ppermute | solution.py:34
  15.8 9.7 %copy-start.2 = (bf16[1,4,14,14,256]{4,1,3,2,0:T(4,128)(2,1)S(1)}, bf16[1,4,14,14,256]{4,1,3,2,0:T(4,128)(2,1)}, u32[]{:S(2)}) copy-start(bf16[1,4,14,14,256]{4,1,3,2,0:T(4,128)(2,1)} %param.16) | copy-start | bytes 1204228
  15.8 9.7 %copy-start.7 = (bf16[256,1024]{1,0:T(8,128)(2,1)S(1)}, bf16[256,1024]{1,0:T(8,128)(2,1)}, u32[]{:S(2)}) copy-start(bf16[256,1024]{1,0:T(8,128)(2,1)} %refs_13_.3) | copy-start | bytes 1572868
  15.8 9.7 %copy-start.8 = (bf16[1,4,14,14,256]{4,1,3,2,0:T(4,128)(2,1)S(1)}, bf16[1,4,14,14,256]{4,1,3,2,0:T(4,128)(2,1)}, u32[]{:S(2)}) copy-start(bf16[1,4,14,14,256]{4,1,3,2,0:T(4,128)(2,1)} %param.18) | copy-start | bytes 1204228
  15.8 9.7 %copy-start.12 = (f32[2,256]{1,0:T(2,128)S(1)}, f32[2,256]{1,0:T(2,128)}, u32[]{:S(2)}) copy-start(f32[2,256]{1,0:T(2,128)} %refs_10_.5) | copy-start | bytes 6148
  15.8 9.7 %copy-start.13 = (f32[2,256]{1,0:T(2,128)S(1)}, f32[2,256]{1,0:T(2,128)}, u32[]{:S(2)}) copy-start(f32[2,256]{1,0:T(2,128)} %refs_9_.3) | copy-start | bytes 6148
  15.8 20.0 %copy-start.1 = (bf16[1,4,14,14,1024]{4,1,3,2,0:T(4,128)(2,1)S(1)}, bf16[1,4,14,14,1024]{4,1,3,2,0:T(4,128)(2,1)}, u32[]{:S(2)}) copy-start(bf16[1,4,14,14,1024]{4,1,3,2,0:T(4,128)(2,1)} %param.17) | copy-start | bytes 4816900
  18.2 1.2 collective-permute-start.4
  19.5 5.4 %collective-permute-start.7 = (f32[8,128]{1,0:T(8,128)S(1)}, f32[8,128]{1,0:T(8,128)S(1)}, u32[]{:S(2)}, u32[]{:S(2)}) collective-permute-start(f32[8,128]{1,0:T(8,128)S(1)} %add.19.refs_0_), channel_id=1, source_target_pairs={{0,6},{1,7},{2,4},{3,5},{4,2},{5,3},{6,0},{7,1},{8,14},{9,15},{10,... | collective-permute-start | bytes 12296 | tf_op jit(solution)/shard_map/ppermute | solution.py:34
  20.9 4.5 %collective-permute-start.6 = (f32[8,128]{1,0:T(8,128)S(1)}, f32[8,128]{1,0:T(8,128)S(1)}, u32[]{:S(2)}, u32[]{:S(2)}) collective-permute-start(f32[8,128]{1,0:T(8,128)S(1)} %add.19.refs_0_), channel_id=1, source_target_pairs={{0,4},{1,5},{2,6},{3,7},{4,0},{5,1},{6,2},{7,3},{8,12},{9,13},{10,... | collective-permute-start | bytes 12296 | tf_op jit(solution)/shard_map/ppermute | solution.py:34
  21.5 4.0 %collective-permute-start.5 = (f32[8,128]{1,0:T(8,128)S(1)}, f32[8,128]{1,0:T(8,128)S(1)}, u32[]{:S(2)}, u32[]{:S(2)}) collective-permute-start(f32[8,128]{1,0:T(8,128)S(1)} %add.19.refs_0_), channel_id=1, source_target_pairs={{0,2},{1,3},{2,0},{3,1},{4,6},{5,7},{6,4},{7,5},{8,10},{9,11},{10,... | collective-permute-start | bytes 12296 | tf_op jit(solution)/shard_map/ppermute | solution.py:34
  25.5 10.3 %copy-start = (bf16[1,4,14,14,1024]{4,1,3,2,0:T(4,128)(2,1)S(1)}, bf16[1,4,14,14,1024]{4,1,3,2,0:T(4,128)(2,1)}, u32[]{:S(2)}) copy-start(bf16[1,4,14,14,1024]{4,1,3,2,0:T(4,128)(2,1)} %param.15) | copy-start | bytes 4816900
  25.5 10.3 %copy-start.9 = (f32[2,1024]{1,0:T(2,128)S(1)}, f32[2,1024]{1,0:T(2,128)}, u32[]{:S(2)}) copy-start(f32[2,1024]{1,0:T(2,128)} %refs_8_.5) | copy-start | bytes 24580
  27.3 1.2 collective-permute-start.8
  28.5 5.6 %collective-permute-start.11 = (f32[24,128]{1,0:T(8,128)S(1)}, f32[24,128]{1,0:T(8,128)S(1)}, u32[]{:S(2)}, u32[]{:S(2)}) collective-permute-start(f32[24,128]{1,0:T(8,128)S(1)} %add.20.refs_0_), channel_id=1, source_target_pairs={{0,6},{1,7},{2,4},{3,5},{4,2},{5,3},{6,0},{7,1},{8,14},{9,15},{10,... | collective-permute-start | bytes 36872 | tf_op jit(solution)/shard_map/ppermute | solution.py:34
  31.1 4.6 %collective-permute-start.10 = (f32[24,128]{1,0:T(8,128)S(1)}, f32[24,128]{1,0:T(8,128)S(1)}, u32[]{:S(2)}, u32[]{:S(2)}) collective-permute-start(f32[24,128]{1,0:T(8,128)S(1)} %add.20.refs_0_), channel_id=1, source_target_pairs={{0,4},{1,5},{2,6},{3,7},{4,0},{5,1},{6,2},{7,3},{8,12},{9,13},{10,... | collective-permute-start | bytes 36872 | tf_op jit(solution)/shard_map/ppermute | solution.py:34
  32.0 3.8 %collective-permute-start.9 = (f32[24,128]{1,0:T(8,128)S(1)}, f32[24,128]{1,0:T(8,128)S(1)}, u32[]{:S(2)}, u32[]{:S(2)}) collective-permute-start(f32[24,128]{1,0:T(8,128)S(1)} %add.20.refs_0_), channel_id=1, source_target_pairs={{0,2},{1,3},{2,0},{3,1},{4,6},{5,7},{6,4},{7,5},{8,10},{9,11},{10,... | collective-permute-start | bytes 36872 | tf_op jit(solution)/shard_map/ppermute | solution.py:34
  39.2 1.2 collective-permute-start.12
  40.4 5.8 %collective-permute-start.15 = (f32[24,128]{1,0:T(8,128)S(1)}, f32[24,128]{1,0:T(8,128)S(1)}, u32[]{:S(2)}, u32[]{:S(2)}) collective-permute-start(f32[24,128]{1,0:T(8,128)S(1)} %add.21.refs_3_.refs_0_), channel_id=1, source_target_pairs={{0,6},{1,7},{2,4},{3,5},{4,2},{5,3},{6,0},{7,1},{8,14},{9,15},{10,... | collective-permute-start | bytes 36872 | tf_op jit(solution)/shard_map/ppermute | solution.py:34
  41.7 4.6 %collective-permute-start.14 = (f32[24,128]{1,0:T(8,128)S(1)}, f32[24,128]{1,0:T(8,128)S(1)}, u32[]{:S(2)}, u32[]{:S(2)}) collective-permute-start(f32[24,128]{1,0:T(8,128)S(1)} %add.21.refs_3_.refs_0_), channel_id=1, source_target_pairs={{0,4},{1,5},{2,6},{3,7},{4,0},{5,1},{6,2},{7,3},{8,12},{9,13},{10,... | collective-permute-start | bytes 36872 | tf_op jit(solution)/shard_map/ppermute | solution.py:34
  42.7 3.8 %collective-permute-start.13 = (f32[24,128]{1,0:T(8,128)S(1)}, f32[24,128]{1,0:T(8,128)S(1)}, u32[]{:S(2)}, u32[]{:S(2)}) collective-permute-start(f32[24,128]{1,0:T(8,128)S(1)} %add.21.refs_3_.refs_0_), channel_id=1, source_target_pairs={{0,2},{1,3},{2,0},{3,1},{4,6},{5,7},{6,4},{7,5},{8,10},{9,11},{10,... | collective-permute-start | bytes 36872 | tf_op jit(solution)/shard_map/ppermute | solution.py:34
  47.9 1.2 collective-permute-start.16
  51.4 7.3 %collective-permute-start.17 = (bf16[2816,256]{1,0:T(8,128)(2,1)S(1)}, bf16[2816,256]{1,0:T(8,128)(2,1)S(1)}, u32[]{:S(2)}, u32[]{:S(2)}) collective-permute-start(bf16[2816,256]{1,0:T(8,128)(2,1)S(1)} %get-tuple-element.114), channel_id=1, source_target_pairs={{0,1},{1,0},{2,3},{3,2},{4,5},{5,4},{6,7},{7,6},{8,9},{9,8},{10,11... | collective-permute-start | bytes 4325384 | tf_op jit(solution)/shard_map/ppermute | solution.py:34
  51.6 5.4 %collective-permute-start.20 = (f32[8,128]{1,0:T(8,128)S(1)}, f32[8,128]{1,0:T(8,128)S(1)}, u32[]{:S(2)}, u32[]{:S(2)}) collective-permute-start(f32[8,128]{1,0:T(8,128)S(1)} %add.22.refs_11_.refs_0_), channel_id=1, source_target_pairs={{0,6},{1,7},{2,4},{3,5},{4,2},{5,3},{6,0},{7,1},{8,14},{9,15},{10,... | collective-permute-start | bytes 12296 | tf_op jit(solution)/shard_map/ppermute | solution.py:34
  54.1 4.5 %collective-permute-start.19 = (f32[8,128]{1,0:T(8,128)S(1)}, f32[8,128]{1,0:T(8,128)S(1)}, u32[]{:S(2)}, u32[]{:S(2)}) collective-permute-start(f32[8,128]{1,0:T(8,128)S(1)} %add.22.refs_11_.refs_0_), channel_id=1, source_target_pairs={{0,4},{1,5},{2,6},{3,7},{4,0},{5,1},{6,2},{7,3},{8,12},{9,13},{10,... | collective-permute-start | bytes 12296 | tf_op jit(solution)/shard_map/ppermute | solution.py:34
  55.1 3.6 %collective-permute-start.18 = (f32[8,128]{1,0:T(8,128)S(1)}, f32[8,128]{1,0:T(8,128)S(1)}, u32[]{:S(2)}, u32[]{:S(2)}) collective-permute-start(f32[8,128]{1,0:T(8,128)S(1)} %add.22.refs_11_.refs_0_), channel_id=1, source_target_pairs={{0,2},{1,3},{2,0},{3,1},{4,6},{5,7},{6,4},{7,5},{8,10},{9,11},{10,... | collective-permute-start | bytes 12296 | tf_op jit(solution)/shard_map/ppermute | solution.py:34
  59.1 11.4 %collective-permute-start.21 = (bf16[1408,256]{1,0:T(8,128)(2,1)S(1)}, bf16[1408,256]{1,0:T(8,128)(2,1)S(1)}, u32[]{:S(2)}, u32[]{:S(2)}) collective-permute-start(bf16[1408,256]{1,0:T(8,128)(2,1)S(1)} %get-tuple-element.116), channel_id=1, source_target_pairs={{0,8},{1,17},{2,10},{3,19},{4,12},{5,21},{6,14},{7,23},{8,0},{9,25... | collective-permute-start | bytes 2162696 | tf_op jit(solution)/shard_map/ppermute | solution.py:585
  62.0 1.2 collective-permute-start.22
  63.2 7.4 %collective-permute-start.26 = (f32[8,128]{1,0:T(8,128)S(1)}, f32[8,128]{1,0:T(8,128)S(1)}, u32[]{:S(2)}, u32[]{:S(2)}) collective-permute-start(f32[8,128]{1,0:T(8,128)S(1)} %add.23.refs_3_.refs_0_), channel_id=1, source_target_pairs={{0,6},{1,7},{2,4},{3,5},{4,2},{5,3},{6,0},{7,1},{8,14},{9,15},{10,... | collective-permute-start | bytes 12296 | tf_op jit(solution)/shard_map/ppermute | solution.py:34
  64.6 6.1 %collective-permute-start.25 = (f32[8,128]{1,0:T(8,128)S(1)}, f32[8,128]{1,0:T(8,128)S(1)}, u32[]{:S(2)}, u32[]{:S(2)}) collective-permute-start(f32[8,128]{1,0:T(8,128)S(1)} %add.23.refs_3_.refs_0_), channel_id=1, source_target_pairs={{0,4},{1,5},{2,6},{3,7},{4,0},{5,1},{6,2},{7,3},{8,12},{9,13},{10,... | collective-permute-start | bytes 12296 | tf_op jit(solution)/shard_map/ppermute | solution.py:34
  65.6 5.1 %collective-permute-start.24 = (f32[8,128]{1,0:T(8,128)S(1)}, f32[8,128]{1,0:T(8,128)S(1)}, u32[]{:S(2)}, u32[]{:S(2)}) collective-permute-start(f32[8,128]{1,0:T(8,128)S(1)} %add.23.refs_3_.refs_0_), channel_id=1, source_target_pairs={{0,2},{1,3},{2,0},{3,1},{4,6},{5,7},{6,4},{7,5},{8,10},{9,11},{10,... | collective-permute-start | bytes 12296 | tf_op jit(solution)/shard_map/ppermute | solution.py:34
  71.7 6.3 %copy-start.6 = (bf16[1024,256]{1,0:T(8,128)(2,1)S(1)}, bf16[1024,256]{1,0:T(8,128)(2,1)}, u32[]{:S(2)}) copy-start(bf16[1024,256]{1,0:T(8,128)(2,1)} %refs_4_.3) | copy-start | bytes 1572868
  71.7 2.5 %collective-permute-start.27 = (bf16[1792,256]{1,0:T(8,128)(2,1)S(1)}, bf16[1792,256]{1,0:T(8,128)(2,1)S(1)}, u32[]{:S(2)}, u32[]{:S(2)}) collective-permute-start(bf16[1792,256]{1,0:T(8,128)(2,1)S(1)} %get-tuple-element.131), channel_id=1, source_target_pairs={{0,1},{1,0},{2,3},{3,2},{4,5},{5,4},{6,7},{7,6},{8,9},{9,8},{10,11... | collective-permute-start | bytes 2752520 | tf_op jit(solution)/shard_map/ppermute | solution.py:34
  71.8 10.2 %collective-permute-start.23 = (bf16[704,256]{1,0:T(8,128)(2,1)S(1)}, bf16[704,256]{1,0:T(8,128)(2,1)S(1)}, u32[]{:S(2)}, u32[]{:S(2)}) collective-permute-start(bf16[704,256]{1,0:T(8,128)(2,1)S(1)} %get-tuple-element.124), channel_id=1, source_target_pairs={{0,16},{1,9},{2,18},{3,11},{4,20},{5,13},{6,22},{7,15},{8,24},{9,1... | collective-permute-start | bytes 1081352 | tf_op jit(solution)/shard_map/ppermute | solution.py:585
  74.4 9.7 %collective-permute-start.31 = (bf16[448,256]{1,0:T(8,128)(2,1)S(1)}, bf16[448,256]{1,0:T(8,128)(2,1)S(1)}, u32[]{:S(2)}, u32[]{:S(2)}) collective-permute-start(bf16[448,256]{1,0:T(8,128)(2,1)S(1)} %get-tuple-element.139), channel_id=1, source_target_pairs={{0,8},{1,9},{2,10},{3,11},{4,12},{5,13},{6,14},{7,15},{8,0},{9,1},... | collective-permute-start | bytes 688136 | tf_op jit(solution)/shard_map/ppermute | solution.py:585
  76.0 12.2 %collective-permute-start.32 = (bf16[448,256]{1,0:T(8,128)(2,1)S(1)}, bf16[448,256]{1,0:T(8,128)(2,1)S(1)}, u32[]{:S(2)}, u32[]{:S(2)}) collective-permute-start(bf16[448,256]{1,0:T(8,128)(2,1)S(1)} %get-tuple-element.140), channel_id=1, source_target_pairs={{0,16},{1,17},{2,18},{3,19},{4,20},{5,21},{6,22},{7,23},{8,24},{9,... | collective-permute-start | bytes 688136 | tf_op jit(solution)/shard_map/ppermute | solution.py:585
  77.5 11.4 %collective-permute-start.33 = (bf16[448,256]{1,0:T(8,128)(2,1)S(1)}, bf16[448,256]{1,0:T(8,128)(2,1)S(1)}, u32[]{:S(2)}, u32[]{:S(2)}) collective-permute-start(bf16[448,256]{1,0:T(8,128)(2,1)S(1)} %get-tuple-element.141), channel_id=1, source_target_pairs={{0,24},{1,25},{2,26},{3,27},{4,28},{5,29},{6,30},{7,31},{8,16},{9,... | collective-permute-start | bytes 688136 | tf_op jit(solution)/shard_map/ppermute | solution.py:585
  78.0 2.1 %copy-start.5 = (bf16[3,3,256,256]{3,2,1,0:T(8,128)(2,1)S(1)}, bf16[3,3,256,256]{3,2,1,0:T(8,128)(2,1)}, u32[]{:S(2)}) copy-start(bf16[3,3,256,256]{3,2,1,0:T(8,128)(2,1)} %refs_3_.3) | copy-start | bytes 3538948
  82.1 7.0 %collective-permute-start.28 = (bf16[176,256]{1,0:T(8,128)(2,1)S(1)}, bf16[176,256]{1,0:T(8,128)(2,1)S(1)}, u32[]{:S(2)}, u32[]{:S(2)}) collective-permute-start(bf16[176,256]{1,0:T(8,128)(2,1)S(1)} %get-tuple-element.136), channel_id=1, source_target_pairs={{0,2},{1,3},{2,0},{3,1},{4,6},{5,7},{6,4},{7,5},{8,10},{9,11},{10,... | collective-permute-start | bytes 270344 | tf_op jit(solution)/shard_map/ppermute | solution.py:585
  83.0 9.3 %collective-permute-start.29 = (bf16[176,256]{1,0:T(8,128)(2,1)S(1)}, bf16[176,256]{1,0:T(8,128)(2,1)S(1)}, u32[]{:S(2)}, u32[]{:S(2)}) collective-permute-start(bf16[176,256]{1,0:T(8,128)(2,1)S(1)} %get-tuple-element.137), channel_id=1, source_target_pairs={{0,4},{1,5},{2,6},{3,7},{4,0},{5,1},{6,2},{7,3},{8,12},{9,13},{10,... | collective-permute-start | bytes 270344 | tf_op jit(solution)/shard_map/ppermute | solution.py:585
  84.1 8.2 %collective-permute-start.30 = (bf16[176,256]{1,0:T(8,128)(2,1)S(1)}, bf16[176,256]{1,0:T(8,128)(2,1)S(1)}, u32[]{:S(2)}, u32[]{:S(2)}) collective-permute-start(bf16[176,256]{1,0:T(8,128)(2,1)S(1)} %get-tuple-element.138), channel_id=1, source_target_pairs={{0,6},{1,7},{2,4},{3,5},{4,2},{5,3},{6,0},{7,1},{8,14},{9,15},{10,... | collective-permute-start | bytes 270344 | tf_op jit(solution)/shard_map/ppermute | solution.py:585
  92.4 7.3 %collective-permute-start.36 = (bf16[176,256]{1,0:T(8,128)(2,1)S(1)}, bf16[176,256]{1,0:T(8,128)(2,1)S(1)}, u32[]{:S(2)}, u32[]{:S(2)}) collective-permute-start(bf16[176,256]{1,0:T(8,128)(2,1)S(1)} %shard_map.271.refs_0_.refs_4_), channel_id=1, source_target_pairs={{0,6},{1,7},{2,4},{3,5},{4,2},{5,3},{6,0},{7,1},{8,14},{9,15},{10,... | collective-permute-start | bytes 270344 | tf_op jit(solution)/shard_map/ppermute | solution.py:585
  94.7 7.7 %collective-permute-start.35 = (bf16[176,256]{1,0:T(8,128)(2,1)S(1)}, bf16[176,256]{1,0:T(8,128)(2,1)S(1)}, u32[]{:S(2)}, u32[]{:S(2)}) collective-permute-start(bf16[176,256]{1,0:T(8,128)(2,1)S(1)} %shard_map.271.refs_0_.refs_4_), channel_id=1, source_target_pairs={{0,4},{1,5},{2,6},{3,7},{4,0},{5,1},{6,2},{7,3},{8,12},{9,13},{10,... | collective-permute-start | bytes 270344 | tf_op jit(solution)/shard_map/ppermute | solution.py:585
  95.4 7.1 %collective-permute-start.34 = (bf16[176,256]{1,0:T(8,128)(2,1)S(1)}, bf16[176,256]{1,0:T(8,128)(2,1)S(1)}, u32[]{:S(2)}, u32[]{:S(2)}) collective-permute-start(bf16[176,256]{1,0:T(8,128)(2,1)S(1)} %shard_map.271.refs_0_.refs_4_), channel_id=1, source_target_pairs={{0,2},{1,3},{2,0},{3,1},{4,6},{5,7},{6,4},{7,5},{8,10},{9,11},{10,... | collective-permute-start | bytes 270344 | tf_op jit(solution)/shard_map/ppermute | solution.py:585
  102.5 9.6 %collective-permute-start.37 = (bf16[704,256]{1,0:T(8,128)(2,1)S(1)}, bf16[704,256]{1,0:T(8,128)(2,1)S(1)}, u32[]{:S(2)}, u32[]{:S(2)}) collective-permute-start(bf16[704,256]{1,0:T(8,128)(2,1)S(1)} %bitcast.80), channel_id=1, source_target_pairs={{0,16},{1,9},{2,18},{3,11},{4,20},{5,13},{6,22},{7,15},{8,24},{9,1... | collective-permute-start | bytes 1081352 | tf_op jit(solution)/shard_map/ppermute | solution.py:585
  104.1 4.4 %collective-permute-start.38 = (bf16[112,256]{1,0:T(8,128)(2,1)S(1)}, bf16[112,256]{1,0:T(8,128)(2,1)S(1)}, u32[]{:S(2)}, u32[]{:S(2)}) collective-permute-start(bf16[112,256]{1,0:T(8,128)(2,1)S(1)} %get-tuple-element.143), channel_id=1, source_target_pairs={{0,2},{1,3},{2,0},{3,1},{4,6},{5,7},{6,4},{7,5},{8,10},{9,11},{10,... | collective-permute-start | bytes 172040 | tf_op jit(solution)/shard_map/ppermute | solution.py:585
  104.1 5.4 %collective-permute-start.39 = (bf16[112,256]{1,0:T(8,128)(2,1)S(1)}, bf16[112,256]{1,0:T(8,128)(2,1)S(1)}, u32[]{:S(2)}, u32[]{:S(2)}) collective-permute-start(bf16[112,256]{1,0:T(8,128)(2,1)S(1)} %get-tuple-element.144), channel_id=1, source_target_pairs={{0,4},{1,5},{2,6},{3,7},{4,0},{5,1},{6,2},{7,3},{8,12},{9,13},{10,... | collective-permute-start | bytes 172040 | tf_op jit(solution)/shard_map/ppermute | solution.py:585
  106.0 6.0 %collective-permute-start.40 = (bf16[112,256]{1,0:T(8,128)(2,1)S(1)}, bf16[112,256]{1,0:T(8,128)(2,1)S(1)}, u32[]{:S(2)}, u32[]{:S(2)}) collective-permute-start(bf16[112,256]{1,0:T(8,128)(2,1)S(1)} %get-tuple-element.145), channel_id=1, source_target_pairs={{0,6},{1,7},{2,4},{3,5},{4,2},{5,3},{6,0},{7,1},{8,14},{9,15},{10,... | collective-permute-start | bytes 172040 | tf_op jit(solution)/shard_map/ppermute | solution.py:585
  112.2 11.4 %collective-permute-start.47 = (bf16[1408,256]{1,0:T(8,128)(2,1)S(1)}, bf16[1408,256]{1,0:T(8,128)(2,1)S(1)}, u32[]{:S(2)}, u32[]{:S(2)}) collective-permute-start(bf16[1408,256]{1,0:T(8,128)(2,1)S(1)} %bitcast.67), channel_id=1, source_target_pairs={{0,8},{1,17},{2,10},{3,19},{4,12},{5,21},{6,14},{7,23},{8,0},{9,25... | collective-permute-start | bytes 2162696 | tf_op jit(solution)/shard_map/ppermute | solution.py:585
  113.8 8.3 %collective-permute-start.43 = (bf16[112,256]{1,0:T(8,128)(2,1)S(1)}, bf16[112,256]{1,0:T(8,128)(2,1)S(1)}, u32[]{:S(2)}, u32[]{:S(2)}) collective-permute-start(bf16[112,256]{1,0:T(8,128)(2,1)S(1)} %shard_map.273.refs_2_.refs_0_), channel_id=1, source_target_pairs={{0,6},{1,7},{2,4},{3,5},{4,2},{5,3},{6,0},{7,1},{8,14},{9,15},{10,... | collective-permute-start | bytes 172040 | tf_op jit(solution)/shard_map/ppermute | solution.py:585
  116.1 6.0 %collective-permute-start.42 = (bf16[112,256]{1,0:T(8,128)(2,1)S(1)}, bf16[112,256]{1,0:T(8,128)(2,1)S(1)}, u32[]{:S(2)}, u32[]{:S(2)}) collective-permute-start(bf16[112,256]{1,0:T(8,128)(2,1)S(1)} %shard_map.273.refs_2_.refs_0_), channel_id=1, source_target_pairs={{0,4},{1,5},{2,6},{3,7},{4,0},{5,1},{6,2},{7,3},{8,12},{9,13},{10,... | collective-permute-start | bytes 172040 | tf_op jit(solution)/shard_map/ppermute | solution.py:585
  116.2 6.0 %collective-permute-start.41 = (bf16[112,256]{1,0:T(8,128)(2,1)S(1)}, bf16[112,256]{1,0:T(8,128)(2,1)S(1)}, u32[]{:S(2)}, u32[]{:S(2)}) collective-permute-start(bf16[112,256]{1,0:T(8,128)(2,1)S(1)} %shard_map.273.refs_2_.refs_0_), channel_id=1, source_target_pairs={{0,2},{1,3},{2,0},{3,1},{4,6},{5,7},{6,4},{7,5},{8,10},{9,11},{10,... | collective-permute-start | bytes 172040 | tf_op jit(solution)/shard_map/ppermute | solution.py:585
  123.6 3.6 %collective-permute-start.48 = (bf16[2816,256]{1,0:T(8,128)(2,1)S(1)}, bf16[2816,256]{1,0:T(8,128)(2,1)S(1)}, u32[]{:S(2)}, u32[]{:S(2)}) collective-permute-start(bf16[2816,256]{1,0:T(8,128)(2,1)S(1)} %bitcast.76), channel_id=1, source_target_pairs={{0,1},{1,0},{2,3},{3,2},{4,5},{5,4},{6,7},{7,6},{8,9},{9,8},{10,11... | collective-permute-start | bytes 4325384 | tf_op jit(solution)/shard_map/ppermute | solution.py:34
  123.7 9.4 %collective-permute-start.46 = (bf16[448,256]{1,0:T(8,128)(2,1)S(1)}, bf16[448,256]{1,0:T(8,128)(2,1)S(1)}, u32[]{:S(2)}, u32[]{:S(2)}) collective-permute-start(bf16[448,256]{1,0:T(8,128)(2,1)S(1)} %bitcast.85), channel_id=1, source_target_pairs={{0,24},{1,25},{2,26},{3,27},{4,28},{5,29},{6,30},{7,31},{8,16},{9,... | collective-permute-start | bytes 688136 | tf_op jit(solution)/shard_map/ppermute | solution.py:585
  125.3 12.3 %collective-permute-start.45 = (bf16[448,256]{1,0:T(8,128)(2,1)S(1)}, bf16[448,256]{1,0:T(8,128)(2,1)S(1)}, u32[]{:S(2)}, u32[]{:S(2)}) collective-permute-start(bf16[448,256]{1,0:T(8,128)(2,1)S(1)} %bitcast.86), channel_id=1, source_target_pairs={{0,16},{1,17},{2,18},{3,19},{4,20},{5,21},{6,22},{7,23},{8,24},{9,... | collective-permute-start | bytes 688136 | tf_op jit(solution)/shard_map/ppermute | solution.py:585
  126.8 10.7 %collective-permute-start.44 = (bf16[448,256]{1,0:T(8,128)(2,1)S(1)}, bf16[448,256]{1,0:T(8,128)(2,1)S(1)}, u32[]{:S(2)}, u32[]{:S(2)}) collective-permute-start(bf16[448,256]{1,0:T(8,128)(2,1)S(1)} %bitcast.87), channel_id=1, source_target_pairs={{0,8},{1,9},{2,10},{3,11},{4,12},{5,13},{6,14},{7,15},{8,0},{9,1},... | collective-permute-start | bytes 688136 | tf_op jit(solution)/shard_map/ppermute | solution.py:585
  137.6 2.5 %collective-permute-start.49 = (bf16[1792,256]{1,0:T(8,128)(2,1)S(1)}, bf16[1792,256]{1,0:T(8,128)(2,1)S(1)}, u32[]{:S(2)}, u32[]{:S(2)}) collective-permute-start(bf16[1792,256]{1,0:T(8,128)(2,1)S(1)} %bitcast.78), channel_id=1, source_target_pairs={{0,1},{1,0},{2,3},{3,2},{4,5},{5,4},{6,7},{7,6},{8,9},{9,8},{10,11... | collective-permute-start | bytes 2752520 | tf_op jit(solution)/shard_map/ppermute | solution.py:34

commit v3 on v2

--- a/solution.py
+++ b/solution.py
@@ -619,31 +619,6 @@
     return [phase(stride, radix) for stride, radix in factors(lax.axis_size("clip"))[0][1:]]
 
 
-def over_clip_halves():
-    def digit(stride, swapped):
-        first = jnp.bitwise_xor(core_here(), swapped) == 0
-        place = lax.axis_index("clip") // stride
-        return jnp.where(first, lax.rem(place, 2), lax.rem(place // 2, 2))
-
-    def partner(stride, swapped, s, c, k):
-        return s, c ^ (stride * (k if (c % 2) ^ swapped == 0 else 2 * k))
-
-    phases = []
-    for step, (stride, radix) in zip(over_clip(), factors(lax.axis_size("clip"))[0][1:]):
-        if radix != 4:
-            phases.append(step)
-            continue
-        for swapped in (0, 1):
-            phases.append(
-                Phase(
-                    2,
-                    functools.partial(digit, stride, swapped),
-                    functools.partial(partner, stride, swapped),
-                )
-            )
-    return phases
-
-
 class GradSum:
     def __init__(self, kept, sent, phases):
         self.phases = phases
@@ -691,10 +666,13 @@
         return call(functools.partial(kernel_finish, kinds), outs, *self.parts, token=token)
 
 
-FIRST_PHASES = (over_section_halves, over_clip)
-SECOND_PHASES = (over_section, over_clip)
-EARLY = 1
-ORDER = ('Ts0', 'I', 'M', 'Fs2', 'Ts1', 'Ft', 'Fg2', 'Tt', 'Fg1', 'O', 'Tg1', 'Fg0', 'X', 'Tg0')
+def order_of(early, clips):
+    order = ["Ts0", "I", "M"]
+    order += [f"Fs{early + k}" for k in range(clips)] + [f"Ts{1 + k}" for k in range(clips)]
+    order += ["Ft"] + [f"Fg{early + k}" for k in reversed(range(clips))]
+    order += ["Tt"] + [f"Tg{k}" for k in reversed(range(2, clips + 1))]
+    order += [f"Fg{k}" for k in reversed(range(1, early))]
+    return order + ["O", "Tg1", "Fg0", "X", "Tg0"]
 
 
 def per_device(
@@ -806,7 +784,7 @@
         after=parts[:1],
         alias=[(9, 2), (10, 3)],
     )
-    first_set = GradSum(kept, sent, FIRST_PHASES[0]() + FIRST_PHASES[1]())
+    first_set = GradSum(kept, sent, over_section_halves() + over_clip())
     first_scattered = first_set.scatter(0, after=parts[1:])
     total_5, upr, same_s, edge_s, sums = call(
         bound(kernel_6),
@@ -826,7 +804,8 @@
         after=parts[:1],
     )
     last = kept
-    for k in range(1, EARLY + 1):
+    early = len(over_section_halves())
+    for k in range(1, early):
         last = first_set.scatter(k, after=[last])
     back_r, kept, sent = call(
         kernel_7,
@@ -836,7 +815,7 @@
         after=[last],
         alias=[(len(parts) + 10, 1), (len(parts) + 11, 2)],
     )
-    second_set = GradSum(kept, sent, SECOND_PHASES[0]() + SECOND_PHASES[1]())
+    second_set = GradSum(kept, sent, over_section() + over_clip())
 
     taps = like((9, narrow, narrow), F32)
     made = {}
@@ -871,7 +850,7 @@
         return token
 
     last = kept
-    for step in ORDER:
+    for step in order_of(early, len(over_clip())):
         if step == "I":
             last = iframe([last])
         elif step == "M":
@@ -882,13 +861,12 @@
             last = finish([last])
         else:
             own = first_set if step[0] == "F" else second_set
-            after = [last] if len(step) < 4 else []
             if step[1] == "t":
-                last = own.total(after)
+                last = own.total([last])
             elif step[1] == "s":
-                last = own.scatter(int(step[2]), after)
+                last = own.scatter(int(step[2:]), [last])
             else:
-                last = own.gather(int(step[2]), after)
+                last = own.gather(int(step[2:]), [last])
     iframe_back, motion_back = made["iframe"], made["motion"]
     iframe_out, motion_out = made["outputs"]
     grad_second, grad_first, grad_expand = made["first"]

time: 142 us -> 142 us (level)
  no operation moved by 1% of the time
where the time goes in v3:
time: 142 us
  starting transfers between devices  59.9 us (42%)
  waiting for transfers between devices  46.4 us (33%)
  Pallas kernels  34.7 us (24%)
    pallas_call x27, Pallas kernels, call(): pl.pallas_call(body, out_shape=outs, in_specs=[pl.BlockSpec(memory_space=...  34.7 us
    ppermute x22, starting transfers between devices, send(): return lax.ppermute(value, ('section', 'clip'), route)  31.1 us
    ppermute x28, starting transfers between devices, swap(): return lax.ppermute(value, axis, [(i, i ^ mask) for i in range(size)])  28.8 us
    ppermute x22, waiting for transfers between devices, send(): return lax.ppermute(value, ('section', 'clip'), route)  25.1 us
    ppermute x28, waiting for transfers between devices, swap(): return lax.ppermute(value, axis, [(i, i ^ mask) for i in range(size)])  21.3 us
  transfers between devices with their start and end apart: 50, of which 31 were waited for; matrix products, arithmetic and copies ran while one was open for 0% of the time, Pallas kernels for 11%

profile of v3, /device:TPU:0, one launch (start us, length us, event | category | flops | bytes accessed | tf_op | source)
XLA Modules:
  0.0 142.2 jit_solution(10376777587296080672)
XLA Ops:
  0.7 4.2 %shard_map.254 = (f32[8,256]{1,0:T(8,128)S(1)}, f32[784,256]{1,0:T(8,128)S(1)}, f32[784,256]{1,0:T(8,128)S(1)}, f32[16,128]{1,0:T(8,128)S(1)}) custom-call(s32[4,4]{1,0:T(4,128)} %refs_0_.1, bf16[196,4,1024]{2,1,0:T(4,128)(2,1)} %bitcast.61, bf16[196,4,256]{2,1,0:T(4,128)(2,1)} %bitcast.72, bf16[1024,256]{1,0:T(8,128)(2,1)} %refs_4_.3, ...), custom_call_target="tpu_custom_call" | custom-call | flops 1024 | bytes 1024 | tf_op jit(solution)/shard_map/pallas_call | solution.py:557
  6.2 4.9 %collective-permute-start.3 = (f32[16,128]{1,0:T(8,128)S(1)}, f32[16,128]{1,0:T(8,128)S(1)}, u32[]{:S(2)}, u32[]{:S(2)}) collective-permute-start(f32[16,128]{1,0:T(8,128)S(1)} %add.18.refs_0_), channel_id=1, source_target_pairs={{0,6},{1,7},{2,4},{3,5},{4,2},{5,3},{6,0},{7,1},{8,14},{9,15},{10,... | collective-permute-start | bytes 24584 | tf_op jit(solution)/shard_map/ppermute | solution.py:34
  11.8 1.1 collective-permute-done.3.refs_3_
  12.8 2.9 %collective-permute-done.2.refs_2_ = f32[16,128]{1,0:T(8,128)S(1)} collective-permute-done((f32[16,128]{1,0:T(8,128)S(1)}, f32[16,128]{1,0:T(8,128)S(1)}, u32[]{:S(2)}, u32[]{:S(2)}) %collective-permute-start.2) | collective-permute-done | bytes 8224 | tf_op jit(solution)/shard_map/ppermute | solution.py:34
  15.8 2.4 %shard_map.255 = (f32[16,128]{1,0:T(8,128)S(1)}, bf16[784,256]{1,0:T(8,128)(2,1)S(1)}, bf16[784,256]{1,0:T(8,128)(2,1)S(1)}, f32[784,256]{1,0:T(8,128)S(1)}, f32...) custom-call(f32[16,128]{1,0:T(8,128)S(1)} %add.18.refs_0_, f32[16,128]{1,0:T(8,128)S(1)} %collective-permute-done.1.refs_1_, ...), custom_call_target="tpu_custom_call" | custom-call | flops 1024 | bytes 1024 | tf_op jit(solution)/shard_map/pallas_call | solution.py:557
  18.3 1.2 collective-permute-done.4
  19.5 1.5 %collective-permute-start.7 = (f32[8,128]{1,0:T(8,128)S(1)}, f32[8,128]{1,0:T(8,128)S(1)}, u32[]{:S(2)}, u32[]{:S(2)}) collective-permute-start(f32[8,128]{1,0:T(8,128)S(1)} %add.19.refs_0_), channel_id=1, source_target_pairs={{0,6},{1,7},{2,4},{3,5},{4,2},{5,3},{6,0},{7,1},{8,14},{9,15},{10,... | collective-permute-start | bytes 12296 | tf_op jit(solution)/shard_map/ppermute | solution.py:34
  21.5 2.4 %collective-permute-start.5 = (f32[8,128]{1,0:T(8,128)S(1)}, f32[8,128]{1,0:T(8,128)S(1)}, u32[]{:S(2)}, u32[]{:S(2)}) collective-permute-start(f32[8,128]{1,0:T(8,128)S(1)} %add.19.refs_0_), channel_id=1, source_target_pairs={{0,2},{1,3},{2,0},{3,1},{4,6},{5,7},{6,4},{7,5},{8,10},{9,11},{10,... | collective-permute-start | bytes 12296 | tf_op jit(solution)/shard_map/ppermute | solution.py:34
  23.9 1.0 collective-permute-done.7.refs_3_
  25.5 1.7 %shard_map.256 = (f32[8,128]{1,0:T(8,128)S(1)}, bf16[784,256]{1,0:T(8,128)(2,1)S(1)}, f32[784,1024]{1,0:T(8,128)S(1)}, f32[784,256]{1,0:T(8,128)S(1)}, f32[24,128]{1,0:T(8,128)S(1)}) custom-call(f32[8,128]{1,0:T(8,128)S(1)} %add.19.refs_0_, f32[8,128]{1,0:T(8,128)S(1)} %collective-permute-done.5.refs_1_, f32[8,128]{1,0:T(8,128)S(1)} %collective-permute-done.6.refs_2_, ...), custom_call_target="tpu_custom_call" | custom-call | flops 1024 | bytes 1024 | tf_op jit(solution)/shard_map/pallas_call | solution.py:557
  27.4 1.2 collective-permute-done.8
  28.5 2.5 %collective-permute-start.11 = (f32[24,128]{1,0:T(8,128)S(1)}, f32[24,128]{1,0:T(8,128)S(1)}, u32[]{:S(2)}, u32[]{:S(2)}) collective-permute-start(f32[24,128]{1,0:T(8,128)S(1)} %add.20.refs_0_), channel_id=1, source_target_pairs={{0,6},{1,7},{2,4},{3,5},{4,2},{5,3},{6,0},{7,1},{8,14},{9,15},{10,... | collective-permute-start | bytes 36872 | tf_op jit(solution)/shard_map/ppermute | solution.py:34
  32.9 1.2 collective-permute-done.11.refs_3_
  34.2 1.5 %collective-permute-done.10.refs_2_ = f32[24,128]{1,0:T(8,128)S(1)} collective-permute-done((f32[24,128]{1,0:T(8,128)S(1)}, f32[24,128]{1,0:T(8,128)S(1)}, u32[]{:S(2)}, u32[]{:S(2)}) %collective-permute-start.10) | collective-permute-done | bytes 12320 | tf_op jit(solution)/shard_map/ppermute | solution.py:34
  35.8 3.3 %shard_map.257 = (f32[24,128]{1,0:T(8,128)S(1)}, f32[784,1024]{1,0:T(8,128)S(1)}, f32[784,256]{1,0:T(8,128)S(1)}, bf16[784,768]{1,0:T(8,128)(2,1)S(1)}, bf16[896...) custom-call(f32[24,128]{1,0:T(8,128)S(1)} %add.20.refs_0_, f32[24,128]{1,0:T(8,128)S(1)} %collective-permute-done.9.refs_1_, ...), custom_call_target="tpu_custom_call" | custom-call | flops 1024 | bytes 1024 | tf_op jit(solution)/shard_map/pallas_call | solution.py:557
  39.2 1.2 collective-permute-done.12
  40.4 1.3 collective-permute-start.15
  42.7 2.1 %collective-permute-start.13 = (f32[24,128]{1,0:T(8,128)S(1)}, f32[24,128]{1,0:T(8,128)S(1)}, u32[]{:S(2)}, u32[]{:S(2)}) collective-permute-start(f32[24,128]{1,0:T(8,128)S(1)} %add.21.refs_3_.refs_0_), channel_id=1, source_target_pairs={{0,2},{1,3},{2,0},{3,1},{4,6},{5,7},{6,4},{7,5},{8,10},{9,11},{10,... | collective-permute-start | bytes 36872 | tf_op jit(solution)/shard_map/ppermute | solution.py:34
  44.8 1.4 %shard_map.258 = (bf16[2816,256]{1,0:T(8,128)(2,1)S(1)}, bf16[2816,256]{1,0:T(8,128)(2,1)S(1)}) custom-call(bf16[784,256]{1,0:T(8,128)(2,1)S(1)} %get-tuple-element.103.refs_0_, bf16[784,768]{1,0:T(8,128)(2,1)S(1)} %get-tuple-element.104.refs_1_, bf16[896,768]{1,0:T(8,128)(2,1)S(1)} %get-tuple-element.105.refs_2_, f32[24,128]{1,0:T(8,128)S(1)} %add.21.refs_3_.refs_0_), custom_call_target="tpu_custom_call" | custom-call | flops 1024 | bytes 1024 | tf_op jit(solution)/shard_map/pallas_call | solution.py:557
  46.5 1.4 shard_map.259
  47.9 1.2 collective-permute-done.16
  49.1 2.3 %shard_map.260 = (bf16[784,768]{1,0:T(8,128)(2,1)S(1)}, bf16[896,768]{1,0:T(8,128)(2,1)S(1)}, bf16[2816,256]{1,0:T(8,128)(2,1)S(1)}, bf16[2816,256]{1,0:T(8,128)(2,1)S(1)}) custom-call(f32[8,256]{1,0:T(8,128)S(1)} %get-tuple-element.88.refs_4_.refs_0_, ...), custom_call_target="tpu_custom_call", output_to_operand_aliasing={{2}: (9, {}), {3}: (10, {})} | custom-call | flops 1024 | bytes 1024 | tf_op jit(solution)/shard_map/pallas_call | solution.py:557
  51.6 2.5 %collective-permute-start.20 = (f32[8,128]{1,0:T(8,128)S(1)}, f32[8,128]{1,0:T(8,128)S(1)}, u32[]{:S(2)}, u32[]{:S(2)}) collective-permute-start(f32[8,128]{1,0:T(8,128)S(1)} %add.22.refs_11_.refs_0_), channel_id=1, source_target_pairs={{0,6},{1,7},{2,4},{3,5},{4,2},{5,3},{6,0},{7,1},{8,14},{9,15},{10,... | collective-permute-start | bytes 12296 | tf_op jit(solution)/shard_map/ppermute | solution.py:34
  54.1 1.0 collective-permute-start.19
  56.0 1.0 collective-permute-done.20.refs_4_.refs_3_
  57.0 1.6 %collective-permute-done.19.refs_3_.refs_2_ = f32[8,128]{1,0:T(8,128)S(1)} collective-permute-done((f32[8,128]{1,0:T(8,128)S(1)}, f32[8,128]{1,0:T(8,128)S(1)}, u32[]{:S(2)}, u32[]{:S(2)}) %collective-permute-start.19) | collective-permute-done | bytes 4128 | tf_op jit(solution)/shard_map/ppermute | solution.py:34
  59.1 1.6 %collective-permute-start.21 = (bf16[1408,256]{1,0:T(8,128)(2,1)S(1)}, bf16[1408,256]{1,0:T(8,128)(2,1)S(1)}, u32[]{:S(2)}, u32[]{:S(2)}) collective-permute-start(bf16[1408,256]{1,0:T(8,128)(2,1)S(1)} %get-tuple-element.116), channel_id=1, source_target_pairs={{0,8},{1,17},{2,10},{3,19},{4,12},{5,21},{6,14},{7,23},{8,0},{9,25... | collective-permute-start | bytes 2162696 | tf_op jit(solution)/shard_map/ppermute | solution.py:585
  60.7 1.3 shard_map.262
  62.1 1.2 collective-permute-done.22
  63.2 1.4 collective-permute-start.26
  64.6 1.0 collective-permute-start.25
  65.6 2.0 %collective-permute-start.24 = (f32[8,128]{1,0:T(8,128)S(1)}, f32[8,128]{1,0:T(8,128)S(1)}, u32[]{:S(2)}, u32[]{:S(2)}) collective-permute-start(f32[8,128]{1,0:T(8,128)S(1)} %add.23.refs_3_.refs_0_), channel_id=1, source_target_pairs={{0,2},{1,3},{2,0},{3,1},{4,6},{5,7},{6,4},{7,5},{8,10},{9,11},{10,... | collective-permute-start | bytes 12296 | tf_op jit(solution)/shard_map/ppermute | solution.py:34
  67.6 1.4 %shard_map.263 = (bf16[1792,256]{1,0:T(8,128)(2,1)S(1)}, bf16[1792,256]{1,0:T(8,128)(2,1)S(1)}) custom-call(bf16[784,256]{1,0:T(8,128)(2,1)S(1)} %get-tuple-element.117.refs_0_, bf16[784,768]{1,0:T(8,128)(2,1)S(1)} %get-tuple-element.119.refs_1_, bf16[896,768]{1,0:T(8,128)(2,1)S(1)} %get-tuple-element.120.refs_2_, f32[8,128]{1,0:T(8,128)S(1)} %add.23.refs_3_.refs_0_), custom_call_target="tpu_custom_call" | custom-call | flops 1024 | bytes 1024 | tf_op jit(solution)/shard_map/pallas_call | solution.py:557
  69.0 1.4 collective-permute-done.21
  71.8 1.6 %collective-permute-start.23 = (bf16[704,256]{1,0:T(8,128)(2,1)S(1)}, bf16[704,256]{1,0:T(8,128)(2,1)S(1)}, u32[]{:S(2)}, u32[]{:S(2)}) collective-permute-start(bf16[704,256]{1,0:T(8,128)(2,1)S(1)} %get-tuple-element.124), channel_id=1, source_target_pairs={{0,16},{1,9},{2,18},{3,11},{4,20},{5,13},{6,22},{7,15},{8,24},{9,1... | collective-permute-start | bytes 1081352 | tf_op jit(solution)/shard_map/ppermute | solution.py:585
  74.4 1.6 %collective-permute-start.31 = (bf16[448,256]{1,0:T(8,128)(2,1)S(1)}, bf16[448,256]{1,0:T(8,128)(2,1)S(1)}, u32[]{:S(2)}, u32[]{:S(2)}) collective-permute-start(bf16[448,256]{1,0:T(8,128)(2,1)S(1)} %get-tuple-element.139), channel_id=1, source_target_pairs={{0,8},{1,9},{2,10},{3,11},{4,12},{5,13},{6,14},{7,15},{8,0},{9,1},... | collective-permute-start | bytes 688136 | tf_op jit(solution)/shard_map/ppermute | solution.py:585
  76.0 1.5 %collective-permute-start.32 = (bf16[448,256]{1,0:T(8,128)(2,1)S(1)}, bf16[448,256]{1,0:T(8,128)(2,1)S(1)}, u32[]{:S(2)}, u32[]{:S(2)}) collective-permute-start(bf16[448,256]{1,0:T(8,128)(2,1)S(1)} %get-tuple-element.140), channel_id=1, source_target_pairs={{0,16},{1,17},{2,18},{3,19},{4,20},{5,21},{6,22},{7,23},{8,24},{9,... | collective-permute-start | bytes 688136 | tf_op jit(solution)/shard_map/ppermute | solution.py:585
  78.0 2.1 %shard_map.267 = (bf16[196,4,1024]{2,1,0:T(4,128)(2,1)}, f32[8,128]{1,0:T(8,128)S(1)}) custom-call(f32[8,256]{1,0:T(8,128)S(1)} %get-tuple-element.88.refs_4_.refs_0_, bf16[196,4,1024]{2,1,0:T(4,128)(2,1)S(1)} %bitcast.71, f32[784,1024]{1,0:T(8,128)S(1)} %get-tuple-element.102.refs_9_.refs_2_, bf16[784,256]{1,0:T(8,128)(2,1)S(1)} %get-tuple-element.129.refs_3_, ...), custom_call_target="tpu_custom_call" | custom-call | flops 1024 | bytes 1024 | tf_op jit(solution)/shard_map/pallas_call | solution.py:557
  80.1 1.9 %shard_map.268 = (bf16[196,4,256]{2,1,0:T(4,128)(2,1)}, f32[8,128]{1,0:T(8,128)S(1)}) custom-call(f32[8,256]{1,0:T(8,128)S(1)} %get-tuple-element.88.refs_4_.refs_0_, bf16[784,768]{1,0:T(8,128)(2,1)S(1)} %get-tuple-element.125.refs_1_, bf16[896,768]{1,0:T(8,128)(2,1)S(1)} %get-tuple-element.126.refs_2_, bf16[3,3,256,256]{3,2,1,0:T(8,128)(2,1)S(1)} %copy-done.5, ...), custom_call_target="tpu_custom_call" | custom-call | flops 1024 | bytes 1024 | tf_op jit(solution)/shard_map/pallas_call | solution.py:557
  83.0 1.1 collective-permute-start.29
  84.1 2.4 %collective-permute-start.30 = (bf16[176,256]{1,0:T(8,128)(2,1)S(1)}, bf16[176,256]{1,0:T(8,128)(2,1)S(1)}, u32[]{:S(2)}, u32[]{:S(2)}) collective-permute-start(bf16[176,256]{1,0:T(8,128)(2,1)S(1)} %get-tuple-element.138), channel_id=1, source_target_pairs={{0,6},{1,7},{2,4},{3,5},{4,2},{5,3},{6,0},{7,1},{8,14},{9,15},{10,... | collective-permute-start | bytes 270344 | tf_op jit(solution)/shard_map/ppermute | solution.py:585
  86.5 1.6 %collective-permute-done.32 = bf16[448,256]{1,0:T(8,128)(2,1)S(1)} collective-permute-done((bf16[448,256]{1,0:T(8,128)(2,1)S(1)}, bf16[448,256]{1,0:T(8,128)(2,1)S(1)}, u32[]{:S(2)}, u32[]{:S(2)}) %collective-permute-start.32) | collective-permute-done | bytes 229408 | tf_op jit(solution)/shard_map/ppermute | solution.py:585
  89.0 3.3 %collective-permute-done.29.refs_2_ = bf16[176,256]{1,0:T(8,128)(2,1)S(1)} collective-permute-done((bf16[176,256]{1,0:T(8,128)(2,1)S(1)}, bf16[176,256]{1,0:T(8,128)(2,1)S(1)}, u32[]{:S(2)}, u32[]{:S(2)}) %collective-permute-start.29) | collective-permute-done | bytes 90144 | tf_op jit(solution)/shard_map/ppermute | solution.py:585
  92.4 2.4 %collective-permute-start.36 = (bf16[176,256]{1,0:T(8,128)(2,1)S(1)}, bf16[176,256]{1,0:T(8,128)(2,1)S(1)}, u32[]{:S(2)}, u32[]{:S(2)}) collective-permute-start(bf16[176,256]{1,0:T(8,128)(2,1)S(1)} %shard_map.271.refs_0_.refs_4_), channel_id=1, source_target_pairs={{0,6},{1,7},{2,4},{3,5},{4,2},{5,3},{6,0},{7,1},{8,14},{9,15},{10,... | collective-permute-start | bytes 270344 | tf_op jit(solution)/shard_map/ppermute | solution.py:585
  95.4 1.4 collective-permute-start.34
  96.8 2.8 %collective-permute-done.36.refs_3_ = bf16[176,256]{1,0:T(8,128)(2,1)S(1)} collective-permute-done((bf16[176,256]{1,0:T(8,128)(2,1)S(1)}, bf16[176,256]{1,0:T(8,128)(2,1)S(1)}, u32[]{:S(2)}, u32[]{:S(2)}) %collective-permute-start.36) | collective-permute-done | bytes 90144 | tf_op jit(solution)/shard_map/ppermute | solution.py:585
  99.6 2.8 %collective-permute-done.35.refs_2_ = bf16[176,256]{1,0:T(8,128)(2,1)S(1)} collective-permute-done((bf16[176,256]{1,0:T(8,128)(2,1)S(1)}, bf16[176,256]{1,0:T(8,128)(2,1)S(1)}, u32[]{:S(2)}, u32[]{:S(2)}) %collective-permute-start.35) | collective-permute-done | bytes 90144 | tf_op jit(solution)/shard_map/ppermute | solution.py:585
  102.5 1.6 %collective-permute-start.37 = (bf16[704,256]{1,0:T(8,128)(2,1)S(1)}, bf16[704,256]{1,0:T(8,128)(2,1)S(1)}, u32[]{:S(2)}, u32[]{:S(2)}) collective-permute-start(bf16[704,256]{1,0:T(8,128)(2,1)S(1)} %bitcast.80), channel_id=1, source_target_pairs={{0,16},{1,9},{2,18},{3,11},{4,20},{5,13},{6,22},{7,15},{8,24},{9,1... | collective-permute-start | bytes 1081352 | tf_op jit(solution)/shard_map/ppermute | solution.py:585
  104.1 1.9 %collective-permute-start.39 = (bf16[112,256]{1,0:T(8,128)(2,1)S(1)}, bf16[112,256]{1,0:T(8,128)(2,1)S(1)}, u32[]{:S(2)}, u32[]{:S(2)}) collective-permute-start(bf16[112,256]{1,0:T(8,128)(2,1)S(1)} %get-tuple-element.144), channel_id=1, source_target_pairs={{0,4},{1,5},{2,6},{3,7},{4,0},{5,1},{6,2},{7,3},{8,12},{9,13},{10,... | collective-permute-start | bytes 172040 | tf_op jit(solution)/shard_map/ppermute | solution.py:585
  106.0 2.4 %collective-permute-start.40 = (bf16[112,256]{1,0:T(8,128)(2,1)S(1)}, bf16[112,256]{1,0:T(8,128)(2,1)S(1)}, u32[]{:S(2)}, u32[]{:S(2)}) collective-permute-start(bf16[112,256]{1,0:T(8,128)(2,1)S(1)} %get-tuple-element.145), channel_id=1, source_target_pairs={{0,6},{1,7},{2,4},{3,5},{4,2},{5,3},{6,0},{7,1},{8,14},{9,15},{10,... | collective-permute-start | bytes 172040 | tf_op jit(solution)/shard_map/ppermute | solution.py:585
  108.5 1.0 collective-permute-done.39.refs_2_
  109.5 2.5 %collective-permute-done.40.refs_3_ = bf16[112,256]{1,0:T(8,128)(2,1)S(1)} collective-permute-done((bf16[112,256]{1,0:T(8,128)(2,1)S(1)}, bf16[112,256]{1,0:T(8,128)(2,1)S(1)}, u32[]{:S(2)}, u32[]{:S(2)}) %collective-permute-start.40) | collective-permute-done | bytes 57376 | tf_op jit(solution)/shard_map/ppermute | solution.py:585
  112.2 1.6 %collective-permute-start.47 = (bf16[1408,256]{1,0:T(8,128)(2,1)S(1)}, bf16[1408,256]{1,0:T(8,128)(2,1)S(1)}, u32[]{:S(2)}, u32[]{:S(2)}) collective-permute-start(bf16[1408,256]{1,0:T(8,128)(2,1)S(1)} %bitcast.67), channel_id=1, source_target_pairs={{0,8},{1,17},{2,10},{3,19},{4,12},{5,21},{6,14},{7,23},{8,0},{9,25... | collective-permute-start | bytes 2162696 | tf_op jit(solution)/shard_map/ppermute | solution.py:585
  113.8 2.3 %collective-permute-start.43 = (bf16[112,256]{1,0:T(8,128)(2,1)S(1)}, bf16[112,256]{1,0:T(8,128)(2,1)S(1)}, u32[]{:S(2)}, u32[]{:S(2)}) collective-permute-start(bf16[112,256]{1,0:T(8,128)(2,1)S(1)} %shard_map.273.refs_2_.refs_0_), channel_id=1, source_target_pairs={{0,6},{1,7},{2,4},{3,5},{4,2},{5,3},{6,0},{7,1},{8,14},{9,15},{10,... | collective-permute-start | bytes 172040 | tf_op jit(solution)/shard_map/ppermute | solution.py:585
  116.2 2.0 %collective-permute-start.41 = (bf16[112,256]{1,0:T(8,128)(2,1)S(1)}, bf16[112,256]{1,0:T(8,128)(2,1)S(1)}, u32[]{:S(2)}, u32[]{:S(2)}) collective-permute-start(bf16[112,256]{1,0:T(8,128)(2,1)S(1)} %shard_map.273.refs_2_.refs_0_), channel_id=1, source_target_pairs={{0,2},{1,3},{2,0},{3,1},{4,6},{5,7},{6,4},{7,5},{8,10},{9,11},{10,... | collective-permute-start | bytes 172040 | tf_op jit(solution)/shard_map/ppermute | solution.py:585
  118.2 3.9 %shard_map.275 = (bf16[196,4,1024]{2,1,0:T(4,128)(2,1)}, bf16[196,4,256]{2,1,0:T(4,128)(2,1)}, f32[8,128]{1,0:T(8,128)S(1)}) custom-call(f32[8,256]{1,0:T(8,128)S(1)} %get-tuple-element.88.refs_4_.refs_0_, f32[16,128]{1,0:T(8,128)S(1)} %get-tuple-element.92.refs_5_.refs_1_, f32[8,128]{1,0:T(8,128)S(1)} %get-tuple-element.96.refs_6_.refs_2_, ...), custom_call_target="tpu_custom_call" | custom-call | flops 1024 | bytes 1024 | tf_op jit(solution)/shard_map/pallas_call | solution.py:557
  122.2 1.3 collective-permute-done.47.refs_1_
  123.7 1.6 %collective-permute-start.46 = (bf16[448,256]{1,0:T(8,128)(2,1)S(1)}, bf16[448,256]{1,0:T(8,128)(2,1)S(1)}, u32[]{:S(2)}, u32[]{:S(2)}) collective-permute-start(bf16[448,256]{1,0:T(8,128)(2,1)S(1)} %bitcast.85), channel_id=1, source_target_pairs={{0,24},{1,25},{2,26},{3,27},{4,28},{5,29},{6,30},{7,31},{8,16},{9,... | collective-permute-start | bytes 688136 | tf_op jit(solution)/shard_map/ppermute | solution.py:585
  125.3 1.5 %collective-permute-start.45 = (bf16[448,256]{1,0:T(8,128)(2,1)S(1)}, bf16[448,256]{1,0:T(8,128)(2,1)S(1)}, u32[]{:S(2)}, u32[]{:S(2)}) collective-permute-start(bf16[448,256]{1,0:T(8,128)(2,1)S(1)} %bitcast.86), channel_id=1, source_target_pairs={{0,16},{1,17},{2,18},{3,19},{4,20},{5,21},{6,22},{7,23},{8,24},{9,... | collective-permute-start | bytes 688136 | tf_op jit(solution)/shard_map/ppermute | solution.py:585
  127.3 2.8 %shard_map.278 = (f32[9,256,256]{2,1,0:T(8,128)}, f32[9,256,256]{2,1,0:T(8,128)}, f32[256,1024]{1,0:T(8,128)}, f32[8,128]{1,0:T(8,128)S(1)}) custom-call(bf16[2816,256]{1,0:T(8,128)(2,1)S(1)} %bitcast.77, bf16[2816,256]{1,0:T(8,128)(2,1)S(1)} %collective-permute-done.48.refs_1_), custom_call_target="tpu_custom_call" | custom-call | flops 1024 | bytes 1024 | tf_op jit(solution)/shard_map/pallas_call | solution.py:557
  130.1 3.0 %collective-permute-done.46.refs_3_ = bf16[448,256]{1,0:T(8,128)(2,1)S(1)} collective-permute-done((bf16[448,256]{1,0:T(8,128)(2,1)S(1)}, bf16[448,256]{1,0:T(8,128)(2,1)S(1)}, u32[]{:S(2)}, u32[]{:S(2)}) %collective-permute-start.46) | collective-permute-done | bytes 229408 | tf_op jit(solution)/shard_map/ppermute | solution.py:585
  133.1 4.4 %collective-permute-done.45.refs_2_ = bf16[448,256]{1,0:T(8,128)(2,1)S(1)} collective-permute-done((bf16[448,256]{1,0:T(8,128)(2,1)S(1)}, bf16[448,256]{1,0:T(8,128)(2,1)S(1)}, u32[]{:S(2)}, u32[]{:S(2)}) %collective-permute-start.45) | collective-permute-done | bytes 229408 | tf_op jit(solution)/shard_map/ppermute | solution.py:585
  137.7 2.4 %collective-permute-done.49.refs_1_ = bf16[1792,256]{1,0:T(8,128)(2,1)S(1)} collective-permute-done((bf16[1792,256]{1,0:T(8,128)(2,1)S(1)}, bf16[1792,256]{1,0:T(8,128)(2,1)S(1)}, u32[]{:S(2)}, u32[]{:S(2)}) %collective-permute-start.49) | collective-permute-done | bytes 917536 | tf_op jit(solution)/shard_map/ppermute | solution.py:34
  140.2 2.0 %shard_map.280 = (f32[9,256,256]{2,1,0:T(8,128)}, f32[1,1024,256]{2,1,0:T(8,128)}, f32[2,256]{1,0:T(2,128)}, f32[2,256]{1,0:T(2,128)}, f32[2,1024]{1,0:T(2,128)}, /*index=5*/f32[2,256]{1,0:T(2,128)}, f32[2,256]{1,0:T(2,128)}) custom-call(bf16[1792,256]{1,0:T(8,128)(2,1)S(1)} %bitcast.79, bf16[1792,256]{1,0:T(8,128)(2,1)S(1)} %collective-permute-done.49.refs_1_), custom_call_target="tpu_custom_call" | custom-call | flops 1024 | bytes 1024 | tf_op jit(solution)/shard_map/pallas_call | solution.py:557
  (97 shorter events, 14.8 us)
Async XLA Ops:
  0.6 15.1 %copy-start.3 = (bf16[3,3,256,256]{3,2,1,0:T(8,128)(2,1)S(1)}, bf16[3,3,256,256]{3,2,1,0:T(8,128)(2,1)}, u32[]{:S(2)}) copy-start(bf16[3,3,256,256]{3,2,1,0:T(8,128)(2,1)} %refs_16_.1) | copy-start | bytes 3538948
  0.7 15.1 %copy-start.4 = (bf16[3,3,256,256]{3,2,1,0:T(8,128)(2,1)S(1)}, bf16[3,3,256,256]{3,2,1,0:T(8,128)(2,1)}, u32[]{:S(2)}) copy-start(bf16[3,3,256,256]{3,2,1,0:T(8,128)(2,1)} %refs_12_.5) | copy-start | bytes 3538948
  0.7 15.1 %copy-start.10 = (f32[2,256]{1,0:T(2,128)S(1)}, f32[2,256]{1,0:T(2,128)}, u32[]{:S(2)}) copy-start(f32[2,256]{1,0:T(2,128)} %refs_5_.1) | copy-start | bytes 6148
  0.7 15.1 %copy-start.11 = (f32[2,256]{1,0:T(2,128)S(1)}, f32[2,256]{1,0:T(2,128)}, u32[]{:S(2)}) copy-start(f32[2,256]{1,0:T(2,128)} %refs_8_.4) | copy-start | bytes 6148
  4.9 1.3 collective-permute-start
  6.2 6.6 %collective-permute-start.3 = (f32[16,128]{1,0:T(8,128)S(1)}, f32[16,128]{1,0:T(8,128)S(1)}, u32[]{:S(2)}, u32[]{:S(2)}) collective-permute-start(f32[16,128]{1,0:T(8,128)S(1)} %add.18.refs_0_), channel_id=1, source_target_pairs={{0,6},{1,7},{2,4},{3,5},{4,2},{5,3},{6,0},{7,1},{8,14},{9,15},{10,... | collective-permute-start | bytes 24584 | tf_op jit(solution)/shard_map/ppermute | solution.py:34
  11.2 4.5 %collective-permute-start.2 = (f32[16,128]{1,0:T(8,128)S(1)}, f32[16,128]{1,0:T(8,128)S(1)}, u32[]{:S(2)}, u32[]{:S(2)}) collective-permute-start(f32[16,128]{1,0:T(8,128)S(1)} %add.18.refs_0_), channel_id=1, source_target_pairs={{0,4},{1,5},{2,6},{3,7},{4,0},{5,1},{6,2},{7,3},{8,12},{9,13},{10,... | collective-permute-start | bytes 24584 | tf_op jit(solution)/shard_map/ppermute | solution.py:34
  11.2 4.5 %collective-permute-start.1 = (f32[16,128]{1,0:T(8,128)S(1)}, f32[16,128]{1,0:T(8,128)S(1)}, u32[]{:S(2)}, u32[]{:S(2)}) collective-permute-start(f32[16,128]{1,0:T(8,128)S(1)} %add.18.refs_0_), channel_id=1, source_target_pairs={{0,2},{1,3},{2,0},{3,1},{4,6},{5,7},{6,4},{7,5},{8,10},{9,11},{10,... | collective-permute-start | bytes 24584 | tf_op jit(solution)/shard_map/ppermute | solution.py:34
  15.8 9.7 %copy-start.2 = (bf16[1,4,14,14,256]{4,1,3,2,0:T(4,128)(2,1)S(1)}, bf16[1,4,14,14,256]{4,1,3,2,0:T(4,128)(2,1)}, u32[]{:S(2)}) copy-start(bf16[1,4,14,14,256]{4,1,3,2,0:T(4,128)(2,1)} %param.16) | copy-start | bytes 1204228
  15.8 9.7 %copy-start.7 = (bf16[256,1024]{1,0:T(8,128)(2,1)S(1)}, bf16[256,1024]{1,0:T(8,128)(2,1)}, u32[]{:S(2)}) copy-start(bf16[256,1024]{1,0:T(8,128)(2,1)} %refs_13_.3) | copy-start | bytes 1572868
  15.8 9.7 %copy-start.8 = (bf16[1,4,14,14,256]{4,1,3,2,0:T(4,128)(2,1)S(1)}, bf16[1,4,14,14,256]{4,1,3,2,0:T(4,128)(2,1)}, u32[]{:S(2)}) copy-start(bf16[1,4,14,14,256]{4,1,3,2,0:T(4,128)(2,1)} %param.18) | copy-start | bytes 1204228
  15.8 9.7 %copy-start.12 = (f32[2,256]{1,0:T(2,128)S(1)}, f32[2,256]{1,0:T(2,128)}, u32[]{:S(2)}) copy-start(f32[2,256]{1,0:T(2,128)} %refs_10_.5) | copy-start | bytes 6148
  15.8 9.7 %copy-start.13 = (f32[2,256]{1,0:T(2,128)S(1)}, f32[2,256]{1,0:T(2,128)}, u32[]{:S(2)}) copy-start(f32[2,256]{1,0:T(2,128)} %refs_9_.3) | copy-start | bytes 6148
  15.8 20.0 %copy-start.1 = (bf16[1,4,14,14,1024]{4,1,3,2,0:T(4,128)(2,1)S(1)}, bf16[1,4,14,14,1024]{4,1,3,2,0:T(4,128)(2,1)}, u32[]{:S(2)}) copy-start(bf16[1,4,14,14,1024]{4,1,3,2,0:T(4,128)(2,1)} %param.17) | copy-start | bytes 4816900
  18.2 1.2 collective-permute-start.4
  19.5 5.4 %collective-permute-start.7 = (f32[8,128]{1,0:T(8,128)S(1)}, f32[8,128]{1,0:T(8,128)S(1)}, u32[]{:S(2)}, u32[]{:S(2)}) collective-permute-start(f32[8,128]{1,0:T(8,128)S(1)} %add.19.refs_0_), channel_id=1, source_target_pairs={{0,6},{1,7},{2,4},{3,5},{4,2},{5,3},{6,0},{7,1},{8,14},{9,15},{10,... | collective-permute-start | bytes 12296 | tf_op jit(solution)/shard_map/ppermute | solution.py:34
  20.9 4.5 %collective-permute-start.6 = (f32[8,128]{1,0:T(8,128)S(1)}, f32[8,128]{1,0:T(8,128)S(1)}, u32[]{:S(2)}, u32[]{:S(2)}) collective-permute-start(f32[8,128]{1,0:T(8,128)S(1)} %add.19.refs_0_), channel_id=1, source_target_pairs={{0,4},{1,5},{2,6},{3,7},{4,0},{5,1},{6,2},{7,3},{8,12},{9,13},{10,... | collective-permute-start | bytes 12296 | tf_op jit(solution)/shard_map/ppermute | solution.py:34
  21.5 4.0 %collective-permute-start.5 = (f32[8,128]{1,0:T(8,128)S(1)}, f32[8,128]{1,0:T(8,128)S(1)}, u32[]{:S(2)}, u32[]{:S(2)}) collective-permute-start(f32[8,128]{1,0:T(8,128)S(1)} %add.19.refs_0_), channel_id=1, source_target_pairs={{0,2},{1,3},{2,0},{3,1},{4,6},{5,7},{6,4},{7,5},{8,10},{9,11},{10,... | collective-permute-start | bytes 12296 | tf_op jit(solution)/shard_map/ppermute | solution.py:34
  25.5 10.3 %copy-start = (bf16[1,4,14,14,1024]{4,1,3,2,0:T(4,128)(2,1)S(1)}, bf16[1,4,14,14,1024]{4,1,3,2,0:T(4,128)(2,1)}, u32[]{:S(2)}) copy-start(bf16[1,4,14,14,1024]{4,1,3,2,0:T(4,128)(2,1)} %param.15) | copy-start | bytes 4816900
  25.5 10.3 %copy-start.9 = (f32[2,1024]{1,0:T(2,128)S(1)}, f32[2,1024]{1,0:T(2,128)}, u32[]{:S(2)}) copy-start(f32[2,1024]{1,0:T(2,128)} %refs_8_.5) | copy-start | bytes 24580
  27.3 1.2 collective-permute-start.8
  28.5 5.6 %collective-permute-start.11 = (f32[24,128]{1,0:T(8,128)S(1)}, f32[24,128]{1,0:T(8,128)S(1)}, u32[]{:S(2)}, u32[]{:S(2)}) collective-permute-start(f32[24,128]{1,0:T(8,128)S(1)} %add.20.refs_0_), channel_id=1, source_target_pairs={{0,6},{1,7},{2,4},{3,5},{4,2},{5,3},{6,0},{7,1},{8,14},{9,15},{10,... | collective-permute-start | bytes 36872 | tf_op jit(solution)/shard_map/ppermute | solution.py:34
  31.1 4.6 %collective-permute-start.10 = (f32[24,128]{1,0:T(8,128)S(1)}, f32[24,128]{1,0:T(8,128)S(1)}, u32[]{:S(2)}, u32[]{:S(2)}) collective-permute-start(f32[24,128]{1,0:T(8,128)S(1)} %add.20.refs_0_), channel_id=1, source_target_pairs={{0,4},{1,5},{2,6},{3,7},{4,0},{5,1},{6,2},{7,3},{8,12},{9,13},{10,... | collective-permute-start | bytes 36872 | tf_op jit(solution)/shard_map/ppermute | solution.py:34
  32.0 3.8 %collective-permute-start.9 = (f32[24,128]{1,0:T(8,128)S(1)}, f32[24,128]{1,0:T(8,128)S(1)}, u32[]{:S(2)}, u32[]{:S(2)}) collective-permute-start(f32[24,128]{1,0:T(8,128)S(1)} %add.20.refs_0_), channel_id=1, source_target_pairs={{0,2},{1,3},{2,0},{3,1},{4,6},{5,7},{6,4},{7,5},{8,10},{9,11},{10,... | collective-permute-start | bytes 36872 | tf_op jit(solution)/shard_map/ppermute | solution.py:34
  39.2 1.2 collective-permute-start.12
  40.4 5.8 %collective-permute-start.15 = (f32[24,128]{1,0:T(8,128)S(1)}, f32[24,128]{1,0:T(8,128)S(1)}, u32[]{:S(2)}, u32[]{:S(2)}) collective-permute-start(f32[24,128]{1,0:T(8,128)S(1)} %add.21.refs_3_.refs_0_), channel_id=1, source_target_pairs={{0,6},{1,7},{2,4},{3,5},{4,2},{5,3},{6,0},{7,1},{8,14},{9,15},{10,... | collective-permute-start | bytes 36872 | tf_op jit(solution)/shard_map/ppermute | solution.py:34
  41.7 4.6 %collective-permute-start.14 = (f32[24,128]{1,0:T(8,128)S(1)}, f32[24,128]{1,0:T(8,128)S(1)}, u32[]{:S(2)}, u32[]{:S(2)}) collective-permute-start(f32[24,128]{1,0:T(8,128)S(1)} %add.21.refs_3_.refs_0_), channel_id=1, source_target_pairs={{0,4},{1,5},{2,6},{3,7},{4,0},{5,1},{6,2},{7,3},{8,12},{9,13},{10,... | collective-permute-start | bytes 36872 | tf_op jit(solution)/shard_map/ppermute | solution.py:34
  42.7 3.8 %collective-permute-start.13 = (f32[24,128]{1,0:T(8,128)S(1)}, f32[24,128]{1,0:T(8,128)S(1)}, u32[]{:S(2)}, u32[]{:S(2)}) collective-permute-start(f32[24,128]{1,0:T(8,128)S(1)} %add.21.refs_3_.refs_0_), channel_id=1, source_target_pairs={{0,2},{1,3},{2,0},{3,1},{4,6},{5,7},{6,4},{7,5},{8,10},{9,11},{10,... | collective-permute-start | bytes 36872 | tf_op jit(solution)/shard_map/ppermute | solution.py:34
  47.9 1.2 collective-permute-start.16
  51.4 7.3 %collective-permute-start.17 = (bf16[2816,256]{1,0:T(8,128)(2,1)S(1)}, bf16[2816,256]{1,0:T(8,128)(2,1)S(1)}, u32[]{:S(2)}, u32[]{:S(2)}) collective-permute-start(bf16[2816,256]{1,0:T(8,128)(2,1)S(1)} %get-tuple-element.114), channel_id=1, source_target_pairs={{0,1},{1,0},{2,3},{3,2},{4,5},{5,4},{6,7},{7,6},{8,9},{9,8},{10,11... | collective-permute-start | bytes 4325384 | tf_op jit(solution)/shard_map/ppermute | solution.py:34
  51.6 5.4 %collective-permute-start.20 = (f32[8,128]{1,0:T(8,128)S(1)}, f32[8,128]{1,0:T(8,128)S(1)}, u32[]{:S(2)}, u32[]{:S(2)}) collective-permute-start(f32[8,128]{1,0:T(8,128)S(1)} %add.22.refs_11_.refs_0_), channel_id=1, source_target_pairs={{0,6},{1,7},{2,4},{3,5},{4,2},{5,3},{6,0},{7,1},{8,14},{9,15},{10,... | collective-permute-start | bytes 12296 | tf_op jit(solution)/shard_map/ppermute | solution.py:34
  54.1 4.5 %collective-permute-start.19 = (f32[8,128]{1,0:T(8,128)S(1)}, f32[8,128]{1,0:T(8,128)S(1)}, u32[]{:S(2)}, u32[]{:S(2)}) collective-permute-start(f32[8,128]{1,0:T(8,128)S(1)} %add.22.refs_11_.refs_0_), channel_id=1, source_target_pairs={{0,4},{1,5},{2,6},{3,7},{4,0},{5,1},{6,2},{7,3},{8,12},{9,13},{10,... | collective-permute-start | bytes 12296 | tf_op jit(solution)/shard_map/ppermute | solution.py:34
  55.1 3.6 %collective-permute-start.18 = (f32[8,128]{1,0:T(8,128)S(1)}, f32[8,128]{1,0:T(8,128)S(1)}, u32[]{:S(2)}, u32[]{:S(2)}) collective-permute-start(f32[8,128]{1,0:T(8,128)S(1)} %add.22.refs_11_.refs_0_), channel_id=1, source_target_pairs={{0,2},{1,3},{2,0},{3,1},{4,6},{5,7},{6,4},{7,5},{8,10},{9,11},{10,... | collective-permute-start | bytes 12296 | tf_op jit(solution)/shard_map/ppermute | solution.py:34
  59.1 11.4 %collective-permute-start.21 = (bf16[1408,256]{1,0:T(8,128)(2,1)S(1)}, bf16[1408,256]{1,0:T(8,128)(2,1)S(1)}, u32[]{:S(2)}, u32[]{:S(2)}) collective-permute-start(bf16[1408,256]{1,0:T(8,128)(2,1)S(1)} %get-tuple-element.116), channel_id=1, source_target_pairs={{0,8},{1,17},{2,10},{3,19},{4,12},{5,21},{6,14},{7,23},{8,0},{9,25... | collective-permute-start | bytes 2162696 | tf_op jit(solution)/shard_map/ppermute | solution.py:585
  62.0 1.2 collective-permute-start.22
  63.2 7.4 %collective-permute-start.26 = (f32[8,128]{1,0:T(8,128)S(1)}, f32[8,128]{1,0:T(8,128)S(1)}, u32[]{:S(2)}, u32[]{:S(2)}) collective-permute-start(f32[8,128]{1,0:T(8,128)S(1)} %add.23.refs_3_.refs_0_), channel_id=1, source_target_pairs={{0,6},{1,7},{2,4},{3,5},{4,2},{5,3},{6,0},{7,1},{8,14},{9,15},{10,... | collective-permute-start | bytes 12296 | tf_op jit(solution)/shard_map/ppermute | solution.py:34
  64.6 6.1 %collective-permute-start.25 = (f32[8,128]{1,0:T(8,128)S(1)}, f32[8,128]{1,0:T(8,128)S(1)}, u32[]{:S(2)}, u32[]{:S(2)}) collective-permute-start(f32[8,128]{1,0:T(8,128)S(1)} %add.23.refs_3_.refs_0_), channel_id=1, source_target_pairs={{0,4},{1,5},{2,6},{3,7},{4,0},{5,1},{6,2},{7,3},{8,12},{9,13},{10,... | collective-permute-start | bytes 12296 | tf_op jit(solution)/shard_map/ppermute | solution.py:34
  65.6 5.1 %collective-permute-start.24 = (f32[8,128]{1,0:T(8,128)S(1)}, f32[8,128]{1,0:T(8,128)S(1)}, u32[]{:S(2)}, u32[]{:S(2)}) collective-permute-start(f32[8,128]{1,0:T(8,128)S(1)} %add.23.refs_3_.refs_0_), channel_id=1, source_target_pairs={{0,2},{1,3},{2,0},{3,1},{4,6},{5,7},{6,4},{7,5},{8,10},{9,11},{10,... | collective-permute-start | bytes 12296 | tf_op jit(solution)/shard_map/ppermute | solution.py:34
  71.7 6.3 %copy-start.6 = (bf16[1024,256]{1,0:T(8,128)(2,1)S(1)}, bf16[1024,256]{1,0:T(8,128)(2,1)}, u32[]{:S(2)}) copy-start(bf16[1024,256]{1,0:T(8,128)(2,1)} %refs_4_.3) | copy-start | bytes 1572868
  71.7 2.5 %collective-permute-start.27 = (bf16[1792,256]{1,0:T(8,128)(2,1)S(1)}, bf16[1792,256]{1,0:T(8,128)(2,1)S(1)}, u32[]{:S(2)}, u32[]{:S(2)}) collective-permute-start(bf16[1792,256]{1,0:T(8,128)(2,1)S(1)} %get-tuple-element.131), channel_id=1, source_target_pairs={{0,1},{1,0},{2,3},{3,2},{4,5},{5,4},{6,7},{7,6},{8,9},{9,8},{10,11... | collective-permute-start | bytes 2752520 | tf_op jit(solution)/shard_map/ppermute | solution.py:34
  71.8 10.2 %collective-permute-start.23 = (bf16[704,256]{1,0:T(8,128)(2,1)S(1)}, bf16[704,256]{1,0:T(8,128)(2,1)S(1)}, u32[]{:S(2)}, u32[]{:S(2)}) collective-permute-start(bf16[704,256]{1,0:T(8,128)(2,1)S(1)} %get-tuple-element.124), channel_id=1, source_target_pairs={{0,16},{1,9},{2,18},{3,11},{4,20},{5,13},{6,22},{7,15},{8,24},{9,1... | collective-permute-start | bytes 1081352 | tf_op jit(solution)/shard_map/ppermute | solution.py:585
  74.4 9.7 %collective-permute-start.31 = (bf16[448,256]{1,0:T(8,128)(2,1)S(1)}, bf16[448,256]{1,0:T(8,128)(2,1)S(1)}, u32[]{:S(2)}, u32[]{:S(2)}) collective-permute-start(bf16[448,256]{1,0:T(8,128)(2,1)S(1)} %get-tuple-element.139), channel_id=1, source_target_pairs={{0,8},{1,9},{2,10},{3,11},{4,12},{5,13},{6,14},{7,15},{8,0},{9,1},... | collective-permute-start | bytes 688136 | tf_op jit(solution)/shard_map/ppermute | solution.py:585
  76.0 12.2 %collective-permute-start.32 = (bf16[448,256]{1,0:T(8,128)(2,1)S(1)}, bf16[448,256]{1,0:T(8,128)(2,1)S(1)}, u32[]{:S(2)}, u32[]{:S(2)}) collective-permute-start(bf16[448,256]{1,0:T(8,128)(2,1)S(1)} %get-tuple-element.140), channel_id=1, source_target_pairs={{0,16},{1,17},{2,18},{3,19},{4,20},{5,21},{6,22},{7,23},{8,24},{9,... | collective-permute-start | bytes 688136 | tf_op jit(solution)/shard_map/ppermute | solution.py:585
  77.5 11.4 %collective-permute-start.33 = (bf16[448,256]{1,0:T(8,128)(2,1)S(1)}, bf16[448,256]{1,0:T(8,128)(2,1)S(1)}, u32[]{:S(2)}, u32[]{:S(2)}) collective-permute-start(bf16[448,256]{1,0:T(8,128)(2,1)S(1)} %get-tuple-element.141), channel_id=1, source_target_pairs={{0,24},{1,25},{2,26},{3,27},{4,28},{5,29},{6,30},{7,31},{8,16},{9,... | collective-permute-start | bytes 688136 | tf_op jit(solution)/shard_map/ppermute | solution.py:585
  78.0 2.1 %copy-start.5 = (bf16[3,3,256,256]{3,2,1,0:T(8,128)(2,1)S(1)}, bf16[3,3,256,256]{3,2,1,0:T(8,128)(2,1)}, u32[]{:S(2)}) copy-start(bf16[3,3,256,256]{3,2,1,0:T(8,128)(2,1)} %refs_3_.3) | copy-start | bytes 3538948
  82.1 7.0 %collective-permute-start.28 = (bf16[176,256]{1,0:T(8,128)(2,1)S(1)}, bf16[176,256]{1,0:T(8,128)(2,1)S(1)}, u32[]{:S(2)}, u32[]{:S(2)}) collective-permute-start(bf16[176,256]{1,0:T(8,128)(2,1)S(1)} %get-tuple-element.136), channel_id=1, source_target_pairs={{0,2},{1,3},{2,0},{3,1},{4,6},{5,7},{6,4},{7,5},{8,10},{9,11},{10,... | collective-permute-start | bytes 270344 | tf_op jit(solution)/shard_map/ppermute | solution.py:585
  83.0 9.3 %collective-permute-start.29 = (bf16[176,256]{1,0:T(8,128)(2,1)S(1)}, bf16[176,256]{1,0:T(8,128)(2,1)S(1)}, u32[]{:S(2)}, u32[]{:S(2)}) collective-permute-start(bf16[176,256]{1,0:T(8,128)(2,1)S(1)} %get-tuple-element.137), channel_id=1, source_target_pairs={{0,4},{1,5},{2,6},{3,7},{4,0},{5,1},{6,2},{7,3},{8,12},{9,13},{10,... | collective-permute-start | bytes 270344 | tf_op jit(solution)/shard_map/ppermute | solution.py:585
  84.1 8.2 %collective-permute-start.30 = (bf16[176,256]{1,0:T(8,128)(2,1)S(1)}, bf16[176,256]{1,0:T(8,128)(2,1)S(1)}, u32[]{:S(2)}, u32[]{:S(2)}) collective-permute-start(bf16[176,256]{1,0:T(8,128)(2,1)S(1)} %get-tuple-element.138), channel_id=1, source_target_pairs={{0,6},{1,7},{2,4},{3,5},{4,2},{5,3},{6,0},{7,1},{8,14},{9,15},{10,... | collective-permute-start | bytes 270344 | tf_op jit(solution)/shard_map/ppermute | solution.py:585
  92.4 7.3 %collective-permute-start.36 = (bf16[176,256]{1,0:T(8,128)(2,1)S(1)}, bf16[176,256]{1,0:T(8,128)(2,1)S(1)}, u32[]{:S(2)}, u32[]{:S(2)}) collective-permute-start(bf16[176,256]{1,0:T(8,128)(2,1)S(1)} %shard_map.271.refs_0_.refs_4_), channel_id=1, source_target_pairs={{0,6},{1,7},{2,4},{3,5},{4,2},{5,3},{6,0},{7,1},{8,14},{9,15},{10,... | collective-permute-start | bytes 270344 | tf_op jit(solution)/shard_map/ppermute | solution.py:585
  94.7 7.7 %collective-permute-start.35 = (bf16[176,256]{1,0:T(8,128)(2,1)S(1)}, bf16[176,256]{1,0:T(8,128)(2,1)S(1)}, u32[]{:S(2)}, u32[]{:S(2)}) collective-permute-start(bf16[176,256]{1,0:T(8,128)(2,1)S(1)} %shard_map.271.refs_0_.refs_4_), channel_id=1, source_target_pairs={{0,4},{1,5},{2,6},{3,7},{4,0},{5,1},{6,2},{7,3},{8,12},{9,13},{10,... | collective-permute-start | bytes 270344 | tf_op jit(solution)/shard_map/ppermute | solution.py:585
  95.4 7.1 %collective-permute-start.34 = (bf16[176,256]{1,0:T(8,128)(2,1)S(1)}, bf16[176,256]{1,0:T(8,128)(2,1)S(1)}, u32[]{:S(2)}, u32[]{:S(2)}) collective-permute-start(bf16[176,256]{1,0:T(8,128)(2,1)S(1)} %shard_map.271.refs_0_.refs_4_), channel_id=1, source_target_pairs={{0,2},{1,3},{2,0},{3,1},{4,6},{5,7},{6,4},{7,5},{8,10},{9,11},{10,... | collective-permute-start | bytes 270344 | tf_op jit(solution)/shard_map/ppermute | solution.py:585
  102.5 9.6 %collective-permute-start.37 = (bf16[704,256]{1,0:T(8,128)(2,1)S(1)}, bf16[704,256]{1,0:T(8,128)(2,1)S(1)}, u32[]{:S(2)}, u32[]{:S(2)}) collective-permute-start(bf16[704,256]{1,0:T(8,128)(2,1)S(1)} %bitcast.80), channel_id=1, source_target_pairs={{0,16},{1,9},{2,18},{3,11},{4,20},{5,13},{6,22},{7,15},{8,24},{9,1... | collective-permute-start | bytes 1081352 | tf_op jit(solution)/shard_map/ppermute | solution.py:585
  104.1 4.4 %collective-permute-start.38 = (bf16[112,256]{1,0:T(8,128)(2,1)S(1)}, bf16[112,256]{1,0:T(8,128)(2,1)S(1)}, u32[]{:S(2)}, u32[]{:S(2)}) collective-permute-start(bf16[112,256]{1,0:T(8,128)(2,1)S(1)} %get-tuple-element.143), channel_id=1, source_target_pairs={{0,2},{1,3},{2,0},{3,1},{4,6},{5,7},{6,4},{7,5},{8,10},{9,11},{10,... | collective-permute-start | bytes 172040 | tf_op jit(solution)/shard_map/ppermute | solution.py:585
  104.1 5.4 %collective-permute-start.39 = (bf16[112,256]{1,0:T(8,128)(2,1)S(1)}, bf16[112,256]{1,0:T(8,128)(2,1)S(1)}, u32[]{:S(2)}, u32[]{:S(2)}) collective-permute-start(bf16[112,256]{1,0:T(8,128)(2,1)S(1)} %get-tuple-element.144), channel_id=1, source_target_pairs={{0,4},{1,5},{2,6},{3,7},{4,0},{5,1},{6,2},{7,3},{8,12},{9,13},{10,... | collective-permute-start | bytes 172040 | tf_op jit(solution)/shard_map/ppermute | solution.py:585
  106.0 6.0 %collective-permute-start.40 = (bf16[112,256]{1,0:T(8,128)(2,1)S(1)}, bf16[112,256]{1,0:T(8,128)(2,1)S(1)}, u32[]{:S(2)}, u32[]{:S(2)}) collective-permute-start(bf16[112,256]{1,0:T(8,128)(2,1)S(1)} %get-tuple-element.145), channel_id=1, source_target_pairs={{0,6},{1,7},{2,4},{3,5},{4,2},{5,3},{6,0},{7,1},{8,14},{9,15},{10,... | collective-permute-start | bytes 172040 | tf_op jit(solution)/shard_map/ppermute | solution.py:585
  112.2 11.4 %collective-permute-start.47 = (bf16[1408,256]{1,0:T(8,128)(2,1)S(1)}, bf16[1408,256]{1,0:T(8,128)(2,1)S(1)}, u32[]{:S(2)}, u32[]{:S(2)}) collective-permute-start(bf16[1408,256]{1,0:T(8,128)(2,1)S(1)} %bitcast.67), channel_id=1, source_target_pairs={{0,8},{1,17},{2,10},{3,19},{4,12},{5,21},{6,14},{7,23},{8,0},{9,25... | collective-permute-start | bytes 2162696 | tf_op jit(solution)/shard_map/ppermute | solution.py:585
  113.8 8.3 %collective-permute-start.43 = (bf16[112,256]{1,0:T(8,128)(2,1)S(1)}, bf16[112,256]{1,0:T(8,128)(2,1)S(1)}, u32[]{:S(2)}, u32[]{:S(2)}) collective-permute-start(bf16[112,256]{1,0:T(8,128)(2,1)S(1)} %shard_map.273.refs_2_.refs_0_), channel_id=1, source_target_pairs={{0,6},{1,7},{2,4},{3,5},{4,2},{5,3},{6,0},{7,1},{8,14},{9,15},{10,... | collective-permute-start | bytes 172040 | tf_op jit(solution)/shard_map/ppermute | solution.py:585
  116.1 6.0 %collective-permute-start.42 = (bf16[112,256]{1,0:T(8,128)(2,1)S(1)}, bf16[112,256]{1,0:T(8,128)(2,1)S(1)}, u32[]{:S(2)}, u32[]{:S(2)}) collective-permute-start(bf16[112,256]{1,0:T(8,128)(2,1)S(1)} %shard_map.273.refs_2_.refs_0_), channel_id=1, source_target_pairs={{0,4},{1,5},{2,6},{3,7},{4,0},{5,1},{6,2},{7,3},{8,12},{9,13},{10,... | collective-permute-start | bytes 172040 | tf_op jit(solution)/shard_map/ppermute | solution.py:585
  116.2 6.0 %collective-permute-start.41 = (bf16[112,256]{1,0:T(8,128)(2,1)S(1)}, bf16[112,256]{1,0:T(8,128)(2,1)S(1)}, u32[]{:S(2)}, u32[]{:S(2)}) collective-permute-start(bf16[112,256]{1,0:T(8,128)(2,1)S(1)} %shard_map.273.refs_2_.refs_0_), channel_id=1, source_target_pairs={{0,2},{1,3},{2,0},{3,1},{4,6},{5,7},{6,4},{7,5},{8,10},{9,11},{10,... | collective-permute-start | bytes 172040 | tf_op jit(solution)/shard_map/ppermute | solution.py:585
  123.6 3.6 %collective-permute-start.48 = (bf16[2816,256]{1,0:T(8,128)(2,1)S(1)}, bf16[2816,256]{1,0:T(8,128)(2,1)S(1)}, u32[]{:S(2)}, u32[]{:S(2)}) collective-permute-start(bf16[2816,256]{1,0:T(8,128)(2,1)S(1)} %bitcast.76), channel_id=1, source_target_pairs={{0,1},{1,0},{2,3},{3,2},{4,5},{5,4},{6,7},{7,6},{8,9},{9,8},{10,11... | collective-permute-start | bytes 4325384 | tf_op jit(solution)/shard_map/ppermute | solution.py:34
  123.7 9.4 %collective-permute-start.46 = (bf16[448,256]{1,0:T(8,128)(2,1)S(1)}, bf16[448,256]{1,0:T(8,128)(2,1)S(1)}, u32[]{:S(2)}, u32[]{:S(2)}) collective-permute-start(bf16[448,256]{1,0:T(8,128)(2,1)S(1)} %bitcast.85), channel_id=1, source_target_pairs={{0,24},{1,25},{2,26},{3,27},{4,28},{5,29},{6,30},{7,31},{8,16},{9,... | collective-permute-start | bytes 688136 | tf_op jit(solution)/shard_map/ppermute | solution.py:585
  125.3 12.3 %collective-permute-start.45 = (bf16[448,256]{1,0:T(8,128)(2,1)S(1)}, bf16[448,256]{1,0:T(8,128)(2,1)S(1)}, u32[]{:S(2)}, u32[]{:S(2)}) collective-permute-start(bf16[448,256]{1,0:T(8,128)(2,1)S(1)} %bitcast.86), channel_id=1, source_target_pairs={{0,16},{1,17},{2,18},{3,19},{4,20},{5,21},{6,22},{7,23},{8,24},{9,... | collective-permute-start | bytes 688136 | tf_op jit(solution)/shard_map/ppermute | solution.py:585
  126.8 10.7 %collective-permute-start.44 = (bf16[448,256]{1,0:T(8,128)(2,1)S(1)}, bf16[448,256]{1,0:T(8,128)(2,1)S(1)}, u32[]{:S(2)}, u32[]{:S(2)}) collective-permute-start(bf16[448,256]{1,0:T(8,128)(2,1)S(1)} %bitcast.87), channel_id=1, source_target_pairs={{0,8},{1,9},{2,10},{3,11},{4,12},{5,13},{6,14},{7,15},{8,0},{9,1},... | collective-permute-start | bytes 688136 | tf_op jit(solution)/shard_map/ppermute | solution.py:585
  137.6 2.5 %collective-permute-start.49 = (bf16[1792,256]{1,0:T(8,128)(2,1)S(1)}, bf16[1792,256]{1,0:T(8,128)(2,1)S(1)}, u32[]{:S(2)}, u32[]{:S(2)}) collective-permute-start(bf16[1792,256]{1,0:T(8,128)(2,1)S(1)} %bitcast.78), channel_id=1, source_target_pairs={{0,1},{1,0},{2,3},{3,2},{4,5},{5,4},{6,7},{7,6},{8,9},{9,8},{10,11... | collective-permute-start | bytes 2752520 | tf_op jit(solution)/shard_map/ppermute | solution.py:34
